TPU v7x, 512 devices: a whole 4x4x16 slice. The times are simulated.
512 devices in a mesh: row: 8 (over y, core), col: 64 (over x, z).
Axes of the slice: x: 4, y: 4, z: 16, core: 2. Of those that a mesh axis runs over, the one named last changes fastest.
Arguments:
- matrix: bfloat16 [8192, 8192], P('row', 'col'), may hold values from -6 to 6
- lower_inverse: bfloat16 [2, 1024, 1024], P(None, 'row'), may hold values from -0.03125 to 0.03125
- upper_inverse: bfloat16 [2, 1024, 1024], P(None, 'row'), may hold values from -0.03125 to 0.03125
Outputs:
- factored: bfloat16 [8192, 8192], P('row', 'col')
All inputs are finite; a program needn't handle non-finite values.
Results may differ from a plain program's by a relative error of at most 0.013.
Values may be sent and summed in bfloat16 or wider, within the bound.
No kernel may reach another device: no remote copies, remote signals or barrier semaphores. Data moves between devices by JAX's collectives and lax.ppermute only.
A program may use at most 64 MiB of HBM per device.

v0:
```python
import jax
import jax.numpy as jnp
from jax import lax
from jax.sharding import PartitionSpec as P

NB = 1024
STEPS = 2


def spread(value, axis, root):
    mine = lax.axis_index(axis) == root
    return lax.psum(jnp.where(mine, value, jnp.zeros_like(value)), axis)


def shards(matrix, lower_inverse, upper_inverse):
    rows_local, cols_local = matrix.shape
    row_index = lax.axis_index("row")
    col_index = lax.axis_index("col")
    global_rows = row_index * rows_local + jnp.arange(rows_local, dtype=jnp.int32)[:, None]
    global_cols = col_index * cols_local + jnp.arange(cols_local, dtype=jnp.int32)[None, :]
    col_width = min(cols_local, NB)
    current = matrix
    for step_index in range(STEPS):
        block_low = step_index * NB
        block_high = block_low + NB
        owner_row = block_low // rows_local
        source_rows = current
        is_owner = row_index == owner_row
        lower_full = lax.all_gather(lower_inverse[step_index], "row", axis=0, tiled=True)
        local_top = jnp.dot(lower_full, source_rows, preferred_element_type=jnp.float32).astype(
            jnp.bfloat16
        )
        masked_top = jnp.where(is_owner, local_top.astype(jnp.float32), jnp.float32(0.0))
        top_share = lax.psum_scatter(
            masked_top.astype(jnp.bfloat16), "row", scatter_dimension=0, tiled=True
        )
        top_factor = lax.all_gather(top_share, "row", axis=0, tiled=True)
        upper_start = jnp.clip(col_index * cols_local - block_low, 0, NB - col_width)
        coupling_piece = jnp.dot(
            upper_inverse[step_index], top_factor, preferred_element_type=jnp.float32
        ).astype(jnp.bfloat16)
        coupling = lax.all_gather(coupling_piece, "row", axis=0, tiled=True)
        upper_part = lax.dynamic_slice_in_dim(upper_inverse[step_index], upper_start, col_width, 1)
        upper_cols = lax.all_gather(upper_part, "row", axis=0, tiled=True)
        members = NB // cols_local
        first_root = block_low // cols_local
        panel_source = current
        panel_slabs = [
            spread(panel_source, "col", first_root + member) for member in range(members)
        ]
        whole_panel = jnp.concatenate(panel_slabs, axis=1)
        product = jnp.dot(whole_panel, coupling, preferred_element_type=jnp.float32)
        factor_sum = jnp.dot(whole_panel, upper_cols, preferred_element_type=jnp.float32)
        trailing = (current.astype(jnp.float32) - product).astype(jnp.bfloat16)
        column_factor = factor_sum.astype(jnp.bfloat16)
        below_block = global_rows >= block_high
        right_block = global_cols >= block_high
        inside_cols = (global_cols >= block_low) & (global_cols < block_high)
        inside_rows = (global_rows >= block_low) & (global_rows < block_high)
        updated = jnp.where(below_block & right_block, trailing, current)
        updated = jnp.where(below_block & inside_cols, column_factor, updated)
        updated = jnp.where(inside_rows & right_block, top_factor, updated)
        current = updated
    return current


def solution(mesh):
    placed = (P("row", "col"), P(None, "row", None), P(None, "row", None))
    return jax.shard_map(
        shards, mesh=mesh, in_specs=placed, out_specs=P("row", "col"), check_vma=False
    )
```

profile of v0, /device:TPU:16, one launch (start us, length us, event | category | flops | bytes accessed | tf_op | source)
XLA Modules:
  0.0 630.7 jit_solution(4877965251172986995)
XLA Ops:
  7.4 1.9 fusion.57
  9.3 2.4 broadcast_select_fusion.8
  11.8 34.8 %all-gather.7.cloned.1.call-done = bf16[1,1024,1024]{2,1,0:T(8,128)(2,1)} async-done(((bf16[1,128,1024]{2,1,0:T(8,128)(2,1)}), bf16[1,1024,1024]{2,1,0:T(8,128)(2,1)}) %all-gather.7.cloned.1.call-update) | async-done | bytes 2097168 | tf_op jit(solution)/shard_map/all_gather | solution.py:29
  46.5 3.0 fusion.25
  49.6 0.7 all-gather.9.cloned.1.call-update
  50.5 0.1 constant_dynamic-slice_fusion.1
  50.6 12.3 %all-gather.1 = bf16[1,1024,128]{2,1,0:T(8,128)(2,1)S(1)} all-gather(bf16[1,128,128]{2,1,0:T(8,128)(2,1)S(1)} %constant_dynamic-slice_fusion.1), channel_id=3, replica_groups=mesh['row'=8,'col'=64] {'row'}, dimensions={1}, use_global_device_ids=true | all-gather | bytes 294912 | tf_op jit(solution)/shard_map/all_gather | solution.py:44
  62.9 237.2 %all-reduce.7.cloned.1.call-done = (bf16[1024,128]{1,0:T(8,128)(2,1)}, bf16[1024,128]{1,0:T(8,128)(2,1)}, bf16[1024,128]{1,0:T(8,128)(2,1)}, bf16[1024,128]{1,0:...) async-done(((bf16[1024,128]{1,0:T(8,128)(2,1)}, bf16[1024,128]{1,0:T(8,128)(2,1)}, ...) | async-done | bytes 2097168 | tf_op jit(solution)/shard_map/psum | solution.py:12
  300.0 1.1 constant_dynamic-update-slice_fusion.7
  301.1 1.0 constant_dynamic-update-slice_fusion.6
  302.2 1.0 constant_dynamic-update-slice_fusion.5
  303.2 1.0 constant_dynamic-update-slice_fusion.4
  304.7 11.8 %all_gather.25 = bf16[1024,128]{1,0:T(8,128)(2,1)S(1)} all-gather(bf16[128,128]{1,0:T(8,128)(2,1)} %reduce-scatter.3.cloned.1.call-done), channel_id=1, replica_groups=mesh['row'=8,'col'=64] {'row'}, dimensions={0}, use_global_device_ids=true | all-gather | bytes 294912 | tf_op jit(solution)/shard_map/all_gather | solution.py:37
  316.5 0.3 fusion.39
  316.8 12.5 %all_gather.27 = bf16[1024,128]{0,1:T(8,128)(2,1)S(1)} all-gather(bf16[128,128]{0,1:T(8,128)(2,1)S(1)} %fusion.39), channel_id=1, replica_groups=mesh['row'=8,'col'=64] {'row'}, dimensions={0}, use_global_device_ids=true | all-gather | bytes 294912 | tf_op jit(solution)/shard_map/all_gather | solution.py:42
  329.3 0.7 fusion.38
  330.0 2.3 broadcast_select_fusion
  332.4 3.1 fusion.30
  335.6 0.5 all-reduce.5.cloned.1.call-update
  336.2 0.1 constant_dynamic-slice_fusion
  336.2 11.9 %all-gather.3 = bf16[1,1024,128]{2,1,0:T(8,128)(2,1)S(1)} all-gather(bf16[1,128,128]{2,1,0:T(8,128)(2,1)S(1)} %constant_dynamic-slice_fusion), channel_id=5, replica_groups=mesh['row'=8,'col'=64] {'row'}, dimensions={1}, use_global_device_ids=true | all-gather | bytes 294912 | tf_op jit(solution)/shard_map/all_gather | solution.py:44
  348.1 15.6 %reduce-scatter.5.cloned.1.call-done = bf16[128,128]{1,0:T(8,128)(2,1)} async-done(((bf16[1024,128]{1,0:T(8,128)(2,1)}), bf16[128,128]{1,0:T(8,128)(2,1)}) %reduce-scatter.5.cloned.1.call-update) | async-done | bytes 32784 | tf_op jit(solution)/shard_map/reduce_scatter | solution.py:34
  363.7 16.6 %all_gather.29 = bf16[1024,128]{1,0:T(8,128)(2,1)S(1)} all-gather(bf16[128,128]{1,0:T(8,128)(2,1)} %reduce-scatter.5.cloned.1.call-done), channel_id=1, replica_groups=mesh['row'=8,'col'=64] {'row'}, dimensions={0}, use_global_device_ids=true | all-gather | bytes 294912 | tf_op jit(solution)/shard_map/all_gather | solution.py:37
  380.3 0.3 fusion.40
  380.5 12.5 %all_gather.31 = bf16[1024,128]{0,1:T(8,128)(2,1)S(1)} all-gather(bf16[128,128]{0,1:T(8,128)(2,1)S(1)} %fusion.40), channel_id=1, replica_groups=mesh['row'=8,'col'=64] {'row'}, dimensions={0}, use_global_device_ids=true | all-gather | bytes 294912 | tf_op jit(solution)/shard_map/all_gather | solution.py:42
  393.0 223.7 %all-reduce.5.cloned.1.call-done = (bf16[1024,128]{1,0:T(8,128)(2,1)}, bf16[1024,128]{1,0:T(8,128)(2,1)}, bf16[1024,128]{1,0:T(8,128)(2,1)}, bf16[1024,128]{1,0:...) async-done(((bf16[1024,128]{1,0:T(8,128)(2,1)}, bf16[1024,128]{1,0:T(8,128)(2,1)}, ...) | async-done | bytes 2097168 | tf_op jit(solution)/shard_map/psum | solution.py:12
  616.8 1.1 constant_dynamic-update-slice_fusion.15
  617.9 1.0 constant_dynamic-update-slice_fusion.14
  618.9 1.0 constant_dynamic-update-slice_fusion.13
  620.0 1.0 constant_dynamic-update-slice_fusion.12
  621.4 0.7 fusion.37
  622.2 1.4 fusion.35
  (50 shorter events, 1.1 us)
Async XLA Ops:
  7.4 39.2 %all-gather.7.cloned.1.call-start = ((), (), s32[]{:S(2)}) async-start(), calls=%async_computation.4 | async-start | bytes 2359296 | tf_op jit(solution)/shard_map/all_gather | solution.py:29
  9.3 290.8 %all-reduce.7.cloned.1.call-start = ((), (), s32[]{:S(2)}) async-start(), calls=%async_computation.7 | async-start | bytes 4194304 | tf_op jit(solution)/shard_map/psum | solution.py:12
  9.3 37.2 %copy-start.1 = (bf16[1024,128]{1,0:T(8,128)(2,1)S(1)}, bf16[1024,128]{1,0:T(8,128)(2,1)}, u32[]{:S(2)}) copy-start(bf16[1024,128]{1,0:T(8,128)(2,1)} %param.3) | copy-start | bytes 786436
  11.7 38.7 %copy-start = (bf16[2,128,1024]{2,1,0:T(8,128)(2,1)S(1)}, bf16[2,128,1024]{2,1,0:T(8,128)(2,1)}, u32[]{:S(2)}) copy-start(bf16[2,128,1024]{2,1,0:T(8,128)(2,1)} %param.5) | copy-start | bytes 1572868
  11.7 293.0 %reduce-scatter.3.cloned.1.call-start = ((), (), s32[]{:S(2)}) async-start(), calls=%async_computation.2 | async-start | bytes 294912 | tf_op jit(solution)/shard_map/reduce_scatter | solution.py:34
  49.6 282.8 %all-gather.9.cloned.1.call-start = ((), (), s32[]{:S(2)}) async-start(), calls=%async_computation.5 | async-start | bytes 2359296 | tf_op jit(solution)/shard_map/all_gather | solution.py:29
  50.3 313.4 %reduce-scatter.5.cloned.1.call-start = ((), (), s32[]{:S(2)}) async-start(), calls=%async_computation.3 | async-start | bytes 294912 | tf_op jit(solution)/shard_map/reduce_scatter | solution.py:34
  300.0 4.2 copy-start.5
  300.0 4.3 copy-start.4
  300.0 4.4 copy-start.3
  300.0 4.5 copy-start.2
  332.4 3.7 copy-start.10
  335.5 281.2 %all-reduce.5.cloned.1.call-start = ((), (), s32[]{:S(2)}) async-start(), calls=%async_computation.6 | async-start | bytes 4194304 | tf_op jit(solution)/shard_map/psum | solution.py:12
  616.8 4.3 copy-start.9
  616.8 4.4 copy-start.8
  616.8 4.5 copy-start.7
  616.8 4.6 copy-start.6
  616.8 4.7 copy-start.11
Sparse Core Ops, SparseCore 0:
  10.3 36.1 all-gather.6
  49.7 34.7 reduce-scatter.2
  86.9 36.3 all-gather.8
  335.6 28.0 reduce-scatter.4
Sparse Core Ops, SparseCore 1:
  14.7 285.3 all-reduce.6
  340.9 275.8 all-reduce.4
where the time goes:
time: 631 us
  waiting for transfers between devices  513 us (81%)
  blocking collectives  77.5 us (12%)
  between operations  15 us (2%)
  matrix products  11.8 us (2%)
  local copies, waits for them, and re-layouts  11.2 us (2%)
    psum x2, waiting for transfers between devices, spread(): return lax.psum(jnp.where(mine, value, jnp.zeros_like(value)), axis)  461 us
    all_gather x2, waiting for transfers between devices, shards(): lax.all_gather(lower_inverse[step_index], 'row', axis=0, tiled=True)  34.8 us
    all_gather x2, blocking collectives, shards(): top_factor = lax.all_gather(top_share, 'row', axis=0, tiled=True)  28.4 us
    all_gather x2, blocking collectives, shards(): coupling = lax.all_gather(coupling_piece, 'row', axis=0, tiled=True)  25 us
    all_gather x2, blocking collectives, shards(): upper_cols = lax.all_gather(upper_part, 'row', axis=0, tiled=True)  24.1 us
    reduce_scatter x2, waiting for transfers between devices, shards(): lax.psum_scatter(masked_top.astype(jnp.bfloat16), 'row', scatter_dimensio...  15.6 us
  transfers between devices with their start and end apart: 6, of which 4 were waited for; matrix products, arithmetic and copies ran while one was open for 2% of the time, Pallas kernels for 0%

commit v1 on v0

v1 whole, which is shorter than its diff:
```python
import jax
import jax.numpy as jnp
from jax import lax
from jax.sharding import Mesh, PartitionSpec as P

NB = 1024
BF = jnp.bfloat16
F32 = jnp.float32


def dot(a, b):
    return jnp.dot(a, b, preferred_element_type=F32)


def from_first(value, axis, count):
    at = lax.axis_index(axis)
    got = [lax.ppermute(value, axis, [(0, k)]) for k in range(1, count)]
    out = value
    for k in range(1, count):
        out = jnp.where(at == k, got[k - 1], out)
    return out


def both(half):
    n = half.shape[-1]
    whole = lax.all_gather(half.reshape(4, 128, n), "core", axis=1)
    return whole.reshape(1024, n)


def spread_to_all(piece, axis, count):
    copies = jnp.broadcast_to(piece[None], (count,) + piece.shape)
    return lax.all_to_all(copies, axis, 0, 0)


def shards(a, lower, upper):
    y = lax.axis_index("y")
    core = lax.axis_index("core")
    x = lax.axis_index("x")
    z = lax.axis_index("z")
    j = x * 16 + z
    in0 = j < 8
    in1 = (j >= 8) & (j < 16)
    start0 = jnp.clip(j * 128, 0, NB - 128)
    start1 = jnp.clip(j * 128 - NB, 0, NB - 128)

    piece = from_first(a, "x", 4)
    panel = lax.all_gather(piece, "z", axis=0)

    packed = jnp.concatenate([lower, upper], axis=0)
    halves = lax.all_gather(packed, "y", axis=0)
    l0, l1, u0, u1 = (halves[:, m].reshape(512, NB) for m in range(4))

    pieces = lax.all_gather(piece, "core", axis=0)
    off = jnp.where(z < 8, pieces[1], pieces[0]).reshape(4, 2, 128, 128)
    mine = lax.dynamic_slice(off, (x, core, 0, 0), (1, 1, 128, 128)).reshape(128, 128)
    off_z = spread_to_all(mine, "z", 16)
    off_all = spread_to_all(off_z, "x", 4)
    a10 = off_all[:, :8].transpose(0, 2, 1, 3).reshape(512, NB)
    a01 = off_all[:, 8:].transpose(0, 2, 1, 3).reshape(512, NB)

    tops = lax.all_gather(a, "core", axis=0)
    top0, top1 = tops[0], tops[1]
    mine1 = lax.dynamic_slice_in_dim(top1.reshape(4, 2, 128, 128), core, 1, 1).reshape(512, 128)
    r0 = both(dot(l0, top0).astype(BF))
    c0_half = dot(u0, r0).astype(BF)
    u0_cols = lax.dynamic_slice_in_dim(u0, start0, 128, 1)
    c0_half = jnp.where(in0, -u0_cols, c0_half)
    c0 = both(c0_half)
    w1 = both((mine1.astype(F32) - dot(a10, c0)).astype(BF))
    r1 = both(dot(l1, w1).astype(BF))
    c1_half = dot(u1, r1).astype(BF)
    u1_cols = lax.dynamic_slice_in_dim(u1, start1, 128, 1)
    c1_half = jnp.where(in0, jnp.zeros_like(c1_half), jnp.where(in1, -u1_cols, c1_half))
    c1 = both(c1_half)
    t = both(dot(a01, c1).astype(BF))
    s = both(dot(l0, t).astype(BF))
    base = jnp.where(in1, jnp.zeros_like(c0_half), c0_half).astype(F32)
    d_half = (base - dot(u0, s)).astype(BF)

    pair = jnp.concatenate([d_half.reshape(4, 128, 128), c1_half.reshape(4, 128, 128)], axis=0)
    pair = from_first(pair, "y", 4)
    right = lax.all_gather(pair, "core", axis=1).reshape(16, 128, 128)

    product = lax.dot_general(
        panel, right, (((0, 2), (0, 1)), ((), ())), preferred_element_type=F32
    )
    trail = (jnp.where(j >= 16, a, jnp.zeros_like(a)).astype(F32) - product).astype(BF)
    row0 = jnp.where(in0, a, r0)
    row1 = jnp.where(in0, trail, jnp.where(in1, w1, r1))
    out = jnp.where(y > 0, trail, jnp.where(core == 0, row0, row1))
    return out


def solution(mesh):
    fine = Mesh(mesh.devices.reshape(4, 2, 4, 16), ("y", "core", "x", "z"))
    placed = (
        P(("y", "core"), ("x", "z")),
        P(None, ("y", "core"), None),
        P(None, ("y", "core"), None),
    )
    return jax.shard_map(
        shards, mesh=fine, in_specs=placed, out_specs=placed[0], check_vma=False
    )
```

time: 631 us -> 163 us (0.26)
  the two profiles are of different devices: /device:TPU:16 before, /device:TPU:4 now
where the time goes in v1:
time: 163 us; the launch traced here: 162 us
  blocking collectives  63.4 us (39%)
  waiting for transfers between devices  48.6 us (30%)
  starting transfers between devices  17.9 us (11%)
  between operations  13.6 us (8%)
  matrix products  7.65 us (5%)
  local copies, waits for them, and re-layouts  6.79 us (4%)
  other arithmetic  4.08 us (3%)
    all_to_all x1, blocking collectives, spread_to_all(): return lax.all_to_all(copies, axis, 0, 0)  42.6 us
    ppermute x6, waiting for transfers between devices, from_first(): got = [lax.ppermute(value, axis, [(0, k)]) for k in range(1, count)]  23 us
    all_to_all x1, waiting for transfers between devices, spread_to_all(): return lax.all_to_all(copies, axis, 0, 0)  14.9 us
    all_gather x7, blocking collectives, both(): whole = lax.all_gather(half.reshape(4, 128, n), 'core', axis=1)  14.1 us
    all_gather x1, waiting for transfers between devices, shards(): panel = lax.all_gather(piece, 'z', axis=0)  10.7 us
    ppermute x6, starting transfers between devices, from_first(): got = [lax.ppermute(value, axis, [(0, k)]) for k in range(1, count)]  10.2 us
    all_to_all x1, starting transfers between devices, spread_to_all(): return lax.all_to_all(copies, axis, 0, 0)  7.69 us
    dot_general x1, matrix products, shards(): lax.dot_general(panel, right, (((0, 2), (0, 1)), ((), ())), preferred_ele...  4.14 us
  transfers between devices with their start and end apart: 9, of which 6 were waited for; matrix products, arithmetic and copies ran while one was open for 7% of the time, Pallas kernels for 0%

profile of v1, /device:TPU:4, one launch (start us, length us, event | category | flops | bytes accessed | tf_op | source)
XLA Modules:
  0.0 162.2 jit_solution(1285231892474857305)
XLA Ops:
  6.5 2.3 %pad_maximum_fusion = bf16[4,128,1024]{2,1,0:T(8,128)(2,1)} fusion(bf16[2,128,1024]{2,1,0:T(8,128)(2,1)} %param.5, bf16[2,128,1024]{2,1,0:T(8,128)(2,1)} %param.4), kind=kLoop, calls=%fused_computation.20 | loop fusion | flops 524288 | bytes 2097152 | tf_op jit(solution)/shard_map/concatenate | solution.py:49
  8.9 0.7 collective-permute-start
  9.6 1.3 collective-permute-start.1
  10.9 0.7 collective-permute-start.2
  11.6 12.8 %collective-permute-done.1 = bf16[1024,128]{1,0:T(8,128)(2,1)S(1)} collective-permute-done((bf16[1024,128]{1,0:T(8,128)(2,1)}, bf16[1024,128]{1,0:T(8,128)(2,1)S(1)}, u32[]{:S(2)}, u32[]{:S(2)}) %collective-permute-start.1) | collective-permute-done | bytes 262176 | tf_op jit(solution)/shard_map/ppermute | solution.py:17
  24.4 1.7 %select_select_fusion.2 = bf16[1024,128]{1,0:T(8,128)(2,1)} fusion(bf16[1024,128]{1,0:T(8,128)(2,1)S(1)} %collective-permute-done, bf16[1024,128]{1,0:T(8,128)(2,1)S(1)} %collective-permute-done.1, bf16[1024,128]{1,0:T(8,128)(2,1)S(1)} %collective-permute-done.2, bf16[1024,128]{1,0:T(8,128)(2,1)} %param.3, pred[]{:T(512)S(6)} %eq.23, pred[]{:T(512)S(6)} %eq.22, ...), kind=kLoop, calls=%fused_computation.26 | loop fusion | flops 393216 | bytes 1310723 | tf_op jit(solution)/shard_map/jit(_where)/select_n | solution.py:20
  26.1 2.4 %all-gather.3 = bf16[2048,128]{1,0:T(8,128)(2,1)S(1)} all-gather(bf16[1024,128]{1,0:T(8,128)(2,1)} %select_select_fusion.2), channel_id=5, replica_groups=mesh['y'=4,'core'=2,'x'=4,'z'=16] {'core'}, dimensions={0}, use_global_device_ids=true | all-gather | bytes 786432 | tf_op jit(solution)/shard_map/all_gather | solution.py:53
  28.7 42.6 %all_to_all.10 = bf16[16,128,128]{2,1,0:T(8,128)(2,1)S(1)} all-to-all(bf16[16,128,128]{2,1,0:T(8,128)(2,1)S(1)} %broadcast_in_dim.18), channel_id=1, replica_groups=mesh['y'=4,'core'=2,'x'=4,'z'=16] {'z'}, dimensions={0} | all-to-all | bytes 1048576 | tf_op jit(solution)/shard_map/all_to_all | solution.py:32
  71.6 1.7 %broadcast_in_dim.19 = bf16[4,16,128,128]{3,1,2,0:T(8,128)(2,1)} broadcast(bf16[16,128,128]{2,0,1:T(8,128)(2,1)S(1)} %copy.22), dimensions={1,2,3} | broadcast | bytes 2621440 | tf_op jit(solution)/shard_map/broadcast_in_dim | solution.py:31
  73.3 7.7 %all-to-all-start.1 = ((bf16[4,16,128,128]{3,1,2,0:T(8,128)(2,1)}), bf16[4,16,128,128]{3,1,2,0:T(8,128)(2,1)S(1)}, u32[]{:S(2)}, u32[]{:S(2)}) async-start(bf16[4,16,128,128]{3,1,2,0:T(8,128)(2,1)} %broadcast_in_dim.19), calls=%async_computation.1 | async-start | bytes 4194304 | tf_op jit(solution)/shard_map/all_to_all | solution.py:32
  81.0 2.2 %all-gather.2 = bf16[2048,128]{1,0:T(8,128)(2,1)S(1)} all-gather(bf16[1024,128]{1,0:T(8,128)(2,1)S(1)} %copy-done), channel_id=4, replica_groups=mesh['y'=4,'core'=2,'x'=4,'z'=16] {'core'}, dimensions={0}, use_global_device_ids=true | all-gather | bytes 786432 | tf_op jit(solution)/shard_map/all_gather | solution.py:61
  83.2 14.9 %all-to-all-done.1 = bf16[4,16,128,128]{3,1,2,0:T(8,128)(2,1)S(1)} async-done(((bf16[4,16,128,128]{3,1,2,0:T(8,128)(2,1)}), bf16[4,16,128,128]{3,1,2,0:T(8,128)(2,1)S(1)}, u32[]{:S(2)}, u32[]{:S(2)}) %all-to-all-start.1) | async-done | bytes 2097184 | tf_op jit(solution)/shard_map/all_to_all | solution.py:32
  98.1 1.8 %fusion.13 = (bf16[4,8,128,128]{3,1,2,0:T(8,128)(2,1)}, bf16[4,8,128,128]{3,1,2,0:T(8,128)(2,1)}) fusion(bf16[4,16,128,128]{3,1,2,0:T(8,128)(2,1)S(1)} %all-to-all-done.1), kind=kLoop, calls=%fused_computation.30 | loop fusion | bytes 4194304 | tf_op jit(solution)/shard_map/slice | solution.py:59
  99.9 2.8 %fusion.12 = (bf16[4,1,128,1024]{3,2,1,0:T(8,128)(2,1)S(1)}, bf16[4,1,128,1024]{3,2,1,0:T(8,128)(2,1)S(1)}, bf16[4,1,128,1024]{3,2,1,0:T(8,128)(2,1)S(1)}, bf16[4,1,128,1024]{3,2,1,0:T(8,128)(2,1)S(1)}) fusion(bf16[4,4,128,1024]{3,2,1,0:T(8,128)(2,1)} %bitcast.78), kind=kLoop, calls=%fused_computation.29 | loop fusion | bytes 8388608 | tf_op jit(solution)/shard_map/slice | solution.py:51
  103.2 2.0 %all_gather.55 = bf16[4,2,128,128]{3,2,0,1:T(8,128)(2,1)S(1)} all-gather(bf16[4,1,128,128]{3,2,0,1:T(8,128)(2,1)S(1)} %bitcast.110), channel_id=1, replica_groups=mesh['y'=4,'core'=2,'x'=4,'z'=16] {'core'}, dimensions={1}, use_global_device_ids=true | all-gather | bytes 393216 | tf_op jit(solution)/shard_map/all_gather | solution.py:26
  105.2 0.4 fusion.4
  105.7 2.1 %all_gather.57 = bf16[4,2,128,128]{3,2,1,0:T(8,128)(2,1)S(1)} all-gather(bf16[4,1,128,128]{3,2,1,0:T(8,128)(2,1)S(1)} %bitcast.107), channel_id=1, replica_groups=mesh['y'=4,'core'=2,'x'=4,'z'=16] {'core'}, dimensions={1}, use_global_device_ids=true | all-gather | bytes 393216 | tf_op jit(solution)/shard_map/all_gather | solution.py:26
  108.2 2.0 %all_gather.58 = bf16[4,2,128,128]{3,2,0,1:T(8,128)(2,1)S(1)} all-gather(bf16[4,1,128,128]{3,2,0,1:T(8,128)(2,1)S(1)} %bitcast.108), channel_id=1, replica_groups=mesh['y'=4,'core'=2,'x'=4,'z'=16] {'core'}, dimensions={1}, use_global_device_ids=true | all-gather | bytes 393216 | tf_op jit(solution)/shard_map/all_gather | solution.py:26
  110.7 2.0 %all_gather.59 = bf16[4,2,128,128]{3,2,0,1:T(8,128)(2,1)S(1)} all-gather(bf16[4,1,128,128]{3,2,0,1:T(8,128)(2,1)S(1)} %bitcast.96), channel_id=1, replica_groups=mesh['y'=4,'core'=2,'x'=4,'z'=16] {'core'}, dimensions={1}, use_global_device_ids=true | all-gather | bytes 393216 | tf_op jit(solution)/shard_map/all_gather | solution.py:26
  112.7 0.4 fusion.6
  113.2 2.0 %all_gather.60 = bf16[4,2,128,128]{3,2,1,0:T(8,128)(2,1)S(1)} all-gather(bf16[4,1,128,128]{3,2,1,0:T(8,128)(2,1)S(1)} %bitcast.82), channel_id=1, replica_groups=mesh['y'=4,'core'=2,'x'=4,'z'=16] {'core'}, dimensions={1}, use_global_device_ids=true | all-gather | bytes 393216 | tf_op jit(solution)/shard_map/all_gather | solution.py:26
  115.6 2.0 %all_gather.61 = bf16[4,2,128,128]{3,2,1,0:T(8,128)(2,1)S(1)} all-gather(bf16[4,1,128,128]{3,2,1,0:T(8,128)(2,1)S(1)} %bitcast.109), channel_id=1, replica_groups=mesh['y'=4,'core'=2,'x'=4,'z'=16] {'core'}, dimensions={1}, use_global_device_ids=true | all-gather | bytes 393216 | tf_op jit(solution)/shard_map/all_gather | solution.py:26
  118.0 2.0 %all_gather.62 = bf16[4,2,128,128]{3,2,1,0:T(8,128)(2,1)S(1)} all-gather(bf16[4,1,128,128]{3,2,1,0:T(8,128)(2,1)S(1)} %bitcast.95), channel_id=1, replica_groups=mesh['y'=4,'core'=2,'x'=4,'z'=16] {'core'}, dimensions={1}, use_global_device_ids=true | all-gather | bytes 393216 | tf_op jit(solution)/shard_map/all_gather | solution.py:26
  120.5 4.9 %collective-permute-start.3 = (bf16[8,128,128]{2,1,0:T(8,128)(2,1)S(1)}, bf16[8,128,128]{2,1,0:T(8,128)(2,1)S(1)}, u32[]{:S(2)}, u32[]{:S(2)}) collective-permute-start(bf16[8,128,128]{2,1,0:T(8,128)(2,1)S(1)} %pad_maximum_fusion.1), channel_id=1, source_target_pairs={{0,384},{1,385},{2,386},{3,387},{4,388},{5,389},{6,390},{7,391},{8... | collective-permute-start | bytes 786440 | tf_op jit(solution)/shard_map/ppermute | solution.py:17
  125.5 1.3 collective-permute-start.4
  126.8 1.3 collective-permute-start.5
  128.1 3.2 %collective-permute-done.3 = bf16[8,128,128]{2,1,0:T(8,128)(2,1)S(1)} collective-permute-done((bf16[8,128,128]{2,1,0:T(8,128)(2,1)S(1)}, bf16[8,128,128]{2,1,0:T(8,128)(2,1)S(1)}, u32[]{:S(2)}, u32[]{:S(2)}) %collective-permute-start.3) | collective-permute-done | bytes 262176 | tf_op jit(solution)/shard_map/ppermute | solution.py:17
  131.3 2.1 %collective-permute-done.4 = bf16[8,128,128]{2,1,0:T(8,128)(2,1)S(1)} collective-permute-done((bf16[8,128,128]{2,1,0:T(8,128)(2,1)S(1)}, bf16[8,128,128]{2,1,0:T(8,128)(2,1)S(1)}, u32[]{:S(2)}, u32[]{:S(2)}) %collective-permute-start.4) | collective-permute-done | bytes 262176 | tf_op jit(solution)/shard_map/ppermute | solution.py:17
  133.4 4.8 %collective-permute-done.5 = bf16[8,128,128]{2,1,0:T(8,128)(2,1)S(1)} collective-permute-done((bf16[8,128,128]{2,1,0:T(8,128)(2,1)S(1)}, bf16[8,128,128]{2,1,0:T(8,128)(2,1)S(1)}, u32[]{:S(2)}, u32[]{:S(2)}) %collective-permute-start.5) | collective-permute-done | bytes 262176 | tf_op jit(solution)/shard_map/ppermute | solution.py:17
  138.3 2.2 %all-gather.4 = bf16[8,256,128]{2,1,0:T(8,128)(2,1)S(1)} all-gather(bf16[8,128,128]{2,1,0:T(8,128)(2,1)S(1)} %select_select_fusion.1), channel_id=6, replica_groups=mesh['y'=4,'core'=2,'x'=4,'z'=16] {'core'}, dimensions={1}, use_global_device_ids=true | all-gather | bytes 786432 | tf_op jit(solution)/shard_map/all_gather | solution.py:82
  140.5 10.7 %all-gather.8.cloned.1.call-done = bf16[16384,128]{1,0:T(8,128)(2,1)} async-done(((bf16[1024,128]{1,0:T(8,128)(2,1)}), bf16[16384,128]{1,0:T(8,128)(2,1)}) %all-gather.8.cloned.1.call-update) | async-done | bytes 4194320 | tf_op jit(solution)/shard_map/all_gather | solution.py:47
  151.2 4.1 %select_select_fusion = bf16[1024,128]{1,0:T(8,128)(2,1)} fusion(bf16[16,1024,128]{2,1,0:T(8,128)(2,1)} %bitcast.112, bf16[16,128,128]{2,1,0:T(8,128)(2,1)S(1)} %bitcast.94, bf16[1024,128]{1,0:T(8,128)(2,1)S(1)} %bitcast.86, bf16[1024,128]{1,0:T(8,128)(2,1)S(1)} %bitcast.106, bf16[1024,128]{1,0:T(8,128)(2,1)S(1)} %copy-done, ...), kind=kOutput, calls=%fused_computation.24 | convolution fusion | flops 538050560 | bytes 6029317 | tf_op jit(solution)/shard_map/dot_general | solution.py:84
  (30 shorter events, 3.4 us)
Async XLA Ops:
  6.5 93.4 %all-gather.10.cloned.1.call-start = ((), (), s32[]{:S(2)}) async-start(), calls=%async_computation.3 | async-start | bytes 5242880 | tf_op jit(solution)/shard_map/all_gather | solution.py:50
  8.8 142.3 %all-gather.8.cloned.1.call-start = ((), (), s32[]{:S(2)}) async-start(), calls=%async_computation.2 | async-start | bytes 4456448 | tf_op jit(solution)/shard_map/all_gather | solution.py:47
  8.9 2.7 %collective-permute-start = (bf16[1024,128]{1,0:T(8,128)(2,1)}, bf16[1024,128]{1,0:T(8,128)(2,1)S(1)}, u32[]{:S(2)}, u32[]{:S(2)}) collective-permute-start(bf16[1024,128]{1,0:T(8,128)(2,1)} %param.3), channel_id=1, source_target_pairs={{0,48},{1,49},{2,50},{3,51},{4,52},{5,53},{6,54},{7,55},{8,56},{9,... | collective-permute-start | bytes 786440 | tf_op jit(solution)/shard_map/ppermute | solution.py:17
  9.6 14.8 %collective-permute-start.1 = (bf16[1024,128]{1,0:T(8,128)(2,1)}, bf16[1024,128]{1,0:T(8,128)(2,1)S(1)}, u32[]{:S(2)}, u32[]{:S(2)}) collective-permute-start(bf16[1024,128]{1,0:T(8,128)(2,1)} %param.3), channel_id=1, source_target_pairs={{0,32},{1,33},{2,34},{3,35},{4,36},{5,37},{6,38},{7,39},{8,40},{9,... | collective-permute-start | bytes 786440 | tf_op jit(solution)/shard_map/ppermute | solution.py:17
  10.9 13.5 %collective-permute-start.2 = (bf16[1024,128]{1,0:T(8,128)(2,1)}, bf16[1024,128]{1,0:T(8,128)(2,1)S(1)}, u32[]{:S(2)}, u32[]{:S(2)}) collective-permute-start(bf16[1024,128]{1,0:T(8,128)(2,1)} %param.3), channel_id=1, source_target_pairs={{0,16},{1,17},{2,18},{3,19},{4,20},{5,21},{6,22},{7,23},{8,24},{9,... | collective-permute-start | bytes 786440 | tf_op jit(solution)/shard_map/ppermute | solution.py:17
  71.3 9.7 %copy-start = (bf16[1024,128]{1,0:T(8,128)(2,1)S(1)}, bf16[1024,128]{1,0:T(8,128)(2,1)}, u32[]{:S(2)}) copy-start(bf16[1024,128]{1,0:T(8,128)(2,1)} %param.3) | copy-start | bytes 786436
  73.3 24.9 %all-to-all-start.1 = ((bf16[4,16,128,128]{3,1,2,0:T(8,128)(2,1)}), bf16[4,16,128,128]{3,1,2,0:T(8,128)(2,1)S(1)}, u32[]{:S(2)}, u32[]{:S(2)}) async-start(bf16[4,16,128,128]{3,1,2,0:T(8,128)(2,1)} %broadcast_in_dim.19), calls=%async_computation.1 | async-start | bytes 4194304 | tf_op jit(solution)/shard_map/all_to_all | solution.py:32
  102.7 5.1 %copy-start.2 = (bf16[4,8,128,128]{3,1,2,0:T(8,128)(2,1)S(1)}, bf16[4,8,128,128]{3,1,2,0:T(8,128)(2,1)}, u32[]{:S(2)}) copy-start(bf16[4,8,128,128]{3,1,2,0:T(8,128)(2,1)} %get-tuple-element.10) | copy-start | bytes 3145732
  105.7 9.5 %copy-start.1 = (bf16[4,8,128,128]{3,1,2,0:T(8,128)(2,1)S(1)}, bf16[4,8,128,128]{3,1,2,0:T(8,128)(2,1)}, u32[]{:S(2)}) copy-start(bf16[4,8,128,128]{3,1,2,0:T(8,128)(2,1)} %get-tuple-element.9) | copy-start | bytes 3145732
  120.5 10.8 %collective-permute-start.3 = (bf16[8,128,128]{2,1,0:T(8,128)(2,1)S(1)}, bf16[8,128,128]{2,1,0:T(8,128)(2,1)S(1)}, u32[]{:S(2)}, u32[]{:S(2)}) collective-permute-start(bf16[8,128,128]{2,1,0:T(8,128)(2,1)S(1)} %pad_maximum_fusion.1), channel_id=1, source_target_pairs={{0,384},{1,385},{2,386},{3,387},{4,388},{5,389},{6,390},{7,391},{8... | collective-permute-start | bytes 786440 | tf_op jit(solution)/shard_map/ppermute | solution.py:17
  125.5 7.9 %collective-permute-start.4 = (bf16[8,128,128]{2,1,0:T(8,128)(2,1)S(1)}, bf16[8,128,128]{2,1,0:T(8,128)(2,1)S(1)}, u32[]{:S(2)}, u32[]{:S(2)}) collective-permute-start(bf16[8,128,128]{2,1,0:T(8,128)(2,1)S(1)} %pad_maximum_fusion.1), channel_id=1, source_target_pairs={{0,256},{1,257},{2,258},{3,259},{4,260},{5,261},{6,262},{7,263},{8... | collective-permute-start | bytes 786440 | tf_op jit(solution)/shard_map/ppermute | solution.py:17
  126.8 11.5 %collective-permute-start.5 = (bf16[8,128,128]{2,1,0:T(8,128)(2,1)S(1)}, bf16[8,128,128]{2,1,0:T(8,128)(2,1)S(1)}, u32[]{:S(2)}, u32[]{:S(2)}) collective-permute-start(bf16[8,128,128]{2,1,0:T(8,128)(2,1)S(1)} %pad_maximum_fusion.1), channel_id=1, source_target_pairs={{0,128},{1,129},{2,130},{3,131},{4,132},{5,133},{6,134},{7,135},{8... | collective-permute-start | bytes 786440 | tf_op jit(solution)/shard_map/ppermute | solution.py:17
Sparse Core Ops, SparseCore 0:
  9.5 60.3 all-gather.9
  72.0 79.1 all-gather.7

commit v2 on v1

v2 whole, which is shorter than its diff:
```python
import jax
import jax.numpy as jnp
from jax import lax
from jax.sharding import Mesh, PartitionSpec as P

NB = 1024
BF = jnp.bfloat16
F32 = jnp.float32


def dot(a, b):
    return jnp.dot(a, b, preferred_element_type=F32)


def after(value, *others):
    return lax.optimization_barrier((value,) + others)[0]


def from_first(values, axis):
    at = lax.axis_index(axis)
    out = values[0]
    got = [lax.ppermute(v, axis, [(0, k)]) for k, v in enumerate(values) if k > 0]
    for k, v in enumerate(got):
        out = jnp.where(at == k + 1, v, out)
    return out


def copies(piece, count):
    return jnp.broadcast_to(piece[None], (count,) + piece.shape)


def cores(value):
    return lax.all_gather(value, "core", axis=0)


def shards(a, lower, upper):
    y = lax.axis_index("y")
    core = lax.axis_index("core")
    x = lax.axis_index("x")
    z = lax.axis_index("z")
    j = x * 16 + z
    in0 = j < 8
    in1 = (j >= 8) & (j < 16)
    zeros = jnp.zeros_like(a)

    panel = lax.all_gather(from_first([a] * 4, "x"), "z", axis=0)

    inverses = jnp.stack([lower, upper], axis=1)
    kept = lax.dynamic_index_in_dim(inverses, core, 0, False)
    given = lax.dynamic_index_in_dim(inverses, 1 - core, 0, False)
    taken = lax.ppermute(given, "core", [(0, 1), (1, 0)])
    pair = jnp.where(core == 0, jnp.stack([kept, taken], 1), jnp.stack([taken, kept], 1))
    parts = [pair] + [lax.ppermute(pair, "y", [(k, 0)]) for k in range(1, 4)]

    inv_l, inv_u = (jnp.concatenate([part[m].reshape(256, NB) for part in parts]) for m in range(2))
    inv_l, inv_u = lax.optimization_barrier((inv_l, inv_u))

    def times(inverse, right):
        return dot(inverse, right).astype(BF)

    r = times(inv_l, a)
    start = jnp.clip(j * 128 - core * NB, 0, NB - 128)
    u_cols = lax.dynamic_slice_in_dim(inv_u, start, 128, 1)
    c0 = jnp.where(in0, -u_cols, times(inv_u, r))
    c0 = cores(c0)[0]

    block = lax.dynamic_slice_in_dim(panel, 8 * (1 - core), 8, 0)

    def product(left, right):
        right = right.reshape(-1, 128, 128)
        return jnp.einsum("zrk,zkn->rn", left, right, preferred_element_type=F32)

    w = (jnp.where(in0, zeros, a).astype(F32) - product(block, c0)).astype(BF)
    r1 = times(inv_l, w)
    c1 = jnp.where(in0, zeros, jnp.where(in1, -u_cols, times(inv_u, r1)))
    c1 = cores(c1)[1]
    t = lax.optimization_barrier(product(block, c1).astype(BF))
    s = lax.optimization_barrier(times(inv_l, t))
    d = (jnp.where(in1, zeros, c0).astype(F32) - dot(inv_u, s)).astype(BF)
    right = jnp.where(core == 0, d, c1)
    right = from_first([right] * 4, "y")
    right = cores(right).reshape(2 * NB, 128)
    changed = product(panel, right)
    trail = (jnp.where(j >= 16, a, zeros).astype(F32) - changed).astype(BF)
    row0 = jnp.where(in0, a, r)
    row1 = jnp.where(j < 16, w, r1)
    return jnp.where(y > 0, trail, jnp.where(core == 0, row0, row1))


def solution(mesh):
    fine = Mesh(mesh.devices.reshape(4, 2, 4, 16), ("y", "core", "x", "z"))
    placed = (
        P(("y", "core"), ("x", "z")),
        P(None, ("y", "core"), None),
        P(None, ("y", "core"), None),
    )
    return jax.shard_map(
        shards, mesh=fine, in_specs=placed, out_specs=placed[0], check_vma=False
    )
```

time: 163 us -> 149 us (0.914)
  the two profiles are of different devices: /device:TPU:4 before, /device:TPU:9 now
where the time goes in v2:
time: 149 us
  waiting for transfers between devices  81 us (54%)
  starting transfers between devices  17.6 us (12%)
  blocking collectives  17.5 us (12%)
  between operations  13.7 us (9%)
  matrix products  11.5 us (8%)
  other arithmetic  3.83 us (3%)
  local copies, waits for them, and re-layouts  3.22 us (2%)
    all_gather x1, waiting for transfers between devices, shards(): panel = lax.all_gather(from_first([a] * 4, 'x'), 'z', axis=0)  35.5 us
    ppermute x6, waiting for transfers between devices, from_first(): lax.ppermute(v, axis, [(0, k)])  24.4 us
    ppermute x3, waiting for transfers between devices, shards(): parts = [pair] + [lax.ppermute(pair, 'y', [(k, 0)]) for k in range(1, 4)]  19.6 us
    all_gather x3, blocking collectives, cores(): return lax.all_gather(value, 'core', axis=0)  17.5 us
    ppermute x6, starting transfers between devices, from_first(): lax.ppermute(v, axis, [(0, k)])  9.65 us
    dot_general x3, matrix products, product(): return jnp.einsum('zrk,zkn->rn', left, right, preferred_element_type=F32)  7.3 us
    ppermute x3, starting transfers between devices, shards(): parts = [pair] + [lax.ppermute(pair, 'y', [(k, 0)]) for k in range(1, 4)]  4.54 us
    dot_general x6, matrix products, dot(): return jnp.dot(a, b, preferred_element_type=F32)  4.24 us
  transfers between devices with their start and end apart: 11, of which 7 were waited for; matrix products, arithmetic and copies ran while one was open for 4% of the time, Pallas kernels for 0%

profile of v2, /device:TPU:9, one launch (start us, length us, event | category | flops | bytes accessed | tf_op | source)
XLA Modules:
  0.0 148.5 jit_solution(4836966605968851653)
XLA Ops:
  6.5 4.4 %collective-permute-start = (bf16[1024,128]{1,0:T(8,128)(2,1)}, bf16[1024,128]{1,0:T(8,128)(2,1)S(1)}, u32[]{:S(2)}, u32[]{:S(2)}) collective-permute-start(bf16[1024,128]{1,0:T(8,128)(2,1)} %param.3), channel_id=1, source_target_pairs={{0,48},{1,49},{2,50},{3,51},{4,52},{5,53},{6,54},{7,55},{8,56},{9,... | collective-permute-start | bytes 786440 | tf_op jit(solution)/shard_map/ppermute | solution.py:22
  10.9 1.3 collective-permute-start.1
  12.2 1.3 collective-permute-start.2
  13.6 2.6 %collective-permute-done = bf16[1024,128]{1,0:T(8,128)(2,1)S(1)} collective-permute-done((bf16[1024,128]{1,0:T(8,128)(2,1)}, bf16[1024,128]{1,0:T(8,128)(2,1)S(1)}, u32[]{:S(2)}, u32[]{:S(2)}) %collective-permute-start) | collective-permute-done | bytes 262176 | tf_op jit(solution)/shard_map/ppermute | solution.py:22
  16.2 1.3 collective-permute-done.1
  17.5 5.6 %collective-permute-done.2 = bf16[1024,128]{1,0:T(8,128)(2,1)S(1)} collective-permute-done((bf16[1024,128]{1,0:T(8,128)(2,1)}, bf16[1024,128]{1,0:T(8,128)(2,1)S(1)}, u32[]{:S(2)}, u32[]{:S(2)}) %collective-permute-start.2) | collective-permute-done | bytes 262176 | tf_op jit(solution)/shard_map/ppermute | solution.py:22
  23.1 1.7 %select_select_fusion.1 = bf16[1024,128]{1,0:T(8,128)(2,1)} fusion(bf16[1024,128]{1,0:T(8,128)(2,1)S(1)} %collective-permute-done, bf16[1024,128]{1,0:T(8,128)(2,1)S(1)} %collective-permute-done.1, bf16[1024,128]{1,0:T(8,128)(2,1)S(1)} %collective-permute-done.2, bf16[1024,128]{1,0:T(8,128)(2,1)} %param.3, pred[]{:T(512)S(6)} %eq.25, pred[]{:T(512)S(6)} %eq.24, ...), kind=kLoop, calls=%fused_computation.37 | loop fusion | flops 393216 | bytes 1310723 | tf_op jit(solution)/shard_map/jit(_where)/select_n | solution.py:24
  24.9 1.3 fusion.30
  26.1 3.5 %collective-permute-start.3 = (bf16[2,128,1024]{2,1,0:T(8,128)(2,1)S(1)}, bf16[2,128,1024]{2,1,0:T(8,128)(2,1)S(1)}, u32[]{:S(2)}, u32[]{:S(2)}) collective-permute-start(bf16[2,128,1024]{2,1,0:T(8,128)(2,1)S(1)} %get-tuple-element.18), channel_id=1, source_target_pairs={{0,64},{64,0},{1,65},{65,1},{2,66},{66,2},{3,67},{67,3},{4,68},{68... | collective-permute-start | bytes 1572872 | tf_op jit(solution)/shard_map/ppermute | solution.py:51
  29.6 1.5 %collective-permute-done.3 = bf16[2,128,1024]{2,1,0:T(8,128)(2,1)S(1)} collective-permute-done((bf16[2,128,1024]{2,1,0:T(8,128)(2,1)S(1)}, bf16[2,128,1024]{2,1,0:T(8,128)(2,1)S(1)}, u32[]{:S(2)}, u32[]{:S(2)}) %collective-permute-start.3) | collective-permute-done | bytes 524320 | tf_op jit(solution)/shard_map/ppermute | solution.py:51
  31.3 3.1 %collective-permute-start.4 = (bf16[2,2,128,1024]{3,2,1,0:T(8,128)(2,1)S(1)}, bf16[2,2,128,1024]{3,2,1,0:T(8,128)(2,1)}, u32[]{:S(2)}, u32[]{:S(2)}) collective-permute-start(bf16[2,2,128,1024]{3,2,1,0:T(8,128)(2,1)S(1)} %maximum_select_fusion), channel_id=1, source_target_pairs={{128,0},{129,1},{130,2},{131,3},{132,4},{133,5},{134,6},{135,7},{1... | collective-permute-start | bytes 3145736 | tf_op jit(solution)/shard_map/ppermute | solution.py:53
  34.4 0.7 collective-permute-start.5
  35.1 0.7 collective-permute-start.6
  35.9 19.6 %collective-permute-done.4 = bf16[2,2,128,1024]{3,2,1,0:T(8,128)(2,1)} collective-permute-done((bf16[2,2,128,1024]{3,2,1,0:T(8,128)(2,1)S(1)}, bf16[2,2,128,1024]{3,2,1,0:T(8,128)(2,1)}, u32[]{:S(2)}, u32[]{:S(2)}) %collective-permute-start.4) | collective-permute-done | bytes 1048608 | tf_op jit(solution)/shard_map/ppermute | solution.py:53
  55.5 1.3 fusion.34
  57.9 0.7 convolution_convert_fusion.4
  58.6 0.7 fusion.22
  59.4 3.0 %all-gather.1 = bf16[2048,128]{1,0:T(8,128)(2,1)S(1)} all-gather(bf16[1024,128]{1,0:T(8,128)(2,1)S(1)} %fusion.22), channel_id=3, replica_groups=mesh['y'=4,'core'=2,'x'=4,'z'=16] {'core'}, dimensions={0}, use_global_device_ids=true | all-gather | bytes 786432 | tf_op jit(solution)/shard_map/all_gather | solution.py:33
  62.4 0.7 slice.50
  63.1 35.5 %all-gather.6.cloned.1.call-done = bf16[16384,128]{1,0:T(8,128)(2,1)} async-done(((bf16[1024,128]{1,0:T(8,128)(2,1)}), bf16[16384,128]{1,0:T(8,128)(2,1)}) %all-gather.6.cloned.1.call-update) | async-done | bytes 4194320 | tf_op jit(solution)/shard_map/all_gather | solution.py:46
  98.6 2.4 %fusion.14 = bf16[1024,128]{1,0:T(8,128)(2,1)S(1)} fusion(bf16[8,128,128]{2,1,0:T(8,128)(2,1)} %bitcast.69, bf16[16,1024,128]{2,1,0:T(8,128)(2,1)} %bitcast.61, s32[]{:T(128)S(6)} %select_n.135, bf16[1024,128]{1,0:T(8,128)(2,1)S(1)} %copy-done.3, pred[]{:T(512)S(6)} %lt.19), kind=kOutput, calls=%fused_computation.12 | convolution fusion | flops 268959744 | bytes 2883589 | tf_op jit(solution)/shard_map/zrk,zkn->rn/dot_general | solution.py:71
  101.0 0.7 convolution_convert_fusion.2
  101.8 0.7 copy-done.4
  102.5 0.7 fusion.24
  103.2 11.5 %all-gather.2 = bf16[2048,128]{1,0:T(8,128)(2,1)S(1)} all-gather(bf16[1024,128]{1,0:T(8,128)(2,1)S(1)} %fusion.24), channel_id=4, replica_groups=mesh['y'=4,'core'=2,'x'=4,'z'=16] {'core'}, dimensions={0}, use_global_device_ids=true | all-gather | bytes 786432 | tf_op jit(solution)/shard_map/all_gather | solution.py:33
  114.7 0.7 fusion.17
  115.4 0.7 convolution_convert_fusion
  116.1 0.7 fusion.25
  118.2 1.3 collective-permute-start.9
  119.6 14.9 %collective-permute-done.9 = bf16[1024,128]{1,0:T(8,128)(2,1)S(1)} collective-permute-done((bf16[1024,128]{1,0:T(8,128)(2,1)S(1)}, bf16[1024,128]{1,0:T(8,128)(2,1)S(1)}, u32[]{:S(2)}, u32[]{:S(2)}) %collective-permute-start.9) | collective-permute-done | bytes 262176 | tf_op jit(solution)/shard_map/ppermute | solution.py:22
  134.5 3.0 %all-gather.3 = bf16[2048,128]{1,0:T(8,128)(2,1)S(1)} all-gather(bf16[1024,128]{1,0:T(8,128)(2,1)S(1)} %select_select_fusion), channel_id=5, replica_groups=mesh['y'=4,'core'=2,'x'=4,'z'=16] {'core'}, dimensions={0}, use_global_device_ids=true | all-gather | bytes 786432 | tf_op jit(solution)/shard_map/all_gather | solution.py:33
  137.5 4.1 %fusion.26 = bf16[1024,128]{1,0:T(8,128)(2,1)} fusion(bf16[16,1024,128]{2,1,0:T(8,128)(2,1)} %bitcast.62, bf16[16,128,128]{2,1,0:T(8,128)(2,1)S(1)} %bitcast.66, bf16[1024,128]{1,0:T(8,128)(2,1)S(1)} %fusion.14, bf16[1024,128]{1,0:T(8,128)(2,1)S(1)} %copy-done.5, bf16[1024,128]{1,0:T(8,128)(2,1)S(1)} %copy-done.3, ...), kind=kOutput, calls=%fused_computation.29 | convolution fusion | flops 537919488 | bytes 6029317 | tf_op jit(solution)/shard_map/zrk,zkn->rn/dot_general | solution.py:71
  (26 shorter events, 2.8 us)
Async XLA Ops:
  6.5 92.1 %all-gather.6.cloned.1.call-start = ((), (), s32[]{:S(2)}) async-start(), calls=%async_computation | async-start | bytes 4456448 | tf_op jit(solution)/shard_map/all_gather | solution.py:46
  6.5 9.7 %collective-permute-start = (bf16[1024,128]{1,0:T(8,128)(2,1)}, bf16[1024,128]{1,0:T(8,128)(2,1)S(1)}, u32[]{:S(2)}, u32[]{:S(2)}) collective-permute-start(bf16[1024,128]{1,0:T(8,128)(2,1)} %param.3), channel_id=1, source_target_pairs={{0,48},{1,49},{2,50},{3,51},{4,52},{5,53},{6,54},{7,55},{8,56},{9,... | collective-permute-start | bytes 786440 | tf_op jit(solution)/shard_map/ppermute | solution.py:22
  10.9 6.6 %collective-permute-start.1 = (bf16[1024,128]{1,0:T(8,128)(2,1)}, bf16[1024,128]{1,0:T(8,128)(2,1)S(1)}, u32[]{:S(2)}, u32[]{:S(2)}) collective-permute-start(bf16[1024,128]{1,0:T(8,128)(2,1)} %param.3), channel_id=1, source_target_pairs={{0,32},{1,33},{2,34},{3,35},{4,36},{5,37},{6,38},{7,39},{8,40},{9,... | collective-permute-start | bytes 786440 | tf_op jit(solution)/shard_map/ppermute | solution.py:22
  12.2 10.9 %collective-permute-start.2 = (bf16[1024,128]{1,0:T(8,128)(2,1)}, bf16[1024,128]{1,0:T(8,128)(2,1)S(1)}, u32[]{:S(2)}, u32[]{:S(2)}) collective-permute-start(bf16[1024,128]{1,0:T(8,128)(2,1)} %param.3), channel_id=1, source_target_pairs={{0,16},{1,17},{2,18},{3,19},{4,20},{5,21},{6,22},{7,23},{8,24},{9,... | collective-permute-start | bytes 786440 | tf_op jit(solution)/shard_map/ppermute | solution.py:22
  26.1 5.0 %collective-permute-start.3 = (bf16[2,128,1024]{2,1,0:T(8,128)(2,1)S(1)}, bf16[2,128,1024]{2,1,0:T(8,128)(2,1)S(1)}, u32[]{:S(2)}, u32[]{:S(2)}) collective-permute-start(bf16[2,128,1024]{2,1,0:T(8,128)(2,1)S(1)} %get-tuple-element.18), channel_id=1, source_target_pairs={{0,64},{64,0},{1,65},{65,1},{2,66},{66,2},{3,67},{67,3},{4,68},{68... | collective-permute-start | bytes 1572872 | tf_op jit(solution)/shard_map/ppermute | solution.py:51
  31.3 24.2 %collective-permute-start.4 = (bf16[2,2,128,1024]{3,2,1,0:T(8,128)(2,1)S(1)}, bf16[2,2,128,1024]{3,2,1,0:T(8,128)(2,1)}, u32[]{:S(2)}, u32[]{:S(2)}) collective-permute-start(bf16[2,2,128,1024]{3,2,1,0:T(8,128)(2,1)S(1)} %maximum_select_fusion), channel_id=1, source_target_pairs={{128,0},{129,1},{130,2},{131,3},{132,4},{133,5},{134,6},{135,7},{1... | collective-permute-start | bytes 3145736 | tf_op jit(solution)/shard_map/ppermute | solution.py:53
  34.4 22.4 %collective-permute-start.5 = (bf16[2,2,128,1024]{3,2,1,0:T(8,128)(2,1)S(1)}, bf16[2,2,128,1024]{3,2,1,0:T(8,128)(2,1)S(1)}, u32[]{:S(2)}, u32[]{:S(2)}) collective-permute-start(bf16[2,2,128,1024]{3,2,1,0:T(8,128)(2,1)S(1)} %maximum_select_fusion), channel_id=1, source_target_pairs={{256,0},{257,1},{258,2},{259,3},{260,4},{261,5},{262,6},{263,7},{2... | collective-permute-start | bytes 3145736 | tf_op jit(solution)/shard_map/ppermute | solution.py:53
  35.1 21.8 %collective-permute-start.6 = (bf16[2,2,128,1024]{3,2,1,0:T(8,128)(2,1)S(1)}, bf16[2,2,128,1024]{3,2,1,0:T(8,128)(2,1)S(1)}, u32[]{:S(2)}, u32[]{:S(2)}) collective-permute-start(bf16[2,2,128,1024]{3,2,1,0:T(8,128)(2,1)S(1)} %maximum_select_fusion), channel_id=1, source_target_pairs={{384,0},{385,1},{386,2},{387,3},{388,4},{389,5},{390,6},{391,7},{3... | collective-permute-start | bytes 3145736 | tf_op jit(solution)/shard_map/ppermute | solution.py:53
  57.0 1.0 copy-start.3
  57.6 1.7 %copy-start = (bf16[1024,1024]{1,0:T(8,128)(2,1)}, bf16[1024,1024]{1,0:T(8,128)(2,1)S(1)}, u32[]{:S(2)}) copy-start(bf16[1024,1024]{1,0:T(8,128)(2,1)S(1)} %get-tuple-element.7) | copy-start | bytes 6291460
  98.6 3.9 %copy-start.1 = (bf16[1024,1024]{1,0:T(8,128)(2,1)S(1)}, bf16[1024,1024]{1,0:T(8,128)(2,1)}, u32[]{:S(2)}) copy-start(bf16[1024,1024]{1,0:T(8,128)(2,1)} %copy-done) | copy-start | bytes 6291460
  101.8 0.7 copy-start.4
  102.5 12.2 %copy-start.2 = (bf16[16384,128]{1,0:T(8,128)(2,1)S(1)}, bf16[16384,128]{1,0:T(8,128)(2,1)}, u32[]{:S(2)}) copy-start(bf16[16384,128]{1,0:T(8,128)(2,1)} %all-gather.6.cloned.1.call-done) | copy-start | bytes 12582916
  116.1 21.4 %copy-start.5 = (bf16[1024,128]{1,0:T(8,128)(2,1)S(1)}, bf16[1024,128]{1,0:T(8,128)(2,1)}, u32[]{:S(2)}) copy-start(bf16[1024,128]{1,0:T(8,128)(2,1)} %copy-done.4) | copy-start | bytes 786436
  116.9 2.7 %collective-permute-start.7 = (bf16[1024,128]{1,0:T(8,128)(2,1)S(1)}, bf16[1024,128]{1,0:T(8,128)(2,1)S(1)}, u32[]{:S(2)}, u32[]{:S(2)}) collective-permute-start(bf16[1024,128]{1,0:T(8,128)(2,1)S(1)} %fusion.25), channel_id=1, source_target_pairs={{0,384},{1,385},{2,386},{3,387},{4,388},{5,389},{6,390},{7,391},{8... | collective-permute-start | bytes 786440 | tf_op jit(solution)/shard_map/ppermute | solution.py:22
  117.5 2.0 %collective-permute-start.8 = (bf16[1024,128]{1,0:T(8,128)(2,1)S(1)}, bf16[1024,128]{1,0:T(8,128)(2,1)S(1)}, u32[]{:S(2)}, u32[]{:S(2)}) collective-permute-start(bf16[1024,128]{1,0:T(8,128)(2,1)S(1)} %fusion.25), channel_id=1, source_target_pairs={{0,256},{1,257},{2,258},{3,259},{4,260},{5,261},{6,262},{7,263},{8... | collective-permute-start | bytes 786440 | tf_op jit(solution)/shard_map/ppermute | solution.py:22
  118.2 16.2 %collective-permute-start.9 = (bf16[1024,128]{1,0:T(8,128)(2,1)S(1)}, bf16[1024,128]{1,0:T(8,128)(2,1)S(1)}, u32[]{:S(2)}, u32[]{:S(2)}) collective-permute-start(bf16[1024,128]{1,0:T(8,128)(2,1)S(1)} %fusion.25), channel_id=1, source_target_pairs={{0,128},{1,129},{2,130},{3,131},{4,132},{5,133},{6,134},{7,135},{8... | collective-permute-start | bytes 786440 | tf_op jit(solution)/shard_map/ppermute | solution.py:22
Sparse Core Ops, SparseCore 0:
  25.0 73.5 all-gather.5

commit v3 on v2

--- a/solution.py
+++ b/solution.py
@@ -43,15 +43,37 @@
     in1 = (j >= 8) & (j < 16)
     zeros = jnp.zeros_like(a)
 
-    panel = lax.all_gather(from_first([a] * 4, "x"), "z", axis=0)
+    share = from_first([a[256 * k : 256 * (k + 1)] for k in range(4)], "x")
 
     inverses = jnp.stack([lower, upper], axis=1)
     kept = lax.dynamic_index_in_dim(inverses, core, 0, False)
     given = lax.dynamic_index_in_dim(inverses, 1 - core, 0, False)
     taken = lax.ppermute(given, "core", [(0, 1), (1, 0)])
     pair = jnp.where(core == 0, jnp.stack([kept, taken], 1), jnp.stack([taken, kept], 1))
+    pair = after(pair, share)
     parts = [pair] + [lax.ppermute(pair, "y", [(k, 0)]) for k in range(1, 4)]
 
+    fours = [[k, k + 4, k + 8, k + 12] for k in range(4)]
+    own = lax.all_to_all(copies(share, 4), "z", 0, 0, axis_index_groups=fours)
+
+    def from_z(value, distance):
+        return lax.ppermute(value, "z", [((k + distance) % 16, k) for k in range(16)])
+
+    plus, minus = from_z(own, 1), from_z(own, -1)
+    two = jnp.concatenate([from_z(own[:, :128], 2), from_z(own[:, 128:], -2)], axis=1)
+    along = jnp.concatenate([own, plus, two, minus, own, plus, two])
+    along = lax.dynamic_slice_in_dim(along, (4 - z % 4) % 4 * 4, 16, 0).reshape(4, 4, 256, 128)
+
+    def half(which):
+        blocks = lax.dynamic_slice_in_dim(along, 2 * which, 2, 1)
+        return blocks.transpose(2, 1, 0, 3).reshape(256, NB)
+
+    sent = copies(half(1 - core), 4)
+    one = lax.all_to_all(sent, "x", 0, 0).reshape(NB, NB)
+    sent_late = copies(half(core), 4)
+    two = lax.all_to_all(sent_late, "x", 0, 0).reshape(NB, NB)
+
+    parts = [after(part, sent) for part in parts]
     inv_l, inv_u = (jnp.concatenate([part[m].reshape(256, NB) for part in parts]) for m in range(2))
     inv_l, inv_u = lax.optimization_barrier((inv_l, inv_u))
 
@@ -62,25 +84,21 @@
     start = jnp.clip(j * 128 - core * NB, 0, NB - 128)
     u_cols = lax.dynamic_slice_in_dim(inv_u, start, 128, 1)
     c0 = jnp.where(in0, -u_cols, times(inv_u, r))
+    c0 = after(c0, sent_late)
     c0 = cores(c0)[0]
 
-    block = lax.dynamic_slice_in_dim(panel, 8 * (1 - core), 8, 0)
-
-    def product(left, right):
-        right = right.reshape(-1, 128, 128)
-        return jnp.einsum("zrk,zkn->rn", left, right, preferred_element_type=F32)
-
-    w = (jnp.where(in0, zeros, a).astype(F32) - product(block, c0)).astype(BF)
+    w = (jnp.where(in0, zeros, a).astype(F32) - dot(one, c0)).astype(BF)
     r1 = times(inv_l, w)
     c1 = jnp.where(in0, zeros, jnp.where(in1, -u_cols, times(inv_u, r1)))
     c1 = cores(c1)[1]
-    t = lax.optimization_barrier(product(block, c1).astype(BF))
+    t = lax.optimization_barrier(dot(one, c1).astype(BF))
     s = lax.optimization_barrier(times(inv_l, t))
     d = (jnp.where(in1, zeros, c0).astype(F32) - dot(inv_u, s)).astype(BF)
     right = jnp.where(core == 0, d, c1)
     right = from_first([right] * 4, "y")
-    right = cores(right).reshape(2 * NB, 128)
-    changed = product(panel, right)
+    d, c1 = lax.optimization_barrier(tuple(cores(right)))
+    changed = dot(one, jnp.where(core == 1, d, c1))
+    changed += dot(two, jnp.where(core == 1, c1, d))
     trail = (jnp.where(j >= 16, a, zeros).astype(F32) - changed).astype(BF)
     row0 = jnp.where(in0, a, r)
     row1 = jnp.where(j < 16, w, r1)

time: 149 us -> 139 us (0.933)
  the two profiles are of different devices: /device:TPU:9 before, /device:TPU:11 now
where the time goes in v3:
time: 139 us; the launch traced here: 138 us
  starting transfers between devices  56.5 us (41%)
  waiting for transfers between devices  38.5 us (28%)
  matrix products  14.2 us (10%)
  blocking collectives  13.6 us (10%)
  local copies, waits for them, and re-layouts  11.2 us (8%)
  other arithmetic  3.05 us (2%)
    ppermute x6, waiting for transfers between devices, from_first(): lax.ppermute(v, axis, [(0, k)])  22.1 us
    ppermute x4, starting transfers between devices, from_z(): lax.ppermute(value, 'z', [((k + distance) % 16, k) for k in range(16)])  18.3 us
    all_to_all x1, starting transfers between devices, shards(): own = lax.all_to_all(copies(share, 4), 'z', 0, 0, axis_index_groups=fours)  14.8 us
    dot_general x10, matrix products, dot(): return jnp.dot(a, b, preferred_element_type=F32)  14.2 us
    all_gather x3, blocking collectives, cores(): return lax.all_gather(value, 'core', axis=0)  13.6 us
    ppermute x3, waiting for transfers between devices, shards(): parts = [pair] + [lax.ppermute(pair, 'y', [(k, 0)]) for k in range(1, 4)]  9.64 us
    ppermute x3, starting transfers between devices, shards(): parts = [pair] + [lax.ppermute(pair, 'y', [(k, 0)]) for k in range(1, 4)]  6.05 us
    all_to_all x1, waiting for transfers between devices, shards(): own = lax.all_to_all(copies(share, 4), 'z', 0, 0, axis_index_groups=fours)  5.3 us
  transfers between devices with their start and end apart: 17, of which 5 were waited for; matrix products, arithmetic and copies ran while one was open for 16% of the time, Pallas kernels for 0%

profile of v3, /device:TPU:11, one launch (start us, length us, event | category | flops | bytes accessed | tf_op | source)
XLA Modules:
  0.0 137.6 jit_solution(10476405710328600911)
XLA Ops:
  0.0 0.9 fusion.28
  2.3 1.3 collective-permute-start.2
  3.6 7.1 %collective-permute-done.2 = bf16[256,128]{1,0:T(8,128)(2,1)S(1)} collective-permute-done((bf16[256,128]{1,0:T(8,128)(2,1)S(1)}, bf16[256,128]{1,0:T(8,128)(2,1)S(1)}, u32[]{:S(2)}, u32[]{:S(2)}) %collective-permute-start.2) | collective-permute-done | bytes 65568 | tf_op jit(solution)/shard_map/ppermute | solution.py:22
  12.3 14.8 %all-to-all-start = ((bf16[4,256,128]{2,1,0:T(8,128)(2,1)}), bf16[4,256,128]{2,1,0:T(8,128)(2,1)S(1)}, u32[]{:S(2)}, u32[]{:S(2)}) async-start(bf16[4,256,128]{2,1,0:T(8,128)(2,1)} %broadcast_in_dim.24), calls=%async_computation | async-start | bytes 524288 | tf_op jit(solution)/shard_map/all_to_all | solution.py:57
  27.1 1.3 fusion.12
  28.4 3.2 %collective-permute-start.7 = (bf16[2,128,1024]{2,1,0:T(8,128)(2,1)S(1)}, bf16[2,128,1024]{2,1,0:T(8,128)(2,1)S(1)}, u32[]{:S(2)}, u32[]{:S(2)}) collective-permute-start(bf16[2,128,1024]{2,1,0:T(8,128)(2,1)S(1)} %get-tuple-element.36), channel_id=1, source_target_pairs={{0,64},{64,0},{1,65},{65,1},{2,66},{66,2},{3,67},{67,3},{4,68},{68... | collective-permute-start | bytes 1572872 | tf_op jit(solution)/shard_map/ppermute | solution.py:51
  31.7 1.5 %collective-permute-done.7 = bf16[2,128,1024]{2,1,0:T(8,128)(2,1)S(1)} collective-permute-done((bf16[2,128,1024]{2,1,0:T(8,128)(2,1)S(1)}, bf16[2,128,1024]{2,1,0:T(8,128)(2,1)S(1)}, u32[]{:S(2)}, u32[]{:S(2)}) %collective-permute-start.7) | collective-permute-done | bytes 524320 | tf_op jit(solution)/shard_map/ppermute | solution.py:51
  33.3 1.7 %collective-permute-start.10 = (bf16[2,2,128,1024]{3,2,1,0:T(8,128)(2,1)S(1)}, bf16[2,2,128,1024]{3,2,1,0:T(8,128)(2,1)}, u32[]{:S(2)}, u32[]{:S(2)}) collective-permute-start(bf16[2,2,128,1024]{3,2,1,0:T(8,128)(2,1)S(1)} %maximum_select_fusion), channel_id=1, source_target_pairs={{384,0},{385,1},{386,2},{387,3},{388,4},{389,5},{390,6},{391,7},{3... | collective-permute-start | bytes 3145736 | tf_op jit(solution)/shard_map/ppermute | solution.py:54
  35.0 5.3 %all-to-all-done = bf16[4,256,128]{2,1,0:T(8,128)(2,1)S(1)} async-done(((bf16[4,256,128]{2,1,0:T(8,128)(2,1)}), bf16[4,256,128]{2,1,0:T(8,128)(2,1)S(1)}, u32[]{:S(2)}, u32[]{:S(2)}) %all-to-all-start) | async-done | bytes 262176 | tf_op jit(solution)/shard_map/all_to_all | solution.py:57
  40.3 4.9 %collective-permute-start.3 = (bf16[4,256,128]{2,1,0:T(8,128)(2,1)S(1)}, bf16[4,256,128]{2,1,0:T(8,128)(2,1)S(1)}, u32[]{:S(2)}, u32[]{:S(2)}) collective-permute-start(bf16[4,256,128]{2,1,0:T(8,128)(2,1)S(1)} %all-to-all-done), channel_id=1, source_target_pairs={{1,0},{2,1},{3,2},{4,3},{5,4},{6,5},{7,6},{8,7},{9,8},{10,9},{11,1... | collective-permute-start | bytes 786440 | tf_op jit(solution)/shard_map/ppermute | solution.py:60
  45.2 7.2 %collective-permute-start.5 = (bf16[4,128,128]{2,1,0:T(8,128)(2,1)S(1)}, bf16[4,128,128]{2,1,0:T(8,128)(2,1)S(1)}, u32[]{:S(2)}, u32[]{:S(2)}) collective-permute-start(bf16[4,128,128]{2,1,0:T(8,128)(2,1)S(1)} %get-tuple-element.40), channel_id=1, source_target_pairs={{14,0},{15,1},{0,2},{1,3},{2,4},{3,5},{4,6},{5,7},{6,8},{7,9},{8,1... | collective-permute-start | bytes 393224 | tf_op jit(solution)/shard_map/ppermute | solution.py:60
  52.4 1.9 %collective-permute-start.4 = (bf16[4,128,128]{2,1,0:T(8,128)(2,1)S(1)}, bf16[4,128,128]{2,1,0:T(8,128)(2,1)S(1)}, u32[]{:S(2)}, u32[]{:S(2)}) collective-permute-start(bf16[4,128,128]{2,1,0:T(8,128)(2,1)S(1)} %get-tuple-element.39), channel_id=1, source_target_pairs={{2,0},{3,1},{4,2},{5,3},{6,4},{7,5},{8,6},{9,7},{10,8},{11,9},{12,... | collective-permute-start | bytes 393224 | tf_op jit(solution)/shard_map/ppermute | solution.py:60
  54.4 4.3 %collective-permute-start.6 = (bf16[4,256,128]{2,1,0:T(8,128)(2,1)S(1)}, bf16[4,256,128]{2,1,0:T(8,128)(2,1)S(1)}, u32[]{:S(2)}, u32[]{:S(2)}) collective-permute-start(bf16[4,256,128]{2,1,0:T(8,128)(2,1)S(1)} %all-to-all-done), channel_id=1, source_target_pairs={{15,0},{0,1},{1,2},{2,3},{3,4},{4,5},{5,6},{6,7},{7,8},{8,9},{9,10... | collective-permute-start | bytes 786440 | tf_op jit(solution)/shard_map/ppermute | solution.py:60
  58.7 1.7 %collective-permute-start.9 = (bf16[2,2,128,1024]{3,2,1,0:T(8,128)(2,1)S(1)}, bf16[2,2,128,1024]{3,2,1,0:T(8,128)(2,1)}, u32[]{:S(2)}, u32[]{:S(2)}) collective-permute-start(bf16[2,2,128,1024]{3,2,1,0:T(8,128)(2,1)S(1)} %maximum_select_fusion), channel_id=1, source_target_pairs={{256,0},{257,1},{258,2},{259,3},{260,4},{261,5},{262,6},{263,7},{2... | collective-permute-start | bytes 3145736 | tf_op jit(solution)/shard_map/ppermute | solution.py:54
  60.4 2.7 %collective-permute-start.8 = (bf16[2,2,128,1024]{3,2,1,0:T(8,128)(2,1)S(1)}, bf16[2,2,128,1024]{3,2,1,0:T(8,128)(2,1)}, u32[]{:S(2)}, u32[]{:S(2)}) collective-permute-start(bf16[2,2,128,1024]{3,2,1,0:T(8,128)(2,1)S(1)} %maximum_select_fusion), channel_id=1, source_target_pairs={{128,0},{129,1},{130,2},{131,3},{132,4},{133,5},{134,6},{135,7},{1... | collective-permute-start | bytes 3145736 | tf_op jit(solution)/shard_map/ppermute | solution.py:54
  64.0 1.6 %broadcast_in_dim.26 = bf16[4,256,1024]{2,1,0:T(8,128)(2,1)} broadcast(bf16[256,1024]{1,0:T(8,128)(2,1)S(1)} %copy.7), dimensions={1,2} | broadcast | bytes 2621440 | tf_op jit(solution)/shard_map/broadcast_in_dim | solution.py:29
  65.6 4.4 %all-to-all-start.1 = ((bf16[4,256,1024]{2,1,0:T(8,128)(2,1)}), bf16[4,256,1024]{2,1,0:T(8,128)(2,1)}, u32[]{:S(2)}, u32[]{:S(2)}) async-start(bf16[4,256,1024]{2,1,0:T(8,128)(2,1)} %broadcast_in_dim.26), calls=%async_computation.1 | async-start | bytes 4194304 | tf_op jit(solution)/shard_map/all_to_all | solution.py:72
  70.6 1.3 fusion.25
  71.8 9.6 %collective-permute-done.8 = bf16[2,2,128,1024]{3,2,1,0:T(8,128)(2,1)} collective-permute-done((bf16[2,2,128,1024]{3,2,1,0:T(8,128)(2,1)S(1)}, bf16[2,2,128,1024]{3,2,1,0:T(8,128)(2,1)}, u32[]{:S(2)}, u32[]{:S(2)}) %collective-permute-start.8) | collective-permute-done | bytes 1048608 | tf_op jit(solution)/shard_map/ppermute | solution.py:54
  81.5 1.3 fusion.24
  82.7 1.3 fusion.23
  86.4 1.6 %broadcast_in_dim.28 = bf16[4,256,1024]{2,1,0:T(8,128)(2,1)} broadcast(bf16[256,1024]{1,0:T(8,128)(2,1)S(1)} %copy.9), dimensions={1,2} | broadcast | bytes 2621440 | tf_op jit(solution)/shard_map/broadcast_in_dim | solution.py:29
  88.0 5.8 %all-gather = bf16[2048,128]{1,0:T(8,128)(2,1)S(1)} all-gather(bf16[1024,128]{1,0:T(8,128)(2,1)S(1)} %fusion.4), channel_id=2, replica_groups=mesh['y'=4,'core'=2,'x'=4,'z'=16] {'core'}, dimensions={0}, use_global_device_ids=true | all-gather | bytes 786432 | tf_op jit(solution)/shard_map/all_gather | solution.py:33
  93.9 4.4 %all-to-all-start.2 = ((bf16[4,256,1024]{2,1,0:T(8,128)(2,1)}), bf16[4,256,1024]{2,1,0:T(8,128)(2,1)}, u32[]{:S(2)}, u32[]{:S(2)}) async-start(bf16[4,256,1024]{2,1,0:T(8,128)(2,1)} %broadcast_in_dim.28), calls=%async_computation.2 | async-start | bytes 4194304 | tf_op jit(solution)/shard_map/all_to_all | solution.py:74
  98.3 2.3 %fusion.2 = bf16[1024,128]{1,0:T(8,128)(2,1)S(1)} fusion(bf16[1024,1024]{1,0:T(8,128)(2,1)} %bitcast.3, bf16[1024,128]{1,0:T(8,128)(2,1)S(1)} %copy-done.2, pred[]{:T(512)S(6)} %lt.39, bf16[2048,128]{1,0:T(8,128)(2,1)S(1)} %all-gather), kind=kOutput, calls=%fused_computation.13 | convolution fusion | flops 268959744 | bytes 2883585 | tf_op jit(solution)/shard_map/dot_general | solution.py:12
  102.9 4.7 %all-gather.1 = bf16[2048,128]{1,0:T(8,128)(2,1)S(1)} all-gather(bf16[1024,128]{1,0:T(8,128)(2,1)S(1)} %fusion.7), channel_id=3, replica_groups=mesh['y'=4,'core'=2,'x'=4,'z'=16] {'core'}, dimensions={0}, use_global_device_ids=true | all-gather | bytes 786432 | tf_op jit(solution)/shard_map/all_gather | solution.py:33
  107.7 2.3 %convolution_convert_fusion.1 = bf16[1024,128]{1,0:T(8,128)(2,1)S(1)} fusion(bf16[1024,1024]{1,0:T(8,128)(2,1)} %bitcast.3, bf16[2048,128]{1,0:T(8,128)(2,1)S(1)} %all-gather.1), kind=kOutput, calls=%fused_computation.8 | convolution fusion | flops 268566528 | bytes 2621440 | tf_op jit(solution)/shard_map/dot_general | solution.py:12
  112.8 1.3 collective-permute-start.13
  114.1 15.0 %collective-permute-done.13 = bf16[1024,128]{1,0:T(8,128)(2,1)S(1)} collective-permute-done((bf16[1024,128]{1,0:T(8,128)(2,1)S(1)}, bf16[1024,128]{1,0:T(8,128)(2,1)S(1)}, u32[]{:S(2)}, u32[]{:S(2)}) %collective-permute-start.13) | collective-permute-done | bytes 262176 | tf_op jit(solution)/shard_map/ppermute | solution.py:22
  129.1 3.0 %all-gather.2 = bf16[2048,128]{1,0:T(8,128)(2,1)S(1)} all-gather(bf16[1024,128]{1,0:T(8,128)(2,1)S(1)} %select_select_fusion), channel_id=4, replica_groups=mesh['y'=4,'core'=2,'x'=4,'z'=16] {'core'}, dimensions={0}, use_global_device_ids=true | all-gather | bytes 786432 | tf_op jit(solution)/shard_map/all_gather | solution.py:33
  132.2 2.3 %fusion.14 = f32[1024,128]{1,0:T(8,128)S(1)} fusion(bf16[1024,1024]{1,0:T(8,128)(2,1)} %bitcast.3, bf16[1024,128]{1,0:T(8,128)(2,1)S(1)} %get-tuple-element.23, bf16[1024,128]{1,0:T(8,128)(2,1)S(1)} %get-tuple-element.24, pred[]{:T(512)S(6)} %eq.33), kind=kOutput, calls=%fused_computation.33 | convolution fusion | flops 268566528 | bytes 3145729 | tf_op jit(solution)/shard_map/dot_general | solution.py:12
  134.6 3.0 %fusion.6 = bf16[1024,128]{1,0:T(8,128)(2,1)} fusion(f32[1024,128]{1,0:T(8,128)S(1)} %fusion.14, bf16[1024,1024]{1,0:T(8,128)(2,1)} %bitcast.19, bf16[1024,128]{1,0:T(8,128)(2,1)S(1)} %fusion.2, bf16[1024,128]{1,0:T(8,128)(2,1)S(1)} %copy-done.4, bf16[1024,128]{1,0:T(8,128)(2,1)S(1)} %copy-done.2, bf16[1024,128]{1,0:T(8,128)(2,1)S(1)} %convolution_convert_fusion.5, ...), kind=kOutput, calls=%fused_computation.21 | convolution fusion | flops 269746176 | bytes 4456454 | tf_op jit(solution)/shard_map/dot_general | solution.py:12
  (53 shorter events, 11.9 us)
Async XLA Ops:
  0.9 2.7 %collective-permute-start = (bf16[256,128]{1,0:T(8,128)(2,1)S(1)}, bf16[256,128]{1,0:T(8,128)(2,1)S(1)}, u32[]{:S(2)}, u32[]{:S(2)}) collective-permute-start(bf16[256,128]{1,0:T(8,128)(2,1)S(1)} %get-tuple-element.43), channel_id=1, source_target_pairs={{0,48},{1,49},{2,50},{3,51},{4,52},{5,53},{6,54},{7,55},{8,56},{9,... | collective-permute-start | bytes 196616 | tf_op jit(solution)/shard_map/ppermute | solution.py:22
  1.6 2.0 %collective-permute-start.1 = (bf16[256,128]{1,0:T(8,128)(2,1)S(1)}, bf16[256,128]{1,0:T(8,128)(2,1)S(1)}, u32[]{:S(2)}, u32[]{:S(2)}) collective-permute-start(bf16[256,128]{1,0:T(8,128)(2,1)S(1)} %get-tuple-element.42), channel_id=1, source_target_pairs={{0,32},{1,33},{2,34},{3,35},{4,36},{5,37},{6,38},{7,39},{8,40},{9,... | collective-permute-start | bytes 196616 | tf_op jit(solution)/shard_map/ppermute | solution.py:22
  2.3 8.4 %collective-permute-start.2 = (bf16[256,128]{1,0:T(8,128)(2,1)S(1)}, bf16[256,128]{1,0:T(8,128)(2,1)S(1)}, u32[]{:S(2)}, u32[]{:S(2)}) collective-permute-start(bf16[256,128]{1,0:T(8,128)(2,1)S(1)} %get-tuple-element.41), channel_id=1, source_target_pairs={{0,16},{1,17},{2,18},{3,19},{4,20},{5,21},{6,22},{7,23},{8,24},{9,... | collective-permute-start | bytes 196616 | tf_op jit(solution)/shard_map/ppermute | solution.py:22
  12.3 28.0 %all-to-all-start = ((bf16[4,256,128]{2,1,0:T(8,128)(2,1)}), bf16[4,256,128]{2,1,0:T(8,128)(2,1)S(1)}, u32[]{:S(2)}, u32[]{:S(2)}) async-start(bf16[4,256,128]{2,1,0:T(8,128)(2,1)} %broadcast_in_dim.24), calls=%async_computation | async-start | bytes 524288 | tf_op jit(solution)/shard_map/all_to_all | solution.py:57
  28.4 4.7 %collective-permute-start.7 = (bf16[2,128,1024]{2,1,0:T(8,128)(2,1)S(1)}, bf16[2,128,1024]{2,1,0:T(8,128)(2,1)S(1)}, u32[]{:S(2)}, u32[]{:S(2)}) collective-permute-start(bf16[2,128,1024]{2,1,0:T(8,128)(2,1)S(1)} %get-tuple-element.36), channel_id=1, source_target_pairs={{0,64},{64,0},{1,65},{65,1},{2,66},{66,2},{3,67},{67,3},{4,68},{68... | collective-permute-start | bytes 1572872 | tf_op jit(solution)/shard_map/ppermute | solution.py:51
  33.3 37.3 %collective-permute-start.10 = (bf16[2,2,128,1024]{3,2,1,0:T(8,128)(2,1)S(1)}, bf16[2,2,128,1024]{3,2,1,0:T(8,128)(2,1)}, u32[]{:S(2)}, u32[]{:S(2)}) collective-permute-start(bf16[2,2,128,1024]{3,2,1,0:T(8,128)(2,1)S(1)} %maximum_select_fusion), channel_id=1, source_target_pairs={{384,0},{385,1},{386,2},{387,3},{388,4},{389,5},{390,6},{391,7},{3... | collective-permute-start | bytes 3145736 | tf_op jit(solution)/shard_map/ppermute | solution.py:54
  40.3 18.4 %collective-permute-start.3 = (bf16[4,256,128]{2,1,0:T(8,128)(2,1)S(1)}, bf16[4,256,128]{2,1,0:T(8,128)(2,1)S(1)}, u32[]{:S(2)}, u32[]{:S(2)}) collective-permute-start(bf16[4,256,128]{2,1,0:T(8,128)(2,1)S(1)} %all-to-all-done), channel_id=1, source_target_pairs={{1,0},{2,1},{3,2},{4,3},{5,4},{6,5},{7,6},{8,7},{9,8},{10,9},{11,1... | collective-permute-start | bytes 786440 | tf_op jit(solution)/shard_map/ppermute | solution.py:60
  45.2 15.2 %collective-permute-start.5 = (bf16[4,128,128]{2,1,0:T(8,128)(2,1)S(1)}, bf16[4,128,128]{2,1,0:T(8,128)(2,1)S(1)}, u32[]{:S(2)}, u32[]{:S(2)}) collective-permute-start(bf16[4,128,128]{2,1,0:T(8,128)(2,1)S(1)} %get-tuple-element.40), channel_id=1, source_target_pairs={{14,0},{15,1},{0,2},{1,3},{2,4},{3,5},{4,6},{5,7},{6,8},{7,9},{8,1... | collective-permute-start | bytes 393224 | tf_op jit(solution)/shard_map/ppermute | solution.py:60
  52.4 10.7 %collective-permute-start.4 = (bf16[4,128,128]{2,1,0:T(8,128)(2,1)S(1)}, bf16[4,128,128]{2,1,0:T(8,128)(2,1)S(1)}, u32[]{:S(2)}, u32[]{:S(2)}) collective-permute-start(bf16[4,128,128]{2,1,0:T(8,128)(2,1)S(1)} %get-tuple-element.39), channel_id=1, source_target_pairs={{2,0},{3,1},{4,2},{5,3},{6,4},{7,5},{8,6},{9,7},{10,8},{11,9},{12,... | collective-permute-start | bytes 393224 | tf_op jit(solution)/shard_map/ppermute | solution.py:60
  54.4 8.8 %collective-permute-start.6 = (bf16[4,256,128]{2,1,0:T(8,128)(2,1)S(1)}, bf16[4,256,128]{2,1,0:T(8,128)(2,1)S(1)}, u32[]{:S(2)}, u32[]{:S(2)}) collective-permute-start(bf16[4,256,128]{2,1,0:T(8,128)(2,1)S(1)} %all-to-all-done), channel_id=1, source_target_pairs={{15,0},{0,1},{1,2},{2,3},{3,4},{4,5},{5,6},{6,7},{7,8},{8,9},{9,10... | collective-permute-start | bytes 786440 | tf_op jit(solution)/shard_map/ppermute | solution.py:60
  58.7 11.8 %collective-permute-start.9 = (bf16[2,2,128,1024]{3,2,1,0:T(8,128)(2,1)S(1)}, bf16[2,2,128,1024]{3,2,1,0:T(8,128)(2,1)}, u32[]{:S(2)}, u32[]{:S(2)}) collective-permute-start(bf16[2,2,128,1024]{3,2,1,0:T(8,128)(2,1)S(1)} %maximum_select_fusion), channel_id=1, source_target_pairs={{256,0},{257,1},{258,2},{259,3},{260,4},{261,5},{262,6},{263,7},{2... | collective-permute-start | bytes 3145736 | tf_op jit(solution)/shard_map/ppermute | solution.py:54
  60.4 21.0 %collective-permute-start.8 = (bf16[2,2,128,1024]{3,2,1,0:T(8,128)(2,1)S(1)}, bf16[2,2,128,1024]{3,2,1,0:T(8,128)(2,1)}, u32[]{:S(2)}, u32[]{:S(2)}) collective-permute-start(bf16[2,2,128,1024]{3,2,1,0:T(8,128)(2,1)S(1)} %maximum_select_fusion), channel_id=1, source_target_pairs={{128,0},{129,1},{130,2},{131,3},{132,4},{133,5},{134,6},{135,7},{1... | collective-permute-start | bytes 3145736 | tf_op jit(solution)/shard_map/ppermute | solution.py:54
  65.6 28.3 %all-to-all-start.1 = ((bf16[4,256,1024]{2,1,0:T(8,128)(2,1)}), bf16[4,256,1024]{2,1,0:T(8,128)(2,1)}, u32[]{:S(2)}, u32[]{:S(2)}) async-start(bf16[4,256,1024]{2,1,0:T(8,128)(2,1)} %broadcast_in_dim.26), calls=%async_computation.1 | async-start | bytes 4194304 | tf_op jit(solution)/shard_map/all_to_all | solution.py:72
  84.0 1.0 copy-start.2
  84.7 1.7 %copy-start = (bf16[1024,1024]{1,0:T(8,128)(2,1)}, bf16[1024,1024]{1,0:T(8,128)(2,1)S(1)}, u32[]{:S(2)}) copy-start(bf16[1024,1024]{1,0:T(8,128)(2,1)S(1)} %get-tuple-element.20) | copy-start | bytes 6291460
  93.9 40.6 %all-to-all-start.2 = ((bf16[4,256,1024]{2,1,0:T(8,128)(2,1)}), bf16[4,256,1024]{2,1,0:T(8,128)(2,1)}, u32[]{:S(2)}, u32[]{:S(2)}) async-start(bf16[4,256,1024]{2,1,0:T(8,128)(2,1)} %broadcast_in_dim.28), calls=%async_computation.2 | async-start | bytes 4194304 | tf_op jit(solution)/shard_map/all_to_all | solution.py:74
  100.6 1.6 %copy-start.1 = (bf16[1024,1024]{1,0:T(8,128)(2,1)S(1)}, bf16[1024,1024]{1,0:T(8,128)(2,1)}, u32[]{:S(2)}) copy-start(bf16[1024,1024]{1,0:T(8,128)(2,1)} %copy-done) | copy-start | bytes 6291460
  101.4 0.7 copy-start.3
  111.4 2.7 %collective-permute-start.11 = (bf16[1024,128]{1,0:T(8,128)(2,1)S(1)}, bf16[1024,128]{1,0:T(8,128)(2,1)S(1)}, u32[]{:S(2)}, u32[]{:S(2)}) collective-permute-start(bf16[1024,128]{1,0:T(8,128)(2,1)S(1)} %fusion.8), channel_id=1, source_target_pairs={{0,384},{1,385},{2,386},{3,387},{4,388},{5,389},{6,390},{7,391},{8... | collective-permute-start | bytes 786440 | tf_op jit(solution)/shard_map/ppermute | solution.py:22
  112.1 2.0 %collective-permute-start.12 = (bf16[1024,128]{1,0:T(8,128)(2,1)S(1)}, bf16[1024,128]{1,0:T(8,128)(2,1)S(1)}, u32[]{:S(2)}, u32[]{:S(2)}) collective-permute-start(bf16[1024,128]{1,0:T(8,128)(2,1)S(1)} %fusion.8), channel_id=1, source_target_pairs={{0,256},{1,257},{2,258},{3,259},{4,260},{5,261},{6,262},{7,263},{8... | collective-permute-start | bytes 786440 | tf_op jit(solution)/shard_map/ppermute | solution.py:22
  112.8 16.3 %collective-permute-start.13 = (bf16[1024,128]{1,0:T(8,128)(2,1)S(1)}, bf16[1024,128]{1,0:T(8,128)(2,1)S(1)}, u32[]{:S(2)}, u32[]{:S(2)}) collective-permute-start(bf16[1024,128]{1,0:T(8,128)(2,1)S(1)} %fusion.8), channel_id=1, source_target_pairs={{0,128},{1,129},{2,130},{3,131},{4,132},{5,133},{6,134},{7,135},{8... | collective-permute-start | bytes 786440 | tf_op jit(solution)/shard_map/ppermute | solution.py:22
  132.2 2.4 %copy-start.4 = (bf16[1024,128]{1,0:T(8,128)(2,1)S(1)}, bf16[1024,128]{1,0:T(8,128)(2,1)}, u32[]{:S(2)}) copy-start(bf16[1024,128]{1,0:T(8,128)(2,1)} %copy-done.3) | copy-start | bytes 786436

commit v4 on v3

--- a/solution.py
+++ b/solution.py
@@ -60,20 +60,17 @@
         return lax.ppermute(value, "z", [((k + distance) % 16, k) for k in range(16)])
 
     plus, minus = from_z(own, 1), from_z(own, -1)
-    two = jnp.concatenate([from_z(own[:, :128], 2), from_z(own[:, 128:], -2)], axis=1)
+    two = lax.ppermute(own, "z", [((k + 2 - 4 * (k % 2)) % 16, k) for k in range(16)])
     along = jnp.concatenate([own, plus, two, minus, own, plus, two])
     along = lax.dynamic_slice_in_dim(along, (4 - z % 4) % 4 * 4, 16, 0).reshape(4, 4, 256, 128)
 
     def half(which):
         blocks = lax.dynamic_slice_in_dim(along, 2 * which, 2, 1)
-        return blocks.transpose(2, 1, 0, 3).reshape(256, NB)
+        return blocks.transpose(1, 0, 2, 3).reshape(8, 256, 128)
 
     sent = copies(half(1 - core), 4)
-    one = lax.all_to_all(sent, "x", 0, 0).reshape(NB, NB)
-    sent_late = copies(half(core), 4)
-    two = lax.all_to_all(sent_late, "x", 0, 0).reshape(NB, NB)
+    one = lax.all_to_all(sent, "x", 0, 0)
 
-    parts = [after(part, sent) for part in parts]
     inv_l, inv_u = (jnp.concatenate([part[m].reshape(256, NB) for part in parts]) for m in range(2))
     inv_l, inv_u = lax.optimization_barrier((inv_l, inv_u))
 
@@ -84,20 +81,27 @@
     start = jnp.clip(j * 128 - core * NB, 0, NB - 128)
     u_cols = lax.dynamic_slice_in_dim(inv_u, start, 128, 1)
     c0 = jnp.where(in0, -u_cols, times(inv_u, r))
+    sent_late = after(half(core), r).transpose(1, 0, 2).reshape(256, NB)
+    sent_late = copies(sent_late, 4)
+    two = lax.all_to_all(sent_late, "x", 0, 0).reshape(NB, NB)
     c0 = after(c0, sent_late)
-    c0 = cores(c0)[0]
+    c0x = lax.ppermute(c0, ("y", "core"), [(0, 1)])
 
-    w = (jnp.where(in0, zeros, a).astype(F32) - dot(one, c0)).astype(BF)
+    def product(left, right):
+        right = right.reshape(8, 128, 128)
+        return jnp.einsum("xzrk,zkn->xrn", left, right, preferred_element_type=F32).reshape(NB, 128)
+
+    w = (jnp.where(in0, zeros, a).astype(F32) - product(one, c0x)).astype(BF)
     r1 = times(inv_l, w)
     c1 = jnp.where(in0, zeros, jnp.where(in1, -u_cols, times(inv_u, r1)))
     c1 = cores(c1)[1]
-    t = lax.optimization_barrier(dot(one, c1).astype(BF))
+    t = lax.optimization_barrier(product(one, c1).astype(BF))
     s = lax.optimization_barrier(times(inv_l, t))
     d = (jnp.where(in1, zeros, c0).astype(F32) - dot(inv_u, s)).astype(BF)
     right = jnp.where(core == 0, d, c1)
     right = from_first([right] * 4, "y")
     d, c1 = lax.optimization_barrier(tuple(cores(right)))
-    changed = dot(one, jnp.where(core == 1, d, c1))
+    changed = product(one, jnp.where(core == 1, d, c1))
     changed += dot(two, jnp.where(core == 1, c1, d))
     trail = (jnp.where(j >= 16, a, zeros).astype(F32) - changed).astype(BF)
     row0 = jnp.where(in0, a, r)

time: 139 us -> 138 us (level)
  the two profiles are of different devices: /device:TPU:11 before, /device:TPU:43 now
where the time goes in v4:
time: 138 us; the launch traced here: 136 us
  waiting for transfers between devices  52 us (38%)
  starting transfers between devices  47.2 us (34%)
  local copies, waits for them, and re-layouts  14.1 us (10%)
  matrix products  11.1 us (8%)
  blocking collectives  7.5 us (5%)
  other arithmetic  4.04 us (3%)
    ppermute x6, waiting for transfers between devices, from_first(): lax.ppermute(v, axis, [(0, k)])  22.2 us
    all_to_all x1, starting transfers between devices, shards(): own = lax.all_to_all(copies(share, 4), 'z', 0, 0, axis_index_groups=fours)  13.9 us
    all_to_all x1, waiting for transfers between devices, shards(): one = lax.all_to_all(sent, 'x', 0, 0)  10.4 us
    all_to_all x1, waiting for transfers between devices, shards(): own = lax.all_to_all(copies(share, 4), 'z', 0, 0, axis_index_groups=fours)  10.1 us
    dot_general x7, matrix products, dot(): return jnp.dot(a, b, preferred_element_type=F32)  8.93 us
    all_gather x2, blocking collectives, cores(): return lax.all_gather(value, 'core', axis=0)  7.5 us
    ppermute x2, waiting for transfers between devices, from_z(): lax.ppermute(value, 'z', [((k + distance) % 16, k) for k in range(16)])  7.5 us
    ppermute x3, starting transfers between devices, shards(): parts = [pair] + [lax.ppermute(pair, 'y', [(k, 0)]) for k in range(1, 4)]  6.39 us
  transfers between devices with their start and end apart: 17, of which 7 were waited for; matrix products, arithmetic and copies ran while one was open for 16% of the time, Pallas kernels for 0%

profile of v4, /device:TPU:43, one launch (start us, length us, event | category | flops | bytes accessed | tf_op | source)
XLA Modules:
  0.0 136.5 jit_solution(14146257012820737640)
XLA Ops:
  0.0 0.9 fusion.22
  2.3 1.3 collective-permute-start.2
  3.6 7.1 %collective-permute-done.2 = bf16[256,128]{1,0:T(8,128)(2,1)S(1)} collective-permute-done((bf16[256,128]{1,0:T(8,128)(2,1)S(1)}, bf16[256,128]{1,0:T(8,128)(2,1)S(1)}, u32[]{:S(2)}, u32[]{:S(2)}) %collective-permute-start.2) | collective-permute-done | bytes 65568 | tf_op jit(solution)/shard_map/ppermute | solution.py:22
  12.3 13.9 %all-to-all-start = ((bf16[4,256,128]{2,1,0:T(8,128)(2,1)}), bf16[4,256,128]{2,1,0:T(8,128)(2,1)S(1)}, u32[]{:S(2)}, u32[]{:S(2)}) async-start(bf16[4,256,128]{2,1,0:T(8,128)(2,1)} %broadcast_in_dim.24), calls=%async_computation | async-start | bytes 524288 | tf_op jit(solution)/shard_map/all_to_all | solution.py:57
  26.2 1.3 fusion.14
  27.5 3.2 %collective-permute-start.6 = (bf16[2,128,1024]{2,1,0:T(8,128)(2,1)S(1)}, bf16[2,128,1024]{2,1,0:T(8,128)(2,1)S(1)}, u32[]{:S(2)}, u32[]{:S(2)}) collective-permute-start(bf16[2,128,1024]{2,1,0:T(8,128)(2,1)S(1)} %get-tuple-element.30), channel_id=1, source_target_pairs={{0,64},{64,0},{1,65},{65,1},{2,66},{66,2},{3,67},{67,3},{4,68},{68... | collective-permute-start | bytes 1572872 | tf_op jit(solution)/shard_map/ppermute | solution.py:51
  30.8 1.5 %collective-permute-done.6 = bf16[2,128,1024]{2,1,0:T(8,128)(2,1)S(1)} collective-permute-done((bf16[2,128,1024]{2,1,0:T(8,128)(2,1)S(1)}, bf16[2,128,1024]{2,1,0:T(8,128)(2,1)S(1)}, u32[]{:S(2)}, u32[]{:S(2)}) %collective-permute-start.6) | collective-permute-done | bytes 524320 | tf_op jit(solution)/shard_map/ppermute | solution.py:51
  32.4 1.7 %collective-permute-start.9 = (bf16[2,2,128,1024]{3,2,1,0:T(8,128)(2,1)S(1)}, bf16[2,2,128,1024]{3,2,1,0:T(8,128)(2,1)}, u32[]{:S(2)}, u32[]{:S(2)}) collective-permute-start(bf16[2,2,128,1024]{3,2,1,0:T(8,128)(2,1)S(1)} %maximum_select_fusion), channel_id=1, source_target_pairs={{384,0},{385,1},{386,2},{387,3},{388,4},{389,5},{390,6},{391,7},{3... | collective-permute-start | bytes 3145736 | tf_op jit(solution)/shard_map/ppermute | solution.py:54
  34.1 1.7 %collective-permute-start.8 = (bf16[2,2,128,1024]{3,2,1,0:T(8,128)(2,1)S(1)}, bf16[2,2,128,1024]{3,2,1,0:T(8,128)(2,1)}, u32[]{:S(2)}, u32[]{:S(2)}) collective-permute-start(bf16[2,2,128,1024]{3,2,1,0:T(8,128)(2,1)S(1)} %maximum_select_fusion), channel_id=1, source_target_pairs={{256,0},{257,1},{258,2},{259,3},{260,4},{261,5},{262,6},{263,7},{2... | collective-permute-start | bytes 3145736 | tf_op jit(solution)/shard_map/ppermute | solution.py:54
  35.7 10.1 %all-to-all-done = bf16[4,256,128]{2,1,0:T(8,128)(2,1)S(1)} async-done(((bf16[4,256,128]{2,1,0:T(8,128)(2,1)}), bf16[4,256,128]{2,1,0:T(8,128)(2,1)S(1)}, u32[]{:S(2)}, u32[]{:S(2)}) %all-to-all-start) | async-done | bytes 262176 | tf_op jit(solution)/shard_map/all_to_all | solution.py:57
  45.8 1.9 %collective-permute-start.3 = (bf16[4,256,128]{2,1,0:T(8,128)(2,1)S(1)}, bf16[4,256,128]{2,1,0:T(8,128)(2,1)S(1)}, u32[]{:S(2)}, u32[]{:S(2)}) collective-permute-start(bf16[4,256,128]{2,1,0:T(8,128)(2,1)S(1)} %all-to-all-done), channel_id=1, source_target_pairs={{1,0},{2,1},{3,2},{4,3},{5,4},{6,5},{7,6},{8,7},{9,8},{10,9},{11,1... | collective-permute-start | bytes 786440 | tf_op jit(solution)/shard_map/ppermute | solution.py:60
  47.7 3.8 %collective-permute-start.4 = (bf16[4,256,128]{2,1,0:T(8,128)(2,1)S(1)}, bf16[4,256,128]{2,1,0:T(8,128)(2,1)S(1)}, u32[]{:S(2)}, u32[]{:S(2)}) collective-permute-start(bf16[4,256,128]{2,1,0:T(8,128)(2,1)S(1)} %all-to-all-done), channel_id=1, source_target_pairs={{2,0},{15,1},{4,2},{1,3},{6,4},{3,5},{8,6},{5,7},{10,8},{7,9},{12,... | collective-permute-start | bytes 786440 | tf_op jit(solution)/shard_map/ppermute | solution.py:63
  51.6 1.9 %collective-permute-start.5 = (bf16[4,256,128]{2,1,0:T(8,128)(2,1)S(1)}, bf16[4,256,128]{2,1,0:T(8,128)(2,1)S(1)}, u32[]{:S(2)}, u32[]{:S(2)}) collective-permute-start(bf16[4,256,128]{2,1,0:T(8,128)(2,1)S(1)} %all-to-all-done), channel_id=1, source_target_pairs={{15,0},{0,1},{1,2},{2,3},{3,4},{4,5},{5,6},{6,7},{7,8},{8,9},{9,10... | collective-permute-start | bytes 786440 | tf_op jit(solution)/shard_map/ppermute | solution.py:60
  53.6 3.0 %collective-permute-start.7 = (bf16[2,2,128,1024]{3,2,1,0:T(8,128)(2,1)S(1)}, bf16[2,2,128,1024]{3,2,1,0:T(8,128)(2,1)}, u32[]{:S(2)}, u32[]{:S(2)}) collective-permute-start(bf16[2,2,128,1024]{3,2,1,0:T(8,128)(2,1)S(1)} %maximum_select_fusion), channel_id=1, source_target_pairs={{128,0},{129,1},{130,2},{131,3},{132,4},{133,5},{134,6},{135,7},{1... | collective-permute-start | bytes 3145736 | tf_op jit(solution)/shard_map/ppermute | solution.py:54
  57.1 7.5 %collective-permute-done.5 = bf16[4,256,128]{2,1,0:T(8,128)(2,1)S(1)} collective-permute-done((bf16[4,256,128]{2,1,0:T(8,128)(2,1)S(1)}, bf16[4,256,128]{2,1,0:T(8,128)(2,1)S(1)}, u32[]{:S(2)}, u32[]{:S(2)}) %collective-permute-start.5) | collective-permute-done | bytes 262176 | tf_op jit(solution)/shard_map/ppermute | solution.py:60
  65.0 1.8 %broadcast_in_dim.26 = bf16[4,8,256,128]{3,2,1,0:T(8,128)(2,1)} broadcast(bf16[8,256,128]{2,1,0:T(8,128)(2,1)S(1)} %bitcast.65), dimensions={1,2,3} | broadcast | bytes 2621440 | tf_op jit(solution)/shard_map/broadcast_in_dim | solution.py:29
  66.8 4.4 %all-to-all-start.1 = ((bf16[4,8,256,128]{3,2,1,0:T(8,128)(2,1)}), bf16[4,8,256,128]{3,2,1,0:T(8,128)(2,1)}, u32[]{:S(2)}, u32[]{:S(2)}) async-start(bf16[4,8,256,128]{3,2,1,0:T(8,128)(2,1)} %broadcast_in_dim.26), calls=%async_computation.1 | async-start | bytes 4194304 | tf_op jit(solution)/shard_map/all_to_all | solution.py:72
  71.2 0.9 copy.11
  72.1 1.3 fusion.20
  73.4 1.3 fusion.19
  74.7 1.3 fusion.18
  76.0 1.7 %pad_maximum_fusion = (bf16[1024,1024]{1,0:T(8,128)(2,1)S(1)}, bf16[1024,1024]{1,0:T(8,128)(2,1)}) fusion(bf16[256,1024]{1,0:T(8,128)(2,1)S(1)} %bitcast.70, bf16[256,1024]{1,0:T(8,128)(2,1)S(1)} %bitcast.72, bf16[256,1024]{1,0:T(8,128)(2,1)S(1)} %bitcast.74, bf16[256,1024]{1,0:T(8,128)(2,1)S(1)} %bitcast.67, bf16[256,1024]{1,0:T(8,128)(2,1)S(1)} %bitcast.69, ...), kind=kLoop, calls=%fused_computation | loop fusion | flops 16777216 | bytes 8388608 | tf_op jit(solution)/shard_map/concatenate | solution.py:74
  79.1 2.3 %fusion.6 = bf16[1024,128]{1,0:T(8,128)(2,1)S(1)} fusion(bf16[1024,1024]{1,0:T(8,128)(2,1)} %get-tuple-element.13, bf16[1024,128]{1,0:T(8,128)(2,1)S(1)} %convolution_convert_fusion.4, pred[]{:T(512)S(6)} %lt.39, s32[]{:T(128)S(6)} %min.4), kind=kOutput, calls=%fused_computation.22 | convolution fusion | flops 269090816 | bytes 2883589 | tf_op jit(solution)/shard_map/dot_general | solution.py:12
  81.5 1.7 %broadcast_in_dim.28 = bf16[4,256,1024]{2,1,0:T(8,128)(2,1)} broadcast(bf16[256,1024]{1,0:T(8,128)(2,1)S(1)} %copy.13), dimensions={1,2} | broadcast | bytes 2621440 | tf_op jit(solution)/shard_map/broadcast_in_dim | solution.py:29
  83.8 10.4 %all-to-all-done.1 = bf16[4,8,256,128]{3,2,1,0:T(8,128)(2,1)} async-done(((bf16[4,8,256,128]{3,2,1,0:T(8,128)(2,1)}), bf16[4,8,256,128]{3,2,1,0:T(8,128)(2,1)}, u32[]{:S(2)}, u32[]{:S(2)}) %all-to-all-start.1) | async-done | bytes 2097184 | tf_op jit(solution)/shard_map/all_to_all | solution.py:72
  94.2 5.6 %all-to-all-start.2 = ((bf16[4,256,1024]{2,1,0:T(8,128)(2,1)}), bf16[4,256,1024]{2,1,0:T(8,128)(2,1)}, u32[]{:S(2)}, u32[]{:S(2)}) async-start(bf16[4,256,1024]{2,1,0:T(8,128)(2,1)} %broadcast_in_dim.28), calls=%async_computation.2 | async-start | bytes 4194304 | tf_op jit(solution)/shard_map/all_to_all | solution.py:86
  99.8 1.8 %copy.10 = bf16[4,256,128,8]{2,1,0,3:T(8,128)(2,1)S(1)} copy(bf16[4,256,128,8]{2,1,3,0:T(8,128)(2,1)} %bitcast.3) | data formatting | bytes 4194304 | tf_op jit(solution)/shard_map/xzrk,zkn->xrn/dot_general | solution.py:92
  104.8 4.5 %all-gather = bf16[2048,128]{1,0:T(8,128)(2,1)S(1)} all-gather(bf16[1024,128]{1,0:T(8,128)(2,1)S(1)} %fusion.9), channel_id=2, replica_groups=mesh['y'=4,'core'=2,'x'=4,'z'=16] {'core'}, dimensions={0}, use_global_device_ids=true | all-gather | bytes 786432 | tf_op jit(solution)/shard_map/all_gather | solution.py:33
  112.9 1.3 collective-permute-start.13
  114.3 15.1 %collective-permute-done.13 = bf16[1024,128]{1,0:T(8,128)(2,1)S(1)} collective-permute-done((bf16[1024,128]{1,0:T(8,128)(2,1)S(1)}, bf16[1024,128]{1,0:T(8,128)(2,1)S(1)}, u32[]{:S(2)}, u32[]{:S(2)}) %collective-permute-start.13) | collective-permute-done | bytes 262176 | tf_op jit(solution)/shard_map/ppermute | solution.py:22
  129.4 3.0 %all-gather.1 = bf16[2048,128]{1,0:T(8,128)(2,1)S(1)} all-gather(bf16[1024,128]{1,0:T(8,128)(2,1)S(1)} %select_select_fusion), channel_id=3, replica_groups=mesh['y'=4,'core'=2,'x'=4,'z'=16] {'core'}, dimensions={0}, use_global_device_ids=true | all-gather | bytes 786432 | tf_op jit(solution)/shard_map/all_gather | solution.py:33
  133.4 3.1 %fusion.8 = bf16[1024,128]{1,0:T(8,128)(2,1)} fusion(f32[1024,128]{1,0:T(8,128)S(1)} %convolution_bitcast_fusion, bf16[1024,1024]{1,0:T(8,128)(2,1)} %bitcast.28, bf16[1024,128]{1,0:T(8,128)(2,1)} %copy-done.8, bf16[1024,128]{1,0:T(8,128)(2,1)} %copy-done.9, bf16[1024,128]{1,0:T(8,128)(2,1)S(1)} %copy-done.6, bf16[1024,128]{1,0:T(8,128)(2,1)} %copy-done.7, ...), kind=kOutput, calls=%fused_computation.24 | convolution fusion | flops 269746176 | bytes 4456454 | tf_op jit(solution)/shard_map/dot_general | solution.py:12
  (64 shorter events, 13.9 us)
Async XLA Ops:
  0.9 2.7 %collective-permute-start = (bf16[256,128]{1,0:T(8,128)(2,1)S(1)}, bf16[256,128]{1,0:T(8,128)(2,1)S(1)}, u32[]{:S(2)}, u32[]{:S(2)}) collective-permute-start(bf16[256,128]{1,0:T(8,128)(2,1)S(1)} %get-tuple-element.35), channel_id=1, source_target_pairs={{0,48},{1,49},{2,50},{3,51},{4,52},{5,53},{6,54},{7,55},{8,56},{9,... | collective-permute-start | bytes 196616 | tf_op jit(solution)/shard_map/ppermute | solution.py:22
  1.6 2.0 %collective-permute-start.1 = (bf16[256,128]{1,0:T(8,128)(2,1)S(1)}, bf16[256,128]{1,0:T(8,128)(2,1)S(1)}, u32[]{:S(2)}, u32[]{:S(2)}) collective-permute-start(bf16[256,128]{1,0:T(8,128)(2,1)S(1)} %get-tuple-element.34), channel_id=1, source_target_pairs={{0,32},{1,33},{2,34},{3,35},{4,36},{5,37},{6,38},{7,39},{8,40},{9,... | collective-permute-start | bytes 196616 | tf_op jit(solution)/shard_map/ppermute | solution.py:22
  2.3 8.4 %collective-permute-start.2 = (bf16[256,128]{1,0:T(8,128)(2,1)S(1)}, bf16[256,128]{1,0:T(8,128)(2,1)S(1)}, u32[]{:S(2)}, u32[]{:S(2)}) collective-permute-start(bf16[256,128]{1,0:T(8,128)(2,1)S(1)} %get-tuple-element.33), channel_id=1, source_target_pairs={{0,16},{1,17},{2,18},{3,19},{4,20},{5,21},{6,22},{7,23},{8,24},{9,... | collective-permute-start | bytes 196616 | tf_op jit(solution)/shard_map/ppermute | solution.py:22
  12.3 33.5 %all-to-all-start = ((bf16[4,256,128]{2,1,0:T(8,128)(2,1)}), bf16[4,256,128]{2,1,0:T(8,128)(2,1)S(1)}, u32[]{:S(2)}, u32[]{:S(2)}) async-start(bf16[4,256,128]{2,1,0:T(8,128)(2,1)} %broadcast_in_dim.24), calls=%async_computation | async-start | bytes 524288 | tf_op jit(solution)/shard_map/all_to_all | solution.py:57
  27.5 4.7 %collective-permute-start.6 = (bf16[2,128,1024]{2,1,0:T(8,128)(2,1)S(1)}, bf16[2,128,1024]{2,1,0:T(8,128)(2,1)S(1)}, u32[]{:S(2)}, u32[]{:S(2)}) collective-permute-start(bf16[2,128,1024]{2,1,0:T(8,128)(2,1)S(1)} %get-tuple-element.30), channel_id=1, source_target_pairs={{0,64},{64,0},{1,65},{65,1},{2,66},{66,2},{3,67},{67,3},{4,68},{68... | collective-permute-start | bytes 1572872 | tf_op jit(solution)/shard_map/ppermute | solution.py:51
  32.4 39.8 %collective-permute-start.9 = (bf16[2,2,128,1024]{3,2,1,0:T(8,128)(2,1)S(1)}, bf16[2,2,128,1024]{3,2,1,0:T(8,128)(2,1)}, u32[]{:S(2)}, u32[]{:S(2)}) collective-permute-start(bf16[2,2,128,1024]{3,2,1,0:T(8,128)(2,1)S(1)} %maximum_select_fusion), channel_id=1, source_target_pairs={{384,0},{385,1},{386,2},{387,3},{388,4},{389,5},{390,6},{391,7},{3... | collective-permute-start | bytes 3145736 | tf_op jit(solution)/shard_map/ppermute | solution.py:54
  34.1 39.3 %collective-permute-start.8 = (bf16[2,2,128,1024]{3,2,1,0:T(8,128)(2,1)S(1)}, bf16[2,2,128,1024]{3,2,1,0:T(8,128)(2,1)}, u32[]{:S(2)}, u32[]{:S(2)}) collective-permute-start(bf16[2,2,128,1024]{3,2,1,0:T(8,128)(2,1)S(1)} %maximum_select_fusion), channel_id=1, source_target_pairs={{256,0},{257,1},{258,2},{259,3},{260,4},{261,5},{262,6},{263,7},{2... | collective-permute-start | bytes 3145736 | tf_op jit(solution)/shard_map/ppermute | solution.py:54
  45.8 7.8 %collective-permute-start.3 = (bf16[4,256,128]{2,1,0:T(8,128)(2,1)S(1)}, bf16[4,256,128]{2,1,0:T(8,128)(2,1)S(1)}, u32[]{:S(2)}, u32[]{:S(2)}) collective-permute-start(bf16[4,256,128]{2,1,0:T(8,128)(2,1)S(1)} %all-to-all-done), channel_id=1, source_target_pairs={{1,0},{2,1},{3,2},{4,3},{5,4},{6,5},{7,6},{8,7},{9,8},{10,9},{11,1... | collective-permute-start | bytes 786440 | tf_op jit(solution)/shard_map/ppermute | solution.py:60
  47.7 9.3 %collective-permute-start.4 = (bf16[4,256,128]{2,1,0:T(8,128)(2,1)S(1)}, bf16[4,256,128]{2,1,0:T(8,128)(2,1)S(1)}, u32[]{:S(2)}, u32[]{:S(2)}) collective-permute-start(bf16[4,256,128]{2,1,0:T(8,128)(2,1)S(1)} %all-to-all-done), channel_id=1, source_target_pairs={{2,0},{15,1},{4,2},{1,3},{6,4},{3,5},{8,6},{5,7},{10,8},{7,9},{12,... | collective-permute-start | bytes 786440 | tf_op jit(solution)/shard_map/ppermute | solution.py:63
  51.6 13.0 %collective-permute-start.5 = (bf16[4,256,128]{2,1,0:T(8,128)(2,1)S(1)}, bf16[4,256,128]{2,1,0:T(8,128)(2,1)S(1)}, u32[]{:S(2)}, u32[]{:S(2)}) collective-permute-start(bf16[4,256,128]{2,1,0:T(8,128)(2,1)S(1)} %all-to-all-done), channel_id=1, source_target_pairs={{15,0},{0,1},{1,2},{2,3},{3,4},{4,5},{5,6},{6,7},{7,8},{8,9},{9,10... | collective-permute-start | bytes 786440 | tf_op jit(solution)/shard_map/ppermute | solution.py:60
  53.6 21.1 %collective-permute-start.7 = (bf16[2,2,128,1024]{3,2,1,0:T(8,128)(2,1)S(1)}, bf16[2,2,128,1024]{3,2,1,0:T(8,128)(2,1)}, u32[]{:S(2)}, u32[]{:S(2)}) collective-permute-start(bf16[2,2,128,1024]{3,2,1,0:T(8,128)(2,1)S(1)} %maximum_select_fusion), channel_id=1, source_target_pairs={{128,0},{129,1},{130,2},{131,3},{132,4},{133,5},{134,6},{135,7},{1... | collective-permute-start | bytes 3145736 | tf_op jit(solution)/shard_map/ppermute | solution.py:54
  66.8 27.4 %all-to-all-start.1 = ((bf16[4,8,256,128]{3,2,1,0:T(8,128)(2,1)}), bf16[4,8,256,128]{3,2,1,0:T(8,128)(2,1)}, u32[]{:S(2)}, u32[]{:S(2)}) async-start(bf16[4,8,256,128]{3,2,1,0:T(8,128)(2,1)} %broadcast_in_dim.26), calls=%async_computation.1 | async-start | bytes 4194304 | tf_op jit(solution)/shard_map/all_to_all | solution.py:72
  76.0 1.7 %copy-start.4 = (bf16[1024,128]{1,0:T(8,128)(2,1)S(1)}, bf16[1024,128]{1,0:T(8,128)(2,1)}, u32[]{:S(2)}) copy-start(bf16[1024,128]{1,0:T(8,128)(2,1)} %param.3) | copy-start | bytes 786436
  77.7 1.0 copy-start.2
  78.4 3.1 %copy-start.7 = (bf16[1024,128]{1,0:T(8,128)(2,1)}, bf16[1024,128]{1,0:T(8,128)(2,1)S(1)}, u32[]{:S(2)}) copy-start(bf16[1024,128]{1,0:T(8,128)(2,1)S(1)} %convolution_convert_fusion.4) | copy-start | bytes 786436
  83.1 18.5 %collective-permute-start.10 = (bf16[1024,128]{1,0:T(8,128)(2,1)S(1)}, bf16[1024,128]{1,0:T(8,128)(2,1)S(1)}, u32[]{:S(2)}, u32[]{:S(2)}) collective-permute-start(bf16[1024,128]{1,0:T(8,128)(2,1)S(1)} %fusion.6), channel_id=1, source_target_pairs={{0,64},{1,65},{2,66},{3,67},{4,68},{5,69},{6,70},{7,71},{8,72},{9,... | collective-permute-start | bytes 786440 | tf_op jit(solution)/shard_map/ppermute | solution.py:88
  94.2 39.0 %all-to-all-start.2 = ((bf16[4,256,1024]{2,1,0:T(8,128)(2,1)}), bf16[4,256,1024]{2,1,0:T(8,128)(2,1)}, u32[]{:S(2)}, u32[]{:S(2)}) async-start(bf16[4,256,1024]{2,1,0:T(8,128)(2,1)} %broadcast_in_dim.28), calls=%async_computation.2 | async-start | bytes 4194304 | tf_op jit(solution)/shard_map/all_to_all | solution.py:86
  99.8 1.8 %copy-start.5 = (bf16[1024,128]{1,0:T(8,128)(2,1)S(1)}, bf16[1024,128]{1,0:T(8,128)(2,1)}, u32[]{:S(2)}) copy-start(bf16[1024,128]{1,0:T(8,128)(2,1)} %param.3) | copy-start | bytes 786436
  101.6 7.7 %copy-start = (bf16[4,256,128,8]{2,1,0,3:T(8,128)(2,1)}, bf16[4,256,128,8]{2,1,0,3:T(8,128)(2,1)S(1)}, u32[]{:S(2)}) copy-start(bf16[4,256,128,8]{2,1,0,3:T(8,128)(2,1)S(1)} %copy.10) | copy-start | bytes 6291460
  101.6 2.4 %copy-start.3 = (bf16[1024,1024]{1,0:T(8,128)(2,1)S(1)}, bf16[1024,1024]{1,0:T(8,128)(2,1)}, u32[]{:S(2)}) copy-start(bf16[1024,1024]{1,0:T(8,128)(2,1)} %get-tuple-element.13) | copy-start | bytes 6291460
  102.3 0.7 copy-start.8
  103.1 0.7 copy-start.9
  111.4 21.1 %copy-start.1 = (bf16[4,256,128,8]{2,1,0,3:T(8,128)(2,1)S(1)}, bf16[4,256,128,8]{2,1,0,3:T(8,128)(2,1)}, u32[]{:S(2)}) copy-start(bf16[4,256,128,8]{2,1,0,3:T(8,128)(2,1)} %copy-done) | copy-start | bytes 6291460
  111.4 2.8 %collective-permute-start.11 = (bf16[1024,128]{1,0:T(8,128)(2,1)S(1)}, bf16[1024,128]{1,0:T(8,128)(2,1)S(1)}, u32[]{:S(2)}, u32[]{:S(2)}) collective-permute-start(bf16[1024,128]{1,0:T(8,128)(2,1)S(1)} %fusion.10), channel_id=1, source_target_pairs={{0,384},{1,385},{2,386},{3,387},{4,388},{5,389},{6,390},{7,391},{8... | collective-permute-start | bytes 786440 | tf_op jit(solution)/shard_map/ppermute | solution.py:22
  112.3 2.0 %collective-permute-start.12 = (bf16[1024,128]{1,0:T(8,128)(2,1)S(1)}, bf16[1024,128]{1,0:T(8,128)(2,1)S(1)}, u32[]{:S(2)}, u32[]{:S(2)}) collective-permute-start(bf16[1024,128]{1,0:T(8,128)(2,1)S(1)} %fusion.10), channel_id=1, source_target_pairs={{0,256},{1,257},{2,258},{3,259},{4,260},{5,261},{6,262},{7,263},{8... | collective-permute-start | bytes 786440 | tf_op jit(solution)/shard_map/ppermute | solution.py:22
  112.9 16.4 %collective-permute-start.13 = (bf16[1024,128]{1,0:T(8,128)(2,1)S(1)}, bf16[1024,128]{1,0:T(8,128)(2,1)S(1)}, u32[]{:S(2)}, u32[]{:S(2)}) collective-permute-start(bf16[1024,128]{1,0:T(8,128)(2,1)S(1)} %fusion.10), channel_id=1, source_target_pairs={{0,128},{1,129},{2,130},{3,131},{4,132},{5,133},{6,134},{7,135},{8... | collective-permute-start | bytes 786440 | tf_op jit(solution)/shard_map/ppermute | solution.py:22
  132.5 1.0 copy-start.6

commit v5 on v4

--- a/solution.py
+++ b/solution.py
@@ -81,11 +81,8 @@
     start = jnp.clip(j * 128 - core * NB, 0, NB - 128)
     u_cols = lax.dynamic_slice_in_dim(inv_u, start, 128, 1)
     c0 = jnp.where(in0, -u_cols, times(inv_u, r))
-    sent_late = after(half(core), r).transpose(1, 0, 2).reshape(256, NB)
-    sent_late = copies(sent_late, 4)
-    two = lax.all_to_all(sent_late, "x", 0, 0).reshape(NB, NB)
-    c0 = after(c0, sent_late)
-    c0x = lax.ppermute(c0, ("y", "core"), [(0, 1)])
+    base = lax.optimization_barrier(jnp.where(in1, zeros, c0))
+    c0x = cores(c0)[0]
 
     def product(left, right):
         right = right.reshape(8, 128, 128)
@@ -97,8 +94,18 @@
     c1 = cores(c1)[1]
     t = lax.optimization_barrier(product(one, c1).astype(BF))
     s = lax.optimization_barrier(times(inv_l, t))
-    d = (jnp.where(in1, zeros, c0).astype(F32) - dot(inv_u, s)).astype(BF)
+    d = (base.astype(F32) - dot(inv_u, s)).astype(BF)
     right = jnp.where(core == 0, d, c1)
+    late = after(half(core), r).transpose(1, 0, 2).reshape(256, NB)
+
+    def from_x(value, distance):
+        planes = [(4 * p + (k + distance) % 4, 4 * p + k) for p in range(1, 4) for k in range(4)]
+        return lax.ppermute(value, ("y", "x"), planes)
+
+    ahead, behind = from_x(late, 1), from_x(late, -1)
+    across = jnp.concatenate([from_x(after(ahead[:128], right), 1), from_x(after(behind[128:], right), -1)])
+    two = jnp.concatenate([late, ahead, across, behind, late, ahead, across])
+    two = lax.dynamic_slice_in_dim(two, (4 - x) % 4 * 256, NB, 0)
     right = from_first([right] * 4, "y")
     d, c1 = lax.optimization_barrier(tuple(cores(right)))
     changed = product(one, jnp.where(core == 1, d, c1))

time: 138 us -> 134 us (0.971)
  the two profiles are of different devices: /device:TPU:43 before, /device:TPU:9 now
where the time goes in v5:
time: 134 us; the launch traced here: 133 us
  starting transfers between devices  64.9 us (48%)
  waiting for transfers between devices  22.9 us (17%)
  local copies, waits for them, and re-layouts  15.3 us (11%)
  blocking collectives  15.3 us (11%)
  matrix products  10.3 us (8%)
  other arithmetic  4.03 us (3%)
    all_gather x3, blocking collectives, cores(): return lax.all_gather(value, 'core', axis=0)  15.3 us
    all_to_all x1, starting transfers between devices, shards(): own = lax.all_to_all(copies(share, 4), 'z', 0, 0, axis_index_groups=fours)  14.8 us
    ppermute x4, starting transfers between devices, from_x(): return lax.ppermute(value, ('y', 'x'), planes)  11.6 us
    ppermute x6, waiting for transfers between devices, from_first(): lax.ppermute(v, axis, [(0, k)])  9.73 us
    ppermute x6, starting transfers between devices, from_first(): lax.ppermute(v, axis, [(0, k)])  9.62 us
    dot_general x7, matrix products, dot(): return jnp.dot(a, b, preferred_element_type=F32)  8.1 us
    ppermute x2, starting transfers between devices, from_z(): lax.ppermute(value, 'z', [((k + distance) % 16, k) for k in range(16)])  7.88 us
    ppermute x1, starting transfers between devices, shards(): lax.ppermute(own, 'z', [((k + 2 - 4 * (k % 2)) % 16, k) for k in range(16)])  6.88 us
  transfers between devices with their start and end apart: 19, of which 7 were waited for; matrix products, arithmetic and copies ran while one was open for 17% of the time, Pallas kernels for 0%

profile of v5, /device:TPU:9, one launch (start us, length us, event | category | flops | bytes accessed | tf_op | source)
XLA Modules:
  0.0 133.3 jit_solution(7958549884013593635)
XLA Ops:
  0.9 4.4 %collective-permute-start = (bf16[256,128]{1,0:T(8,128)(2,1)S(1)}, bf16[256,128]{1,0:T(8,128)(2,1)S(1)}, u32[]{:S(2)}, u32[]{:S(2)}) collective-permute-start(bf16[256,128]{1,0:T(8,128)(2,1)S(1)} %get-tuple-element.37), channel_id=1, source_target_pairs={{0,48},{1,49},{2,50},{3,51},{4,52},{5,53},{6,54},{7,55},{8,56},{9,... | collective-permute-start | bytes 196616 | tf_op jit(solution)/shard_map/ppermute | solution.py:22
  5.3 1.3 collective-permute-start.1
  6.6 1.3 collective-permute-start.2
  7.9 1.7 %collective-permute-done.2 = bf16[256,128]{1,0:T(8,128)(2,1)S(1)} collective-permute-done((bf16[256,128]{1,0:T(8,128)(2,1)S(1)}, bf16[256,128]{1,0:T(8,128)(2,1)S(1)}, u32[]{:S(2)}, u32[]{:S(2)}) %collective-permute-start.2) | collective-permute-done | bytes 65568 | tf_op jit(solution)/shard_map/ppermute | solution.py:22
  11.2 14.8 %all-to-all-start = ((bf16[4,256,128]{2,1,0:T(8,128)(2,1)}), bf16[4,256,128]{2,1,0:T(8,128)(2,1)S(1)}, u32[]{:S(2)}, u32[]{:S(2)}) async-start(bf16[4,256,128]{2,1,0:T(8,128)(2,1)} %broadcast_in_dim.17), calls=%async_computation | async-start | bytes 524288 | tf_op jit(solution)/shard_map/all_to_all | solution.py:57
  27.3 3.3 %collective-permute-start.6 = (bf16[2,128,1024]{2,1,0:T(8,128)(2,1)S(1)}, bf16[2,128,1024]{2,1,0:T(8,128)(2,1)S(1)}, u32[]{:S(2)}, u32[]{:S(2)}) collective-permute-start(bf16[2,128,1024]{2,1,0:T(8,128)(2,1)S(1)} %get-tuple-element.32), channel_id=1, source_target_pairs={{0,64},{64,0},{1,65},{65,1},{2,66},{66,2},{3,67},{67,3},{4,68},{68... | collective-permute-start | bytes 1572872 | tf_op jit(solution)/shard_map/ppermute | solution.py:51
  30.7 1.5 %collective-permute-done.6 = bf16[2,128,1024]{2,1,0:T(8,128)(2,1)S(1)} collective-permute-done((bf16[2,128,1024]{2,1,0:T(8,128)(2,1)S(1)}, bf16[2,128,1024]{2,1,0:T(8,128)(2,1)S(1)}, u32[]{:S(2)}, u32[]{:S(2)}) %collective-permute-start.6) | collective-permute-done | bytes 524320 | tf_op jit(solution)/shard_map/ppermute | solution.py:51
  32.3 1.7 %collective-permute-start.9 = (bf16[2,2,128,1024]{3,2,1,0:T(8,128)(2,1)S(1)}, bf16[2,2,128,1024]{3,2,1,0:T(8,128)(2,1)}, u32[]{:S(2)}, u32[]{:S(2)}) collective-permute-start(bf16[2,2,128,1024]{3,2,1,0:T(8,128)(2,1)S(1)} %maximum_select_fusion), channel_id=1, source_target_pairs={{384,0},{385,1},{386,2},{387,3},{388,4},{389,5},{390,6},{391,7},{3... | collective-permute-start | bytes 3145736 | tf_op jit(solution)/shard_map/ppermute | solution.py:54
  34.0 1.6 %collective-permute-start.8 = (bf16[2,2,128,1024]{3,2,1,0:T(8,128)(2,1)S(1)}, bf16[2,2,128,1024]{3,2,1,0:T(8,128)(2,1)}, u32[]{:S(2)}, u32[]{:S(2)}) collective-permute-start(bf16[2,2,128,1024]{3,2,1,0:T(8,128)(2,1)S(1)} %maximum_select_fusion), channel_id=1, source_target_pairs={{256,0},{257,1},{258,2},{259,3},{260,4},{261,5},{262,6},{263,7},{2... | collective-permute-start | bytes 3145736 | tf_op jit(solution)/shard_map/ppermute | solution.py:54
  35.6 3.6 %all-to-all-done = bf16[4,256,128]{2,1,0:T(8,128)(2,1)S(1)} async-done(((bf16[4,256,128]{2,1,0:T(8,128)(2,1)}), bf16[4,256,128]{2,1,0:T(8,128)(2,1)S(1)}, u32[]{:S(2)}, u32[]{:S(2)}) %all-to-all-start) | async-done | bytes 262176 | tf_op jit(solution)/shard_map/all_to_all | solution.py:57
  39.2 4.9 %collective-permute-start.3 = (bf16[4,256,128]{2,1,0:T(8,128)(2,1)S(1)}, bf16[4,256,128]{2,1,0:T(8,128)(2,1)S(1)}, u32[]{:S(2)}, u32[]{:S(2)}) collective-permute-start(bf16[4,256,128]{2,1,0:T(8,128)(2,1)S(1)} %all-to-all-done), channel_id=1, source_target_pairs={{1,0},{2,1},{3,2},{4,3},{5,4},{6,5},{7,6},{8,7},{9,8},{10,9},{11,1... | collective-permute-start | bytes 786440 | tf_op jit(solution)/shard_map/ppermute | solution.py:60
  44.1 6.9 %collective-permute-start.4 = (bf16[4,256,128]{2,1,0:T(8,128)(2,1)S(1)}, bf16[4,256,128]{2,1,0:T(8,128)(2,1)S(1)}, u32[]{:S(2)}, u32[]{:S(2)}) collective-permute-start(bf16[4,256,128]{2,1,0:T(8,128)(2,1)S(1)} %all-to-all-done), channel_id=1, source_target_pairs={{2,0},{15,1},{4,2},{1,3},{6,4},{3,5},{8,6},{5,7},{10,8},{7,9},{12,... | collective-permute-start | bytes 786440 | tf_op jit(solution)/shard_map/ppermute | solution.py:63
  51.1 3.0 %collective-permute-start.5 = (bf16[4,256,128]{2,1,0:T(8,128)(2,1)S(1)}, bf16[4,256,128]{2,1,0:T(8,128)(2,1)S(1)}, u32[]{:S(2)}, u32[]{:S(2)}) collective-permute-start(bf16[4,256,128]{2,1,0:T(8,128)(2,1)S(1)} %all-to-all-done), channel_id=1, source_target_pairs={{15,0},{0,1},{1,2},{2,3},{3,4},{4,5},{5,6},{6,7},{7,8},{8,9},{9,10... | collective-permute-start | bytes 786440 | tf_op jit(solution)/shard_map/ppermute | solution.py:60
  54.1 3.1 %collective-permute-start.7 = (bf16[2,2,128,1024]{3,2,1,0:T(8,128)(2,1)S(1)}, bf16[2,2,128,1024]{3,2,1,0:T(8,128)(2,1)}, u32[]{:S(2)}, u32[]{:S(2)}) collective-permute-start(bf16[2,2,128,1024]{3,2,1,0:T(8,128)(2,1)S(1)} %maximum_select_fusion), channel_id=1, source_target_pairs={{128,0},{129,1},{130,2},{131,3},{132,4},{133,5},{134,6},{135,7},{1... | collective-permute-start | bytes 3145736 | tf_op jit(solution)/shard_map/ppermute | solution.py:54
  57.2 1.6 %collective-permute-done.4 = bf16[4,256,128]{2,1,0:T(8,128)(2,1)S(1)} collective-permute-done((bf16[4,256,128]{2,1,0:T(8,128)(2,1)S(1)}, bf16[4,256,128]{2,1,0:T(8,128)(2,1)S(1)}, u32[]{:S(2)}, u32[]{:S(2)}) %collective-permute-start.4) | collective-permute-done | bytes 262176 | tf_op jit(solution)/shard_map/ppermute | solution.py:63
  58.8 4.1 %collective-permute-done.5 = bf16[4,256,128]{2,1,0:T(8,128)(2,1)S(1)} collective-permute-done((bf16[4,256,128]{2,1,0:T(8,128)(2,1)S(1)}, bf16[4,256,128]{2,1,0:T(8,128)(2,1)S(1)}, u32[]{:S(2)}, u32[]{:S(2)}) %collective-permute-start.5) | collective-permute-done | bytes 262176 | tf_op jit(solution)/shard_map/ppermute | solution.py:60
  63.3 1.8 %broadcast_in_dim.19 = bf16[4,8,256,128]{3,2,1,0:T(8,128)(2,1)} broadcast(bf16[8,256,128]{2,1,0:T(8,128)(2,1)S(1)} %bitcast.67), dimensions={1,2,3} | broadcast | bytes 2621440 | tf_op jit(solution)/shard_map/broadcast_in_dim | solution.py:29
  65.2 4.4 %all-to-all-start.1 = ((bf16[4,8,256,128]{3,2,1,0:T(8,128)(2,1)}), bf16[4,8,256,128]{3,2,1,0:T(8,128)(2,1)}, u32[]{:S(2)}, u32[]{:S(2)}) async-start(bf16[4,8,256,128]{3,2,1,0:T(8,128)(2,1)} %broadcast_in_dim.19), calls=%async_computation.1 | async-start | bytes 4194304 | tf_op jit(solution)/shard_map/all_to_all | solution.py:72
  73.0 2.4 %collective-permute-done.7 = bf16[2,2,128,1024]{3,2,1,0:T(8,128)(2,1)} collective-permute-done((bf16[2,2,128,1024]{3,2,1,0:T(8,128)(2,1)S(1)}, bf16[2,2,128,1024]{3,2,1,0:T(8,128)(2,1)}, u32[]{:S(2)}, u32[]{:S(2)}) %collective-permute-start.7) | collective-permute-done | bytes 1048608 | tf_op jit(solution)/shard_map/ppermute | solution.py:54
  76.7 1.7 %pad_maximum_fusion = (bf16[1024,1024]{1,0:T(8,128)(2,1)S(1)}, bf16[1024,1024]{1,0:T(8,128)(2,1)}) fusion(bf16[256,1024]{1,0:T(8,128)(2,1)S(1)} %bitcast.72, bf16[256,1024]{1,0:T(8,128)(2,1)S(1)} %bitcast.74, bf16[256,1024]{1,0:T(8,128)(2,1)S(1)} %bitcast.76, bf16[256,1024]{1,0:T(8,128)(2,1)S(1)} %bitcast.69, bf16[256,1024]{1,0:T(8,128)(2,1)S(1)} %bitcast.71, ...), kind=kLoop, calls=%fused_computation | loop fusion | flops 16777216 | bytes 8388608 | tf_op jit(solution)/shard_map/concatenate | solution.py:74
  79.6 2.2 %collective-permute-start.13 = (bf16[256,1024]{0,1:T(8,128)(2,1)S(1)}, bf16[256,1024]{0,1:T(8,128)(2,1)S(1)}, u32[]{:S(2)}, u32[]{:S(2)}) collective-permute-start(bf16[256,1024]{0,1:T(8,128)(2,1)S(1)} %bitcast.62), channel_id=1, source_target_pairs={{144,128},{160,144},{176,160},{128,176},{272,256},{288,272},{304,2... | collective-permute-start | bytes 1572872 | tf_op jit(solution)/shard_map/ppermute | solution.py:103
  81.8 4.0 %collective-permute-start.15 = (bf16[256,1024]{0,1:T(8,128)(2,1)S(1)}, bf16[256,1024]{0,1:T(8,128)(2,1)}, u32[]{:S(2)}, u32[]{:S(2)}) collective-permute-start(bf16[256,1024]{0,1:T(8,128)(2,1)S(1)} %bitcast.63), channel_id=1, source_target_pairs={{176,128},{128,144},{144,160},{160,176},{304,256},{256,272},{272,2... | collective-permute-start | bytes 1572872 | tf_op jit(solution)/shard_map/ppermute | solution.py:103
  85.8 3.1 %broadcast_select_fusion = (bf16[1024,128]{1,0:T(8,128)(2,1)}, bf16[1024,128]{1,0:T(8,128)(2,1)S(1)}) fusion(pred[]{:T(512)S(6)} %and.22, bf16[1024,1024]{1,0:T(8,128)(2,1)} %get-tuple-element.14, bf16[1024,128]{1,0:T(8,128)(2,1)S(1)} %convolution_convert_fusion.4, s32[]{:T(128)S(6)} %min.4, pred[]{:T(512)S(6)} %lt.46), kind=kOutput, calls=%fused_computation.39 | convolution fusion | flops 269221888 | bytes 3145734 | tf_op jit(solution)/shard_map/dot_general | solution.py:12
  88.9 6.2 %all-gather = bf16[2048,128]{1,0:T(8,128)(2,1)S(1)} all-gather(bf16[1024,128]{1,0:T(8,128)(2,1)S(1)} %get-tuple-element.39), channel_id=2, replica_groups=mesh['y'=4,'core'=2,'x'=4,'z'=16] {'core'}, dimensions={0}, use_global_device_ids=true | all-gather | bytes 786432 | tf_op jit(solution)/shard_map/all_gather | solution.py:33
  95.8 1.8 %copy.8 = bf16[4,256,128,8]{2,1,0,3:T(8,128)(2,1)S(1)} copy(bf16[4,256,128,8]{2,1,3,0:T(8,128)(2,1)} %bitcast.3) | data formatting | bytes 4194304 | tf_op jit(solution)/shard_map/xzrk,zkn->xrn/dot_general | solution.py:89
  100.8 6.1 %all-gather.1 = bf16[2048,128]{1,0:T(8,128)(2,1)S(1)} all-gather(bf16[1024,128]{1,0:T(8,128)(2,1)S(1)} %fusion.17), channel_id=3, replica_groups=mesh['y'=4,'core'=2,'x'=4,'z'=16] {'core'}, dimensions={0}, use_global_device_ids=true | all-gather | bytes 786432 | tf_op jit(solution)/shard_map/all_gather | solution.py:33
  110.4 1.3 collective-permute-start.12
  112.8 3.5 %collective-permute-start.14 = (bf16[128,1024]{0,1:T(8,128)(2,1)S(1)}, bf16[128,1024]{0,1:T(8,128)(2,1)S(1)}, u32[]{:S(2)}, u32[]{:S(2)}) collective-permute-start(bf16[128,1024]{0,1:T(8,128)(2,1)S(1)} %slice.78), channel_id=1, source_target_pairs={{144,128},{160,144},{176,160},{128,176},{272,256},{288,272},{304,2... | collective-permute-start | bytes 786440 | tf_op jit(solution)/shard_map/ppermute | solution.py:103
  116.4 1.9 %collective-permute-start.16 = (bf16[128,1024]{0,1:T(8,128)(2,1)S(1)}, bf16[128,1024]{0,1:T(8,128)(2,1)S(1)}, u32[]{:S(2)}, u32[]{:S(2)}) collective-permute-start(bf16[128,1024]{0,1:T(8,128)(2,1)S(1)} %slice.79), channel_id=1, source_target_pairs={{176,128},{128,144},{144,160},{160,176},{304,256},{256,272},{272,2... | collective-permute-start | bytes 786440 | tf_op jit(solution)/shard_map/ppermute | solution.py:103
  118.3 8.0 %collective-permute-done.12 = bf16[1024,128]{1,0:T(8,128)(2,1)S(1)} collective-permute-done((bf16[1024,128]{1,0:T(8,128)(2,1)S(1)}, bf16[1024,128]{1,0:T(8,128)(2,1)S(1)}, u32[]{:S(2)}, u32[]{:S(2)}) %collective-permute-start.12) | collective-permute-done | bytes 262176 | tf_op jit(solution)/shard_map/ppermute | solution.py:22
  126.4 3.0 %all-gather.2 = bf16[2048,128]{1,0:T(8,128)(2,1)S(1)} all-gather(bf16[1024,128]{1,0:T(8,128)(2,1)S(1)} %select_select_fusion), channel_id=4, replica_groups=mesh['y'=4,'core'=2,'x'=4,'z'=16] {'core'}, dimensions={0}, use_global_device_ids=true | all-gather | bytes 786432 | tf_op jit(solution)/shard_map/all_gather | solution.py:33
  131.9 1.5 %fusion.19 = bf16[1024,128]{1,0:T(8,128)(2,1)} fusion(f32[1024,128]{1,0:T(8,128)S(1)} %convolution_bitcast_fusion, bf16[1792,1024]{0,1:T(8,128)(2,1)S(1)} %constant_dynamic-update-slice_fusion.7, s32[]{:T(128)S(6)} %select_n.185, bf16[1024,128]{1,0:T(8,128)(2,1)S(1)} %copy-done.10, bf16[1024,128]{1,0:T(8,128)(2,1)S(1)} %copy-done.12, ...), kind=kOutput, calls=%fused_computation.28 | convolution fusion | flops 269746176 | bytes 4456458 | tf_op jit(solution)/shard_map/dot_general | solution.py:12
  (89 shorter events, 21.2 us)
Async XLA Ops:
  0.9 7.0 %collective-permute-start = (bf16[256,128]{1,0:T(8,128)(2,1)S(1)}, bf16[256,128]{1,0:T(8,128)(2,1)S(1)}, u32[]{:S(2)}, u32[]{:S(2)}) collective-permute-start(bf16[256,128]{1,0:T(8,128)(2,1)S(1)} %get-tuple-element.37), channel_id=1, source_target_pairs={{0,48},{1,49},{2,50},{3,51},{4,52},{5,53},{6,54},{7,55},{8,56},{9,... | collective-permute-start | bytes 196616 | tf_op jit(solution)/shard_map/ppermute | solution.py:22
  5.3 2.6 %collective-permute-start.1 = (bf16[256,128]{1,0:T(8,128)(2,1)S(1)}, bf16[256,128]{1,0:T(8,128)(2,1)S(1)}, u32[]{:S(2)}, u32[]{:S(2)}) collective-permute-start(bf16[256,128]{1,0:T(8,128)(2,1)S(1)} %get-tuple-element.36), channel_id=1, source_target_pairs={{0,32},{1,33},{2,34},{3,35},{4,36},{5,37},{6,38},{7,39},{8,40},{9,... | collective-permute-start | bytes 196616 | tf_op jit(solution)/shard_map/ppermute | solution.py:22
  6.6 3.0 %collective-permute-start.2 = (bf16[256,128]{1,0:T(8,128)(2,1)S(1)}, bf16[256,128]{1,0:T(8,128)(2,1)S(1)}, u32[]{:S(2)}, u32[]{:S(2)}) collective-permute-start(bf16[256,128]{1,0:T(8,128)(2,1)S(1)} %get-tuple-element.35), channel_id=1, source_target_pairs={{0,16},{1,17},{2,18},{3,19},{4,20},{5,21},{6,22},{7,23},{8,24},{9,... | collective-permute-start | bytes 196616 | tf_op jit(solution)/shard_map/ppermute | solution.py:22
  11.2 28.0 %all-to-all-start = ((bf16[4,256,128]{2,1,0:T(8,128)(2,1)}), bf16[4,256,128]{2,1,0:T(8,128)(2,1)S(1)}, u32[]{:S(2)}, u32[]{:S(2)}) async-start(bf16[4,256,128]{2,1,0:T(8,128)(2,1)} %broadcast_in_dim.17), calls=%async_computation | async-start | bytes 524288 | tf_op jit(solution)/shard_map/all_to_all | solution.py:57
  27.3 4.8 %collective-permute-start.6 = (bf16[2,128,1024]{2,1,0:T(8,128)(2,1)S(1)}, bf16[2,128,1024]{2,1,0:T(8,128)(2,1)S(1)}, u32[]{:S(2)}, u32[]{:S(2)}) collective-permute-start(bf16[2,128,1024]{2,1,0:T(8,128)(2,1)S(1)} %get-tuple-element.32), channel_id=1, source_target_pairs={{0,64},{64,0},{1,65},{65,1},{2,66},{66,2},{3,67},{67,3},{4,68},{68... | collective-permute-start | bytes 1572872 | tf_op jit(solution)/shard_map/ppermute | solution.py:51
  32.3 38.2 %collective-permute-start.9 = (bf16[2,2,128,1024]{3,2,1,0:T(8,128)(2,1)S(1)}, bf16[2,2,128,1024]{3,2,1,0:T(8,128)(2,1)}, u32[]{:S(2)}, u32[]{:S(2)}) collective-permute-start(bf16[2,2,128,1024]{3,2,1,0:T(8,128)(2,1)S(1)} %maximum_select_fusion), channel_id=1, source_target_pairs={{384,0},{385,1},{386,2},{387,3},{388,4},{389,5},{390,6},{391,7},{3... | collective-permute-start | bytes 3145736 | tf_op jit(solution)/shard_map/ppermute | solution.py:54
  34.0 37.8 %collective-permute-start.8 = (bf16[2,2,128,1024]{3,2,1,0:T(8,128)(2,1)S(1)}, bf16[2,2,128,1024]{3,2,1,0:T(8,128)(2,1)}, u32[]{:S(2)}, u32[]{:S(2)}) collective-permute-start(bf16[2,2,128,1024]{3,2,1,0:T(8,128)(2,1)S(1)} %maximum_select_fusion), channel_id=1, source_target_pairs={{256,0},{257,1},{258,2},{259,3},{260,4},{261,5},{262,6},{263,7},{2... | collective-permute-start | bytes 3145736 | tf_op jit(solution)/shard_map/ppermute | solution.py:54
  39.2 14.9 %collective-permute-start.3 = (bf16[4,256,128]{2,1,0:T(8,128)(2,1)S(1)}, bf16[4,256,128]{2,1,0:T(8,128)(2,1)S(1)}, u32[]{:S(2)}, u32[]{:S(2)}) collective-permute-start(bf16[4,256,128]{2,1,0:T(8,128)(2,1)S(1)} %all-to-all-done), channel_id=1, source_target_pairs={{1,0},{2,1},{3,2},{4,3},{5,4},{6,5},{7,6},{8,7},{9,8},{10,9},{11,1... | collective-permute-start | bytes 786440 | tf_op jit(solution)/shard_map/ppermute | solution.py:60
  44.1 14.6 %collective-permute-start.4 = (bf16[4,256,128]{2,1,0:T(8,128)(2,1)S(1)}, bf16[4,256,128]{2,1,0:T(8,128)(2,1)S(1)}, u32[]{:S(2)}, u32[]{:S(2)}) collective-permute-start(bf16[4,256,128]{2,1,0:T(8,128)(2,1)S(1)} %all-to-all-done), channel_id=1, source_target_pairs={{2,0},{15,1},{4,2},{1,3},{6,4},{3,5},{8,6},{5,7},{10,8},{7,9},{12,... | collective-permute-start | bytes 786440 | tf_op jit(solution)/shard_map/ppermute | solution.py:63
  51.1 11.8 %collective-permute-start.5 = (bf16[4,256,128]{2,1,0:T(8,128)(2,1)S(1)}, bf16[4,256,128]{2,1,0:T(8,128)(2,1)S(1)}, u32[]{:S(2)}, u32[]{:S(2)}) collective-permute-start(bf16[4,256,128]{2,1,0:T(8,128)(2,1)S(1)} %all-to-all-done), channel_id=1, source_target_pairs={{15,0},{0,1},{1,2},{2,3},{3,4},{4,5},{5,6},{6,7},{7,8},{8,9},{9,10... | collective-permute-start | bytes 786440 | tf_op jit(solution)/shard_map/ppermute | solution.py:60
  54.1 21.3 %collective-permute-start.7 = (bf16[2,2,128,1024]{3,2,1,0:T(8,128)(2,1)S(1)}, bf16[2,2,128,1024]{3,2,1,0:T(8,128)(2,1)}, u32[]{:S(2)}, u32[]{:S(2)}) collective-permute-start(bf16[2,2,128,1024]{3,2,1,0:T(8,128)(2,1)S(1)} %maximum_select_fusion), channel_id=1, source_target_pairs={{128,0},{129,1},{130,2},{131,3},{132,4},{133,5},{134,6},{135,7},{1... | collective-permute-start | bytes 3145736 | tf_op jit(solution)/shard_map/ppermute | solution.py:54
  65.2 30.6 %all-to-all-start.1 = ((bf16[4,8,256,128]{3,2,1,0:T(8,128)(2,1)}), bf16[4,8,256,128]{3,2,1,0:T(8,128)(2,1)}, u32[]{:S(2)}, u32[]{:S(2)}) async-start(bf16[4,8,256,128]{3,2,1,0:T(8,128)(2,1)} %broadcast_in_dim.19), calls=%async_computation.1 | async-start | bytes 4194304 | tf_op jit(solution)/shard_map/all_to_all | solution.py:72
  76.7 1.7 %copy-start.4 = (bf16[1024,128]{1,0:T(8,128)(2,1)S(1)}, bf16[1024,128]{1,0:T(8,128)(2,1)}, u32[]{:S(2)}) copy-start(bf16[1024,128]{1,0:T(8,128)(2,1)} %param.3) | copy-start | bytes 786436
  79.1 9.8 %copy-start.7 = (bf16[1024,128]{1,0:T(8,128)(2,1)}, bf16[1024,128]{1,0:T(8,128)(2,1)S(1)}, u32[]{:S(2)}) copy-start(bf16[1024,128]{1,0:T(8,128)(2,1)S(1)} %convolution_convert_fusion.4) | copy-start | bytes 786436
  79.6 32.1 %collective-permute-start.13 = (bf16[256,1024]{0,1:T(8,128)(2,1)S(1)}, bf16[256,1024]{0,1:T(8,128)(2,1)S(1)}, u32[]{:S(2)}, u32[]{:S(2)}) collective-permute-start(bf16[256,1024]{0,1:T(8,128)(2,1)S(1)} %bitcast.62), channel_id=1, source_target_pairs={{144,128},{160,144},{176,160},{128,176},{272,256},{288,272},{304,2... | collective-permute-start | bytes 1572872 | tf_op jit(solution)/shard_map/ppermute | solution.py:103
  81.8 30.0 %collective-permute-start.15 = (bf16[256,1024]{0,1:T(8,128)(2,1)S(1)}, bf16[256,1024]{0,1:T(8,128)(2,1)}, u32[]{:S(2)}, u32[]{:S(2)}) collective-permute-start(bf16[256,1024]{0,1:T(8,128)(2,1)S(1)} %bitcast.63), channel_id=1, source_target_pairs={{176,128},{128,144},{144,160},{160,176},{304,256},{256,272},{272,2... | collective-permute-start | bytes 1572872 | tf_op jit(solution)/shard_map/ppermute | solution.py:103
  95.8 1.8 %copy-start.5 = (bf16[1024,128]{1,0:T(8,128)(2,1)S(1)}, bf16[1024,128]{1,0:T(8,128)(2,1)}, u32[]{:S(2)}) copy-start(bf16[1024,128]{1,0:T(8,128)(2,1)} %param.3) | copy-start | bytes 786436
  95.8 1.8 %copy-start.13 = (bf16[1024,128]{1,0:T(8,128)(2,1)S(1)}, bf16[1024,128]{1,0:T(8,128)(2,1)}, u32[]{:S(2)}) copy-start(bf16[1024,128]{1,0:T(8,128)(2,1)} %slice.74) | copy-start | bytes 786436
  97.6 9.3 %copy-start = (bf16[4,256,128,8]{2,1,0,3:T(8,128)(2,1)}, bf16[4,256,128,8]{2,1,0,3:T(8,128)(2,1)S(1)}, u32[]{:S(2)}) copy-start(bf16[4,256,128,8]{2,1,0,3:T(8,128)(2,1)S(1)} %copy.8) | copy-start | bytes 6291460
  97.6 2.4 %copy-start.3 = (bf16[1024,1024]{1,0:T(8,128)(2,1)S(1)}, bf16[1024,1024]{1,0:T(8,128)(2,1)}, u32[]{:S(2)}) copy-start(bf16[1024,1024]{1,0:T(8,128)(2,1)} %get-tuple-element.14) | copy-start | bytes 6291460
  100.0 6.8 %copy-start.11 = (bf16[1024,128]{1,0:T(8,128)(2,1)}, bf16[1024,128]{1,0:T(8,128)(2,1)S(1)}, u32[]{:S(2)}) copy-start(bf16[1024,128]{1,0:T(8,128)(2,1)S(1)} %convolution_convert_fusion.2) | copy-start | bytes 786436
  106.9 1.4 %copy-start.14 = (bf16[1024,128]{1,0:T(8,128)(2,1)S(1)}, bf16[1024,128]{1,0:T(8,128)(2,1)}, u32[]{:S(2)}) copy-start(bf16[1024,128]{1,0:T(8,128)(2,1)} %get-tuple-element.38) | copy-start | bytes 786436
  109.0 9.3 %collective-permute-start.10 = (bf16[1024,128]{1,0:T(8,128)(2,1)S(1)}, bf16[1024,128]{1,0:T(8,128)(2,1)S(1)}, u32[]{:S(2)}, u32[]{:S(2)}) collective-permute-start(bf16[1024,128]{1,0:T(8,128)(2,1)S(1)} %fusion.18), channel_id=1, source_target_pairs={{0,384},{1,385},{2,386},{3,387},{4,388},{5,389},{6,390},{7,391},{8... | collective-permute-start | bytes 786440 | tf_op jit(solution)/shard_map/ppermute | solution.py:22
  109.7 8.6 %collective-permute-start.11 = (bf16[1024,128]{1,0:T(8,128)(2,1)S(1)}, bf16[1024,128]{1,0:T(8,128)(2,1)S(1)}, u32[]{:S(2)}, u32[]{:S(2)}) collective-permute-start(bf16[1024,128]{1,0:T(8,128)(2,1)S(1)} %fusion.18), channel_id=1, source_target_pairs={{0,256},{1,257},{2,258},{3,259},{4,260},{5,261},{6,262},{7,263},{8... | collective-permute-start | bytes 786440 | tf_op jit(solution)/shard_map/ppermute | solution.py:22
  110.4 16.0 %collective-permute-start.12 = (bf16[1024,128]{1,0:T(8,128)(2,1)S(1)}, bf16[1024,128]{1,0:T(8,128)(2,1)S(1)}, u32[]{:S(2)}, u32[]{:S(2)}) collective-permute-start(bf16[1024,128]{1,0:T(8,128)(2,1)S(1)} %fusion.18), channel_id=1, source_target_pairs={{0,128},{1,129},{2,130},{3,131},{4,132},{5,133},{6,134},{7,135},{8... | collective-permute-start | bytes 786440 | tf_op jit(solution)/shard_map/ppermute | solution.py:22
  112.8 16.7 %copy-start.1 = (bf16[4,256,128,8]{2,1,0,3:T(8,128)(2,1)S(1)}, bf16[4,256,128,8]{2,1,0,3:T(8,128)(2,1)}, u32[]{:S(2)}) copy-start(bf16[4,256,128,8]{2,1,0,3:T(8,128)(2,1)} %copy-done) | copy-start | bytes 6291460
  112.8 16.7 %collective-permute-start.14 = (bf16[128,1024]{0,1:T(8,128)(2,1)S(1)}, bf16[128,1024]{0,1:T(8,128)(2,1)S(1)}, u32[]{:S(2)}, u32[]{:S(2)}) collective-permute-start(bf16[128,1024]{0,1:T(8,128)(2,1)S(1)} %slice.78), channel_id=1, source_target_pairs={{144,128},{160,144},{176,160},{128,176},{272,256},{288,272},{304,2... | collective-permute-start | bytes 786440 | tf_op jit(solution)/shard_map/ppermute | solution.py:103
  116.4 13.9 %collective-permute-start.16 = (bf16[128,1024]{0,1:T(8,128)(2,1)S(1)}, bf16[128,1024]{0,1:T(8,128)(2,1)S(1)}, u32[]{:S(2)}, u32[]{:S(2)}) collective-permute-start(bf16[128,1024]{0,1:T(8,128)(2,1)S(1)} %slice.79), channel_id=1, source_target_pairs={{176,128},{128,144},{144,160},{160,176},{304,256},{256,272},{272,2... | collective-permute-start | bytes 786440 | tf_op jit(solution)/shard_map/ppermute | solution.py:103
  130.4 1.4 %copy-start.6 = (bf16[1024,128]{1,0:T(8,128)(2,1)S(1)}, bf16[1024,128]{1,0:T(8,128)(2,1)}, u32[]{:S(2)}) copy-start(bf16[1024,128]{1,0:T(8,128)(2,1)} %param.3) | copy-start | bytes 786436
  130.4 1.4 %copy-start.8 = (bf16[1024,128]{1,0:T(8,128)(2,1)S(1)}, bf16[1024,128]{1,0:T(8,128)(2,1)}, u32[]{:S(2)}) copy-start(bf16[1024,128]{1,0:T(8,128)(2,1)} %copy-done.7) | copy-start | bytes 786436
  130.4 1.4 %copy-start.10 = (bf16[1024,128]{1,0:T(8,128)(2,1)S(1)}, bf16[1024,128]{1,0:T(8,128)(2,1)}, u32[]{:S(2)}) copy-start(bf16[1024,128]{1,0:T(8,128)(2,1)} %copy-done.9) | copy-start | bytes 786436
  130.4 1.4 %copy-start.12 = (bf16[1024,128]{1,0:T(8,128)(2,1)S(1)}, bf16[1024,128]{1,0:T(8,128)(2,1)}, u32[]{:S(2)}) copy-start(bf16[1024,128]{1,0:T(8,128)(2,1)} %copy-done.11) | copy-start | bytes 786436
  (2 other events, 1.8 us)

commit v6 on v5

--- a/solution.py
+++ b/solution.py
@@ -19,9 +19,9 @@
 def from_first(values, axis):
     at = lax.axis_index(axis)
     out = values[0]
-    got = [lax.ppermute(v, axis, [(0, k)]) for k, v in enumerate(values) if k > 0]
-    for k, v in enumerate(got):
-        out = jnp.where(at == k + 1, v, out)
+    got = {k: lax.ppermute(values[k], axis, [(0, k)]) for k in (3, 1, 2)}
+    for k in (3, 1, 2):
+        out = jnp.where(at == k, got[k], out)
     return out
 
 
@@ -80,7 +80,8 @@
     r = times(inv_l, a)
     start = jnp.clip(j * 128 - core * NB, 0, NB - 128)
     u_cols = lax.dynamic_slice_in_dim(inv_u, start, 128, 1)
-    c0 = jnp.where(in0, -u_cols, times(inv_u, r))
+    minus_u = lax.optimization_barrier(-u_cols)
+    c0 = jnp.where(in0, minus_u, times(inv_u, r))
     base = lax.optimization_barrier(jnp.where(in1, zeros, c0))
     c0x = cores(c0)[0]
 
@@ -90,13 +91,13 @@
 
     w = (jnp.where(in0, zeros, a).astype(F32) - product(one, c0x)).astype(BF)
     r1 = times(inv_l, w)
-    c1 = jnp.where(in0, zeros, jnp.where(in1, -u_cols, times(inv_u, r1)))
+    c1 = jnp.where(in0, zeros, jnp.where(in1, minus_u, times(inv_u, r1)))
     c1 = cores(c1)[1]
     t = lax.optimization_barrier(product(one, c1).astype(BF))
     s = lax.optimization_barrier(times(inv_l, t))
     d = (base.astype(F32) - dot(inv_u, s)).astype(BF)
     right = jnp.where(core == 0, d, c1)
-    late = after(half(core), r).transpose(1, 0, 2).reshape(256, NB)
+    late = after(half(core), c0).transpose(1, 0, 2).reshape(256, NB)
 
     def from_x(value, distance):
         planes = [(4 * p + (k + distance) % 4, 4 * p + k) for p in range(1, 4) for k in range(4)]

time: 134 us -> 134 us (level)
  blocking collectives: 15.3 us -> 17.5 us
  matrix products: 10.3 us -> 8.68 us
  waiting for transfers between devices: 22.9 us -> 21.3 us
    all_gather x3, blocking collectives: 15.3 us -> 17.5 us  [cores(): return lax.all_gather(value, 'core', axis=0)]
    dot_general x7, matrix products: 8.1 us -> 6.53 us  [dot(): return jnp.dot(a, b, preferred_element_type=F32)]
    unnamed x44 -> x46, local copies, waits for them, and re-layouts: 3.04 us -> 2.88 us
  transfers between devices with their start and end apart: 19 -> 19, of which waited for: 7 -> 8; matrix products, arithmetic and copies ran while one was open for 17% -> 15% of each run, Pallas kernels for 0% -> 0%
where the time goes in v6:
time: 134 us; the launch traced here: 133 us
  starting transfers between devices  66.1 us (49%)
  waiting for transfers between devices  21.3 us (16%)
  blocking collectives  17.5 us (13%)
  local copies, waits for them, and re-layouts  15.2 us (11%)
  matrix products  8.68 us (6%)
  other arithmetic  3.16 us (2%)
    all_gather x3, blocking collectives, cores(): return lax.all_gather(value, 'core', axis=0)  17.5 us
    all_to_all x1, starting transfers between devices, shards(): own = lax.all_to_all(copies(share, 4), 'z', 0, 0, axis_index_groups=fours)  14.8 us
    ppermute x4, starting transfers between devices, from_x(): return lax.ppermute(value, ('y', 'x'), planes)  12.1 us
    ppermute x6, starting transfers between devices, from_first(): got = {k: lax.ppermute(values[k], axis, [(0, k)]) for k in (3, 1, 2)}  9.88 us
    ppermute x6, waiting for transfers between devices, from_first(): got = {k: lax.ppermute(values[k], axis, [(0, k)]) for k in (3, 1, 2)}  8.68 us
    ppermute x2, starting transfers between devices, from_z(): lax.ppermute(value, 'z', [((k + distance) % 16, k) for k in range(16)])  7.73 us
    ppermute x1, starting transfers between devices, shards(): lax.ppermute(own, 'z', [((k + 2 - 4 * (k % 2)) % 16, k) for k in range(16)])  7 us
    dot_general x7, matrix products, dot(): return jnp.dot(a, b, preferred_element_type=F32)  6.53 us
  transfers between devices with their start and end apart: 19, of which 8 were waited for; matrix products, arithmetic and copies ran while one was open for 15% of the time, Pallas kernels for 0%

profile of v6, /device:TPU:9, one launch (start us, length us, event | category | flops | bytes accessed | tf_op | source)
XLA Modules:
  0.0 132.6 jit_solution(14599684218734707706)
XLA Ops:
  0.9 4.7 %collective-permute-start = (bf16[256,128]{1,0:T(8,128)(2,1)S(1)}, bf16[256,128]{1,0:T(8,128)(2,1)S(1)}, u32[]{:S(2)}, u32[]{:S(2)}) collective-permute-start(bf16[256,128]{1,0:T(8,128)(2,1)S(1)} %get-tuple-element.37), channel_id=1, source_target_pairs={{0,32},{1,33},{2,34},{3,35},{4,36},{5,37},{6,38},{7,39},{8,40},{9,... | collective-permute-start | bytes 196616 | tf_op jit(solution)/shard_map/ppermute | solution.py:22
  5.6 1.3 collective-permute-start.1
  6.9 1.3 collective-permute-start.2
  11.1 14.8 %all-to-all-start = ((bf16[4,256,128]{2,1,0:T(8,128)(2,1)}), bf16[4,256,128]{2,1,0:T(8,128)(2,1)S(1)}, u32[]{:S(2)}, u32[]{:S(2)}) async-start(bf16[4,256,128]{2,1,0:T(8,128)(2,1)} %broadcast_in_dim.17), calls=%async_computation | async-start | bytes 524288 | tf_op jit(solution)/shard_map/all_to_all | solution.py:57
  25.9 1.3 fusion.25
  27.2 3.7 %collective-permute-start.6 = (bf16[2,128,1024]{2,1,0:T(8,128)(2,1)S(1)}, bf16[2,128,1024]{2,1,0:T(8,128)(2,1)S(1)}, u32[]{:S(2)}, u32[]{:S(2)}) collective-permute-start(bf16[2,128,1024]{2,1,0:T(8,128)(2,1)S(1)} %get-tuple-element.32), channel_id=1, source_target_pairs={{0,64},{64,0},{1,65},{65,1},{2,66},{66,2},{3,67},{67,3},{4,68},{68... | collective-permute-start | bytes 1572872 | tf_op jit(solution)/shard_map/ppermute | solution.py:51
  31.0 1.5 %collective-permute-done.6 = bf16[2,128,1024]{2,1,0:T(8,128)(2,1)S(1)} collective-permute-done((bf16[2,128,1024]{2,1,0:T(8,128)(2,1)S(1)}, bf16[2,128,1024]{2,1,0:T(8,128)(2,1)S(1)}, u32[]{:S(2)}, u32[]{:S(2)}) %collective-permute-start.6) | collective-permute-done | bytes 524320 | tf_op jit(solution)/shard_map/ppermute | solution.py:51
  32.6 1.7 %collective-permute-start.9 = (bf16[2,2,128,1024]{3,2,1,0:T(8,128)(2,1)S(1)}, bf16[2,2,128,1024]{3,2,1,0:T(8,128)(2,1)}, u32[]{:S(2)}, u32[]{:S(2)}) collective-permute-start(bf16[2,2,128,1024]{3,2,1,0:T(8,128)(2,1)S(1)} %maximum_select_fusion), channel_id=1, source_target_pairs={{384,0},{385,1},{386,2},{387,3},{388,4},{389,5},{390,6},{391,7},{3... | collective-permute-start | bytes 3145736 | tf_op jit(solution)/shard_map/ppermute | solution.py:54
  34.2 1.6 %collective-permute-start.8 = (bf16[2,2,128,1024]{3,2,1,0:T(8,128)(2,1)S(1)}, bf16[2,2,128,1024]{3,2,1,0:T(8,128)(2,1)}, u32[]{:S(2)}, u32[]{:S(2)}) collective-permute-start(bf16[2,2,128,1024]{3,2,1,0:T(8,128)(2,1)S(1)} %maximum_select_fusion), channel_id=1, source_target_pairs={{256,0},{257,1},{258,2},{259,3},{260,4},{261,5},{262,6},{263,7},{2... | collective-permute-start | bytes 3145736 | tf_op jit(solution)/shard_map/ppermute | solution.py:54
  35.9 3.2 %all-to-all-done = bf16[4,256,128]{2,1,0:T(8,128)(2,1)S(1)} async-done(((bf16[4,256,128]{2,1,0:T(8,128)(2,1)}), bf16[4,256,128]{2,1,0:T(8,128)(2,1)S(1)}, u32[]{:S(2)}, u32[]{:S(2)}) %all-to-all-start) | async-done | bytes 262176 | tf_op jit(solution)/shard_map/all_to_all | solution.py:57
  39.1 4.8 %collective-permute-start.3 = (bf16[4,256,128]{2,1,0:T(8,128)(2,1)S(1)}, bf16[4,256,128]{2,1,0:T(8,128)(2,1)S(1)}, u32[]{:S(2)}, u32[]{:S(2)}) collective-permute-start(bf16[4,256,128]{2,1,0:T(8,128)(2,1)S(1)} %all-to-all-done), channel_id=1, source_target_pairs={{1,0},{2,1},{3,2},{4,3},{5,4},{6,5},{7,6},{8,7},{9,8},{10,9},{11,1... | collective-permute-start | bytes 786440 | tf_op jit(solution)/shard_map/ppermute | solution.py:60
  43.9 7.0 %collective-permute-start.4 = (bf16[4,256,128]{2,1,0:T(8,128)(2,1)S(1)}, bf16[4,256,128]{2,1,0:T(8,128)(2,1)S(1)}, u32[]{:S(2)}, u32[]{:S(2)}) collective-permute-start(bf16[4,256,128]{2,1,0:T(8,128)(2,1)S(1)} %all-to-all-done), channel_id=1, source_target_pairs={{2,0},{15,1},{4,2},{1,3},{6,4},{3,5},{8,6},{5,7},{10,8},{7,9},{12,... | collective-permute-start | bytes 786440 | tf_op jit(solution)/shard_map/ppermute | solution.py:63
  51.0 2.9 %collective-permute-start.5 = (bf16[4,256,128]{2,1,0:T(8,128)(2,1)S(1)}, bf16[4,256,128]{2,1,0:T(8,128)(2,1)S(1)}, u32[]{:S(2)}, u32[]{:S(2)}) collective-permute-start(bf16[4,256,128]{2,1,0:T(8,128)(2,1)S(1)} %all-to-all-done), channel_id=1, source_target_pairs={{15,0},{0,1},{1,2},{2,3},{3,4},{4,5},{5,6},{6,7},{7,8},{8,9},{9,10... | collective-permute-start | bytes 786440 | tf_op jit(solution)/shard_map/ppermute | solution.py:60
  53.9 3.1 %collective-permute-start.7 = (bf16[2,2,128,1024]{3,2,1,0:T(8,128)(2,1)S(1)}, bf16[2,2,128,1024]{3,2,1,0:T(8,128)(2,1)}, u32[]{:S(2)}, u32[]{:S(2)}) collective-permute-start(bf16[2,2,128,1024]{3,2,1,0:T(8,128)(2,1)S(1)} %maximum_select_fusion), channel_id=1, source_target_pairs={{128,0},{129,1},{130,2},{131,3},{132,4},{133,5},{134,6},{135,7},{1... | collective-permute-start | bytes 3145736 | tf_op jit(solution)/shard_map/ppermute | solution.py:54
  57.0 1.6 %collective-permute-done.4 = bf16[4,256,128]{2,1,0:T(8,128)(2,1)S(1)} collective-permute-done((bf16[4,256,128]{2,1,0:T(8,128)(2,1)S(1)}, bf16[4,256,128]{2,1,0:T(8,128)(2,1)S(1)}, u32[]{:S(2)}, u32[]{:S(2)}) %collective-permute-start.4) | collective-permute-done | bytes 262176 | tf_op jit(solution)/shard_map/ppermute | solution.py:63
  58.7 4.1 %collective-permute-done.5 = bf16[4,256,128]{2,1,0:T(8,128)(2,1)S(1)} collective-permute-done((bf16[4,256,128]{2,1,0:T(8,128)(2,1)S(1)}, bf16[4,256,128]{2,1,0:T(8,128)(2,1)S(1)}, u32[]{:S(2)}, u32[]{:S(2)}) %collective-permute-start.5) | collective-permute-done | bytes 262176 | tf_op jit(solution)/shard_map/ppermute | solution.py:60
  63.2 1.8 %broadcast_in_dim.19 = bf16[4,8,256,128]{3,2,1,0:T(8,128)(2,1)} broadcast(bf16[8,256,128]{2,1,0:T(8,128)(2,1)S(1)} %bitcast.67), dimensions={1,2,3} | broadcast | bytes 2621440 | tf_op jit(solution)/shard_map/broadcast_in_dim | solution.py:29
  65.0 4.5 %all-to-all-start.1 = ((bf16[4,8,256,128]{3,2,1,0:T(8,128)(2,1)}), bf16[4,8,256,128]{3,2,1,0:T(8,128)(2,1)}, u32[]{:S(2)}, u32[]{:S(2)}) async-start(bf16[4,8,256,128]{3,2,1,0:T(8,128)(2,1)} %broadcast_in_dim.19), calls=%async_computation.1 | async-start | bytes 4194304 | tf_op jit(solution)/shard_map/all_to_all | solution.py:72
  71.6 1.3 fusion.31
  72.9 2.3 %collective-permute-done.7 = bf16[2,2,128,1024]{3,2,1,0:T(8,128)(2,1)} collective-permute-done((bf16[2,2,128,1024]{3,2,1,0:T(8,128)(2,1)S(1)}, bf16[2,2,128,1024]{3,2,1,0:T(8,128)(2,1)}, u32[]{:S(2)}, u32[]{:S(2)}) %collective-permute-start.7) | collective-permute-done | bytes 1048608 | tf_op jit(solution)/shard_map/ppermute | solution.py:54
  78.1 1.5 %broadcast_select_fusion = (bf16[1024,128]{1,0:T(8,128)(2,1)}, bf16[1024,128]{1,0:T(8,128)(2,1)}) fusion(pred[]{:T(512)S(6)} %and.22, bf16[1024,128]{1,0:T(8,128)(2,1)S(1)} %dynamic-slice_negate_fusion, bf16[1024,1024]{1,0:T(8,128)(2,1)S(1)} %get-tuple-element.14, bf16[1024,128]{1,0:T(8,128)(2,1)S(1)} %convolution_convert_fusion.4, pred[]{:T(512)S(6)} %lt.46), kind=kOutput, calls=%fused_computation.39 | convolution fusion | flops 268828672 | bytes 3145730 | tf_op jit(solution)/shard_map/dot_general | solution.py:12
  79.9 4.8 %collective-permute-start.13 = (bf16[256,1024]{0,1:T(8,128)(2,1)S(1)}, bf16[256,1024]{0,1:T(8,128)(2,1)S(1)}, u32[]{:S(2)}, u32[]{:S(2)}) collective-permute-start(bf16[256,1024]{0,1:T(8,128)(2,1)S(1)} %bitcast.62), channel_id=1, source_target_pairs={{144,128},{160,144},{176,160},{128,176},{272,256},{288,272},{304,2... | collective-permute-start | bytes 1572872 | tf_op jit(solution)/shard_map/ppermute | solution.py:104
  84.7 1.9 %collective-permute-start.15 = (bf16[256,1024]{0,1:T(8,128)(2,1)S(1)}, bf16[256,1024]{0,1:T(8,128)(2,1)}, u32[]{:S(2)}, u32[]{:S(2)}) collective-permute-start(bf16[256,1024]{0,1:T(8,128)(2,1)S(1)} %bitcast.63), channel_id=1, source_target_pairs={{176,128},{128,144},{144,160},{160,176},{304,256},{256,272},{272,2... | collective-permute-start | bytes 1572872 | tf_op jit(solution)/shard_map/ppermute | solution.py:104
  86.6 6.6 %all-gather = bf16[2048,128]{1,0:T(8,128)(2,1)S(1)} all-gather(bf16[1024,128]{1,0:T(8,128)(2,1)} %get-tuple-element.39), channel_id=2, replica_groups=mesh['y'=4,'core'=2,'x'=4,'z'=16] {'core'}, dimensions={0}, use_global_device_ids=true | all-gather | bytes 786432 | tf_op jit(solution)/shard_map/all_gather | solution.py:33
  93.9 1.8 %copy.8 = bf16[4,256,128,8]{2,1,0,3:T(8,128)(2,1)S(1)} copy(bf16[4,256,128,8]{2,1,3,0:T(8,128)(2,1)} %bitcast.3) | data formatting | bytes 4194304 | tf_op jit(solution)/shard_map/xzrk,zkn->xrn/dot_general | solution.py:90
  98.9 7.9 %all-gather.1 = bf16[2048,128]{1,0:T(8,128)(2,1)S(1)} all-gather(bf16[1024,128]{1,0:T(8,128)(2,1)S(1)} %fusion.17), channel_id=3, replica_groups=mesh['y'=4,'core'=2,'x'=4,'z'=16] {'core'}, dimensions={0}, use_global_device_ids=true | all-gather | bytes 786432 | tf_op jit(solution)/shard_map/all_gather | solution.py:33
  109.7 1.3 collective-permute-start.11
  112.9 2.9 %collective-permute-start.14 = (bf16[128,1024]{0,1:T(8,128)(2,1)S(1)}, bf16[128,1024]{0,1:T(8,128)(2,1)S(1)}, u32[]{:S(2)}, u32[]{:S(2)}) collective-permute-start(bf16[128,1024]{0,1:T(8,128)(2,1)S(1)} %slice.78), channel_id=1, source_target_pairs={{144,128},{160,144},{176,160},{128,176},{272,256},{288,272},{304,2... | collective-permute-start | bytes 786440 | tf_op jit(solution)/shard_map/ppermute | solution.py:104
  115.8 2.5 %collective-permute-start.16 = (bf16[128,1024]{0,1:T(8,128)(2,1)S(1)}, bf16[128,1024]{0,1:T(8,128)(2,1)S(1)}, u32[]{:S(2)}, u32[]{:S(2)}) collective-permute-start(bf16[128,1024]{0,1:T(8,128)(2,1)S(1)} %slice.79), channel_id=1, source_target_pairs={{176,128},{128,144},{144,160},{160,176},{304,256},{256,272},{272,2... | collective-permute-start | bytes 786440 | tf_op jit(solution)/shard_map/ppermute | solution.py:104
  118.3 7.4 %collective-permute-done.11 = bf16[1024,128]{1,0:T(8,128)(2,1)S(1)} collective-permute-done((bf16[1024,128]{1,0:T(8,128)(2,1)S(1)}, bf16[1024,128]{1,0:T(8,128)(2,1)S(1)}, u32[]{:S(2)}, u32[]{:S(2)}) %collective-permute-start.11) | collective-permute-done | bytes 262176 | tf_op jit(solution)/shard_map/ppermute | solution.py:22
  125.7 3.0 %all-gather.2 = bf16[2048,128]{1,0:T(8,128)(2,1)S(1)} all-gather(bf16[1024,128]{1,0:T(8,128)(2,1)S(1)} %select_select_fusion), channel_id=4, replica_groups=mesh['y'=4,'core'=2,'x'=4,'z'=16] {'core'}, dimensions={0}, use_global_device_ids=true | all-gather | bytes 786432 | tf_op jit(solution)/shard_map/all_gather | solution.py:33
  131.2 1.5 %fusion.19 = bf16[1024,128]{1,0:T(8,128)(2,1)} fusion(f32[1024,128]{1,0:T(8,128)S(1)} %convolution_bitcast_fusion, bf16[1792,1024]{0,1:T(8,128)(2,1)S(1)} %constant_dynamic-update-slice_fusion.7, s32[]{:T(128)S(6)} %select_n.185, bf16[1024,128]{1,0:T(8,128)(2,1)S(1)} %copy-done.9, bf16[1024,128]{1,0:T(8,128)(2,1)S(1)} %copy-done.11, ...), kind=kOutput, calls=%fused_computation.28 | convolution fusion | flops 269746176 | bytes 4456458 | tf_op jit(solution)/shard_map/dot_general | solution.py:12
  (92 shorter events, 20.6 us)
Async XLA Ops:
  0.9 7.3 %collective-permute-start = (bf16[256,128]{1,0:T(8,128)(2,1)S(1)}, bf16[256,128]{1,0:T(8,128)(2,1)S(1)}, u32[]{:S(2)}, u32[]{:S(2)}) collective-permute-start(bf16[256,128]{1,0:T(8,128)(2,1)S(1)} %get-tuple-element.37), channel_id=1, source_target_pairs={{0,32},{1,33},{2,34},{3,35},{4,36},{5,37},{6,38},{7,39},{8,40},{9,... | collective-permute-start | bytes 196616 | tf_op jit(solution)/shard_map/ppermute | solution.py:22
  5.6 3.0 %collective-permute-start.1 = (bf16[256,128]{1,0:T(8,128)(2,1)S(1)}, bf16[256,128]{1,0:T(8,128)(2,1)S(1)}, u32[]{:S(2)}, u32[]{:S(2)}) collective-permute-start(bf16[256,128]{1,0:T(8,128)(2,1)S(1)} %get-tuple-element.36), channel_id=1, source_target_pairs={{0,16},{1,17},{2,18},{3,19},{4,20},{5,21},{6,22},{7,23},{8,24},{9,... | collective-permute-start | bytes 196616 | tf_op jit(solution)/shard_map/ppermute | solution.py:22
  6.9 2.6 %collective-permute-start.2 = (bf16[256,128]{1,0:T(8,128)(2,1)S(1)}, bf16[256,128]{1,0:T(8,128)(2,1)S(1)}, u32[]{:S(2)}, u32[]{:S(2)}) collective-permute-start(bf16[256,128]{1,0:T(8,128)(2,1)S(1)} %get-tuple-element.35), channel_id=1, source_target_pairs={{0,48},{1,49},{2,50},{3,51},{4,52},{5,53},{6,54},{7,55},{8,56},{9,... | collective-permute-start | bytes 196616 | tf_op jit(solution)/shard_map/ppermute | solution.py:22
  11.1 28.0 %all-to-all-start = ((bf16[4,256,128]{2,1,0:T(8,128)(2,1)}), bf16[4,256,128]{2,1,0:T(8,128)(2,1)S(1)}, u32[]{:S(2)}, u32[]{:S(2)}) async-start(bf16[4,256,128]{2,1,0:T(8,128)(2,1)} %broadcast_in_dim.17), calls=%async_computation | async-start | bytes 524288 | tf_op jit(solution)/shard_map/all_to_all | solution.py:57
  27.2 5.2 %collective-permute-start.6 = (bf16[2,128,1024]{2,1,0:T(8,128)(2,1)S(1)}, bf16[2,128,1024]{2,1,0:T(8,128)(2,1)S(1)}, u32[]{:S(2)}, u32[]{:S(2)}) collective-permute-start(bf16[2,128,1024]{2,1,0:T(8,128)(2,1)S(1)} %get-tuple-element.32), channel_id=1, source_target_pairs={{0,64},{64,0},{1,65},{65,1},{2,66},{66,2},{3,67},{67,3},{4,68},{68... | collective-permute-start | bytes 1572872 | tf_op jit(solution)/shard_map/ppermute | solution.py:51
  32.6 37.8 %collective-permute-start.9 = (bf16[2,2,128,1024]{3,2,1,0:T(8,128)(2,1)S(1)}, bf16[2,2,128,1024]{3,2,1,0:T(8,128)(2,1)}, u32[]{:S(2)}, u32[]{:S(2)}) collective-permute-start(bf16[2,2,128,1024]{3,2,1,0:T(8,128)(2,1)S(1)} %maximum_select_fusion), channel_id=1, source_target_pairs={{384,0},{385,1},{386,2},{387,3},{388,4},{389,5},{390,6},{391,7},{3... | collective-permute-start | bytes 3145736 | tf_op jit(solution)/shard_map/ppermute | solution.py:54
  34.2 37.4 %collective-permute-start.8 = (bf16[2,2,128,1024]{3,2,1,0:T(8,128)(2,1)S(1)}, bf16[2,2,128,1024]{3,2,1,0:T(8,128)(2,1)}, u32[]{:S(2)}, u32[]{:S(2)}) collective-permute-start(bf16[2,2,128,1024]{3,2,1,0:T(8,128)(2,1)S(1)} %maximum_select_fusion), channel_id=1, source_target_pairs={{256,0},{257,1},{258,2},{259,3},{260,4},{261,5},{262,6},{263,7},{2... | collective-permute-start | bytes 3145736 | tf_op jit(solution)/shard_map/ppermute | solution.py:54
  39.1 14.9 %collective-permute-start.3 = (bf16[4,256,128]{2,1,0:T(8,128)(2,1)S(1)}, bf16[4,256,128]{2,1,0:T(8,128)(2,1)S(1)}, u32[]{:S(2)}, u32[]{:S(2)}) collective-permute-start(bf16[4,256,128]{2,1,0:T(8,128)(2,1)S(1)} %all-to-all-done), channel_id=1, source_target_pairs={{1,0},{2,1},{3,2},{4,3},{5,4},{6,5},{7,6},{8,7},{9,8},{10,9},{11,1... | collective-permute-start | bytes 786440 | tf_op jit(solution)/shard_map/ppermute | solution.py:60
  43.9 14.8 %collective-permute-start.4 = (bf16[4,256,128]{2,1,0:T(8,128)(2,1)S(1)}, bf16[4,256,128]{2,1,0:T(8,128)(2,1)S(1)}, u32[]{:S(2)}, u32[]{:S(2)}) collective-permute-start(bf16[4,256,128]{2,1,0:T(8,128)(2,1)S(1)} %all-to-all-done), channel_id=1, source_target_pairs={{2,0},{15,1},{4,2},{1,3},{6,4},{3,5},{8,6},{5,7},{10,8},{7,9},{12,... | collective-permute-start | bytes 786440 | tf_op jit(solution)/shard_map/ppermute | solution.py:63
  51.0 11.8 %collective-permute-start.5 = (bf16[4,256,128]{2,1,0:T(8,128)(2,1)S(1)}, bf16[4,256,128]{2,1,0:T(8,128)(2,1)S(1)}, u32[]{:S(2)}, u32[]{:S(2)}) collective-permute-start(bf16[4,256,128]{2,1,0:T(8,128)(2,1)S(1)} %all-to-all-done), channel_id=1, source_target_pairs={{15,0},{0,1},{1,2},{2,3},{3,4},{4,5},{5,6},{6,7},{7,8},{8,9},{9,10... | collective-permute-start | bytes 786440 | tf_op jit(solution)/shard_map/ppermute | solution.py:60
  53.9 21.2 %collective-permute-start.7 = (bf16[2,2,128,1024]{3,2,1,0:T(8,128)(2,1)S(1)}, bf16[2,2,128,1024]{3,2,1,0:T(8,128)(2,1)}, u32[]{:S(2)}, u32[]{:S(2)}) collective-permute-start(bf16[2,2,128,1024]{3,2,1,0:T(8,128)(2,1)S(1)} %maximum_select_fusion), channel_id=1, source_target_pairs={{128,0},{129,1},{130,2},{131,3},{132,4},{133,5},{134,6},{135,7},{1... | collective-permute-start | bytes 3145736 | tf_op jit(solution)/shard_map/ppermute | solution.py:54
  65.0 28.9 %all-to-all-start.1 = ((bf16[4,8,256,128]{3,2,1,0:T(8,128)(2,1)}), bf16[4,8,256,128]{3,2,1,0:T(8,128)(2,1)}, u32[]{:S(2)}, u32[]{:S(2)}) async-start(bf16[4,8,256,128]{3,2,1,0:T(8,128)(2,1)} %broadcast_in_dim.19), calls=%async_computation.1 | async-start | bytes 4194304 | tf_op jit(solution)/shard_map/all_to_all | solution.py:72
  77.1 2.5 %copy-start.2 = (bf16[1024,1024]{1,0:T(8,128)(2,1)}, bf16[1024,1024]{1,0:T(8,128)(2,1)S(1)}, u32[]{:S(2)}) copy-start(bf16[1024,1024]{1,0:T(8,128)(2,1)S(1)} %get-tuple-element.14) | copy-start | bytes 6291460
  77.3 2.4 %copy-start.12 = (bf16[1024,128]{1,0:T(8,128)(2,1)}, bf16[1024,128]{1,0:T(8,128)(2,1)S(1)}, u32[]{:S(2)}) copy-start(bf16[1024,128]{1,0:T(8,128)(2,1)S(1)} %dynamic-slice_negate_fusion) | copy-start | bytes 786436
  78.1 1.6 %copy-start.6 = (bf16[1024,128]{1,0:T(8,128)(2,1)}, bf16[1024,128]{1,0:T(8,128)(2,1)S(1)}, u32[]{:S(2)}) copy-start(bf16[1024,128]{1,0:T(8,128)(2,1)S(1)} %convolution_convert_fusion.4) | copy-start | bytes 786436
  78.1 1.6 %copy-start.4 = (bf16[2,4,256,128]{3,2,1,0:T(8,128)(2,1)S(1)}, bf16[2,4,256,128]{3,2,1,0:T(8,128)(2,1)}, u32[]{:S(2)}) copy-start(bf16[2,4,256,128]{3,2,1,0:T(8,128)(2,1)} %copy.9) | copy-start | bytes 1572868
  79.9 31.9 %collective-permute-start.13 = (bf16[256,1024]{0,1:T(8,128)(2,1)S(1)}, bf16[256,1024]{0,1:T(8,128)(2,1)S(1)}, u32[]{:S(2)}, u32[]{:S(2)}) collective-permute-start(bf16[256,1024]{0,1:T(8,128)(2,1)S(1)} %bitcast.62), channel_id=1, source_target_pairs={{144,128},{160,144},{176,160},{128,176},{272,256},{288,272},{304,2... | collective-permute-start | bytes 1572872 | tf_op jit(solution)/shard_map/ppermute | solution.py:104
  84.7 27.1 %collective-permute-start.15 = (bf16[256,1024]{0,1:T(8,128)(2,1)S(1)}, bf16[256,1024]{0,1:T(8,128)(2,1)}, u32[]{:S(2)}, u32[]{:S(2)}) collective-permute-start(bf16[256,1024]{0,1:T(8,128)(2,1)S(1)} %bitcast.63), channel_id=1, source_target_pairs={{176,128},{128,144},{144,160},{160,176},{304,256},{256,272},{272,2... | collective-permute-start | bytes 1572872 | tf_op jit(solution)/shard_map/ppermute | solution.py:104
  93.9 1.8 %copy-start.14 = (bf16[1024,128]{1,0:T(8,128)(2,1)S(1)}, bf16[1024,128]{1,0:T(8,128)(2,1)}, u32[]{:S(2)}) copy-start(bf16[1024,128]{1,0:T(8,128)(2,1)} %slice.74) | copy-start | bytes 786436
  95.7 11.2 %copy-start = (bf16[4,256,128,8]{2,1,0,3:T(8,128)(2,1)}, bf16[4,256,128,8]{2,1,0,3:T(8,128)(2,1)S(1)}, u32[]{:S(2)}) copy-start(bf16[4,256,128,8]{2,1,0,3:T(8,128)(2,1)S(1)} %copy.8) | copy-start | bytes 6291460
  95.7 2.4 %copy-start.3 = (bf16[1024,1024]{1,0:T(8,128)(2,1)S(1)}, bf16[1024,1024]{1,0:T(8,128)(2,1)}, u32[]{:S(2)}) copy-start(bf16[1024,1024]{1,0:T(8,128)(2,1)} %copy-done.2) | copy-start | bytes 6291460
  95.7 2.5 %copy-start.13 = (bf16[1024,128]{1,0:T(8,128)(2,1)S(1)}, bf16[1024,128]{1,0:T(8,128)(2,1)}, u32[]{:S(2)}) copy-start(bf16[1024,128]{1,0:T(8,128)(2,1)} %copy-done.12) | copy-start | bytes 786436
  106.9 1.4 %copy-start.15 = (bf16[1024,128]{1,0:T(8,128)(2,1)S(1)}, bf16[1024,128]{1,0:T(8,128)(2,1)}, u32[]{:S(2)}) copy-start(bf16[1024,128]{1,0:T(8,128)(2,1)} %get-tuple-element.38) | copy-start | bytes 786436
  109.0 9.3 %collective-permute-start.10 = (bf16[1024,128]{1,0:T(8,128)(2,1)S(1)}, bf16[1024,128]{1,0:T(8,128)(2,1)S(1)}, u32[]{:S(2)}, u32[]{:S(2)}) collective-permute-start(bf16[1024,128]{1,0:T(8,128)(2,1)S(1)} %fusion.18), channel_id=1, source_target_pairs={{0,256},{1,257},{2,258},{3,259},{4,260},{5,261},{6,262},{7,263},{8... | collective-permute-start | bytes 786440 | tf_op jit(solution)/shard_map/ppermute | solution.py:22
  109.7 16.0 %collective-permute-start.11 = (bf16[1024,128]{1,0:T(8,128)(2,1)S(1)}, bf16[1024,128]{1,0:T(8,128)(2,1)S(1)}, u32[]{:S(2)}, u32[]{:S(2)}) collective-permute-start(bf16[1024,128]{1,0:T(8,128)(2,1)S(1)} %fusion.18), channel_id=1, source_target_pairs={{0,128},{1,129},{2,130},{3,131},{4,132},{5,133},{6,134},{7,135},{8... | collective-permute-start | bytes 786440 | tf_op jit(solution)/shard_map/ppermute | solution.py:22
  111.0 14.7 %collective-permute-start.12 = (bf16[1024,128]{1,0:T(8,128)(2,1)S(1)}, bf16[1024,128]{1,0:T(8,128)(2,1)S(1)}, u32[]{:S(2)}, u32[]{:S(2)}) collective-permute-start(bf16[1024,128]{1,0:T(8,128)(2,1)S(1)} %fusion.18), channel_id=1, source_target_pairs={{0,384},{1,385},{2,386},{3,387},{4,388},{5,389},{6,390},{7,391},{8... | collective-permute-start | bytes 786440 | tf_op jit(solution)/shard_map/ppermute | solution.py:22
  112.8 16.1 %copy-start.1 = (bf16[4,256,128,8]{2,1,0,3:T(8,128)(2,1)S(1)}, bf16[4,256,128,8]{2,1,0,3:T(8,128)(2,1)}, u32[]{:S(2)}) copy-start(bf16[4,256,128,8]{2,1,0,3:T(8,128)(2,1)} %copy-done) | copy-start | bytes 6291460
  112.9 16.0 %collective-permute-start.14 = (bf16[128,1024]{0,1:T(8,128)(2,1)S(1)}, bf16[128,1024]{0,1:T(8,128)(2,1)S(1)}, u32[]{:S(2)}, u32[]{:S(2)}) collective-permute-start(bf16[128,1024]{0,1:T(8,128)(2,1)S(1)} %slice.78), channel_id=1, source_target_pairs={{144,128},{160,144},{176,160},{128,176},{272,256},{288,272},{304,2... | collective-permute-start | bytes 786440 | tf_op jit(solution)/shard_map/ppermute | solution.py:104
  115.8 13.8 %collective-permute-start.16 = (bf16[128,1024]{0,1:T(8,128)(2,1)S(1)}, bf16[128,1024]{0,1:T(8,128)(2,1)S(1)}, u32[]{:S(2)}, u32[]{:S(2)}) collective-permute-start(bf16[128,1024]{0,1:T(8,128)(2,1)S(1)} %slice.79), channel_id=1, source_target_pairs={{176,128},{128,144},{144,160},{160,176},{304,256},{256,272},{272,2... | collective-permute-start | bytes 786440 | tf_op jit(solution)/shard_map/ppermute | solution.py:104
  129.7 1.4 %copy-start.7 = (bf16[1024,128]{1,0:T(8,128)(2,1)S(1)}, bf16[1024,128]{1,0:T(8,128)(2,1)}, u32[]{:S(2)}) copy-start(bf16[1024,128]{1,0:T(8,128)(2,1)} %copy-done.6) | copy-start | bytes 786436
  129.7 1.4 %copy-start.9 = (bf16[1024,128]{1,0:T(8,128)(2,1)S(1)}, bf16[1024,128]{1,0:T(8,128)(2,1)}, u32[]{:S(2)}) copy-start(bf16[1024,128]{1,0:T(8,128)(2,1)} %copy-done.8) | copy-start | bytes 786436
  129.7 1.4 %copy-start.11 = (bf16[1024,128]{1,0:T(8,128)(2,1)S(1)}, bf16[1024,128]{1,0:T(8,128)(2,1)}, u32[]{:S(2)}) copy-start(bf16[1024,128]{1,0:T(8,128)(2,1)} %copy-done.10) | copy-start | bytes 786436
  (3 other events, 2.4 us)

commit v7 on v6

--- a/solution.py
+++ b/solution.py
@@ -84,6 +84,7 @@
     c0 = jnp.where(in0, minus_u, times(inv_u, r))
     base = lax.optimization_barrier(jnp.where(in1, zeros, c0))
     c0x = cores(c0)[0]
+    kept_half, c0x = lax.optimization_barrier((half(core), c0x))
 
     def product(left, right):
         right = right.reshape(8, 128, 128)
@@ -97,7 +98,7 @@
     s = lax.optimization_barrier(times(inv_l, t))
     d = (base.astype(F32) - dot(inv_u, s)).astype(BF)
     right = jnp.where(core == 0, d, c1)
-    late = after(half(core), c0).transpose(1, 0, 2).reshape(256, NB)
+    late = kept_half.transpose(1, 0, 2).reshape(256, NB)
 
     def from_x(value, distance):
         planes = [(4 * p + (k + distance) % 4, 4 * p + k) for p in range(1, 4) for k in range(4)]

time: 134 us -> 134 us (level)
  blocking collectives: 17.5 us -> 14.7 us
  starting transfers between devices: 66.1 us -> 68.2 us
    all_gather x3, blocking collectives: 17.5 us -> 14.7 us  [cores(): return lax.all_gather(value, 'core', axis=0)]
    ppermute x4, starting transfers between devices: 12.1 us -> 14.3 us  [from_x(): return lax.ppermute(value, ('y', 'x'), planes)]
where the time goes in v7:
time: 134 us; the launch traced here: 133 us
  starting transfers between devices  68.2 us (51%)
  waiting for transfers between devices  21.9 us (16%)
  local copies, waits for them, and re-layouts  15.3 us (11%)
  blocking collectives  14.7 us (11%)
  matrix products  8.59 us (6%)
  other arithmetic  3.16 us (2%)
    all_to_all x1, starting transfers between devices, shards(): own = lax.all_to_all(copies(share, 4), 'z', 0, 0, axis_index_groups=fours)  14.8 us
    all_gather x3, blocking collectives, cores(): return lax.all_gather(value, 'core', axis=0)  14.7 us
    ppermute x4, starting transfers between devices, from_x(): return lax.ppermute(value, ('y', 'x'), planes)  14.3 us
    ppermute x6, starting transfers between devices, from_first(): got = {k: lax.ppermute(values[k], axis, [(0, k)]) for k in (3, 1, 2)}  9.88 us
    ppermute x6, waiting for transfers between devices, from_first(): got = {k: lax.ppermute(values[k], axis, [(0, k)]) for k in (3, 1, 2)}  9.24 us
    ppermute x2, starting transfers between devices, from_z(): lax.ppermute(value, 'z', [((k + distance) % 16, k) for k in range(16)])  7.73 us
    ppermute x1, starting transfers between devices, shards(): lax.ppermute(own, 'z', [((k + 2 - 4 * (k % 2)) % 16, k) for k in range(16)])  7 us
    dot_general x7, matrix products, dot(): return jnp.dot(a, b, preferred_element_type=F32)  6.44 us
  transfers between devices with their start and end apart: 19, of which 8 were waited for; matrix products, arithmetic and copies ran while one was open for 15% of the time, Pallas kernels for 0%

profile of v7, /device:TPU:9, one launch (start us, length us, event | category | flops | bytes accessed | tf_op | source)
XLA Modules:
  0.0 132.6 jit_solution(3557770132769475595)
XLA Ops:
  0.9 4.7 %collective-permute-start = (bf16[256,128]{1,0:T(8,128)(2,1)S(1)}, bf16[256,128]{1,0:T(8,128)(2,1)S(1)}, u32[]{:S(2)}, u32[]{:S(2)}) collective-permute-start(bf16[256,128]{1,0:T(8,128)(2,1)S(1)} %get-tuple-element.39), channel_id=1, source_target_pairs={{0,32},{1,33},{2,34},{3,35},{4,36},{5,37},{6,38},{7,39},{8,40},{9,... | collective-permute-start | bytes 196616 | tf_op jit(solution)/shard_map/ppermute | solution.py:22
  5.6 1.3 collective-permute-start.1
  6.9 1.3 collective-permute-start.2
  11.1 14.8 %all-to-all-start = ((bf16[4,256,128]{2,1,0:T(8,128)(2,1)}), bf16[4,256,128]{2,1,0:T(8,128)(2,1)S(1)}, u32[]{:S(2)}, u32[]{:S(2)}) async-start(bf16[4,256,128]{2,1,0:T(8,128)(2,1)} %broadcast_in_dim.17), calls=%async_computation | async-start | bytes 524288 | tf_op jit(solution)/shard_map/all_to_all | solution.py:57
  25.9 1.3 fusion.25
  27.2 3.7 %collective-permute-start.6 = (bf16[2,128,1024]{2,1,0:T(8,128)(2,1)S(1)}, bf16[2,128,1024]{2,1,0:T(8,128)(2,1)S(1)}, u32[]{:S(2)}, u32[]{:S(2)}) collective-permute-start(bf16[2,128,1024]{2,1,0:T(8,128)(2,1)S(1)} %get-tuple-element.34), channel_id=1, source_target_pairs={{0,64},{64,0},{1,65},{65,1},{2,66},{66,2},{3,67},{67,3},{4,68},{68... | collective-permute-start | bytes 1572872 | tf_op jit(solution)/shard_map/ppermute | solution.py:51
  31.0 1.5 %collective-permute-done.6 = bf16[2,128,1024]{2,1,0:T(8,128)(2,1)S(1)} collective-permute-done((bf16[2,128,1024]{2,1,0:T(8,128)(2,1)S(1)}, bf16[2,128,1024]{2,1,0:T(8,128)(2,1)S(1)}, u32[]{:S(2)}, u32[]{:S(2)}) %collective-permute-start.6) | collective-permute-done | bytes 524320 | tf_op jit(solution)/shard_map/ppermute | solution.py:51
  32.6 1.7 %collective-permute-start.9 = (bf16[2,2,128,1024]{3,2,1,0:T(8,128)(2,1)S(1)}, bf16[2,2,128,1024]{3,2,1,0:T(8,128)(2,1)}, u32[]{:S(2)}, u32[]{:S(2)}) collective-permute-start(bf16[2,2,128,1024]{3,2,1,0:T(8,128)(2,1)S(1)} %maximum_select_fusion), channel_id=1, source_target_pairs={{384,0},{385,1},{386,2},{387,3},{388,4},{389,5},{390,6},{391,7},{3... | collective-permute-start | bytes 3145736 | tf_op jit(solution)/shard_map/ppermute | solution.py:54
  34.2 1.6 %collective-permute-start.8 = (bf16[2,2,128,1024]{3,2,1,0:T(8,128)(2,1)S(1)}, bf16[2,2,128,1024]{3,2,1,0:T(8,128)(2,1)}, u32[]{:S(2)}, u32[]{:S(2)}) collective-permute-start(bf16[2,2,128,1024]{3,2,1,0:T(8,128)(2,1)S(1)} %maximum_select_fusion), channel_id=1, source_target_pairs={{256,0},{257,1},{258,2},{259,3},{260,4},{261,5},{262,6},{263,7},{2... | collective-permute-start | bytes 3145736 | tf_op jit(solution)/shard_map/ppermute | solution.py:54
  35.9 3.2 %all-to-all-done = bf16[4,256,128]{2,1,0:T(8,128)(2,1)S(1)} async-done(((bf16[4,256,128]{2,1,0:T(8,128)(2,1)}), bf16[4,256,128]{2,1,0:T(8,128)(2,1)S(1)}, u32[]{:S(2)}, u32[]{:S(2)}) %all-to-all-start) | async-done | bytes 262176 | tf_op jit(solution)/shard_map/all_to_all | solution.py:57
  39.1 4.8 %collective-permute-start.3 = (bf16[4,256,128]{2,1,0:T(8,128)(2,1)S(1)}, bf16[4,256,128]{2,1,0:T(8,128)(2,1)S(1)}, u32[]{:S(2)}, u32[]{:S(2)}) collective-permute-start(bf16[4,256,128]{2,1,0:T(8,128)(2,1)S(1)} %all-to-all-done), channel_id=1, source_target_pairs={{1,0},{2,1},{3,2},{4,3},{5,4},{6,5},{7,6},{8,7},{9,8},{10,9},{11,1... | collective-permute-start | bytes 786440 | tf_op jit(solution)/shard_map/ppermute | solution.py:60
  43.9 7.0 %collective-permute-start.4 = (bf16[4,256,128]{2,1,0:T(8,128)(2,1)S(1)}, bf16[4,256,128]{2,1,0:T(8,128)(2,1)S(1)}, u32[]{:S(2)}, u32[]{:S(2)}) collective-permute-start(bf16[4,256,128]{2,1,0:T(8,128)(2,1)S(1)} %all-to-all-done), channel_id=1, source_target_pairs={{2,0},{15,1},{4,2},{1,3},{6,4},{3,5},{8,6},{5,7},{10,8},{7,9},{12,... | collective-permute-start | bytes 786440 | tf_op jit(solution)/shard_map/ppermute | solution.py:63
  51.0 2.9 %collective-permute-start.5 = (bf16[4,256,128]{2,1,0:T(8,128)(2,1)S(1)}, bf16[4,256,128]{2,1,0:T(8,128)(2,1)S(1)}, u32[]{:S(2)}, u32[]{:S(2)}) collective-permute-start(bf16[4,256,128]{2,1,0:T(8,128)(2,1)S(1)} %all-to-all-done), channel_id=1, source_target_pairs={{15,0},{0,1},{1,2},{2,3},{3,4},{4,5},{5,6},{6,7},{7,8},{8,9},{9,10... | collective-permute-start | bytes 786440 | tf_op jit(solution)/shard_map/ppermute | solution.py:60
  53.9 3.1 %collective-permute-start.7 = (bf16[2,2,128,1024]{3,2,1,0:T(8,128)(2,1)S(1)}, bf16[2,2,128,1024]{3,2,1,0:T(8,128)(2,1)}, u32[]{:S(2)}, u32[]{:S(2)}) collective-permute-start(bf16[2,2,128,1024]{3,2,1,0:T(8,128)(2,1)S(1)} %maximum_select_fusion), channel_id=1, source_target_pairs={{128,0},{129,1},{130,2},{131,3},{132,4},{133,5},{134,6},{135,7},{1... | collective-permute-start | bytes 3145736 | tf_op jit(solution)/shard_map/ppermute | solution.py:54
  57.0 1.6 %collective-permute-done.4 = bf16[4,256,128]{2,1,0:T(8,128)(2,1)S(1)} collective-permute-done((bf16[4,256,128]{2,1,0:T(8,128)(2,1)S(1)}, bf16[4,256,128]{2,1,0:T(8,128)(2,1)S(1)}, u32[]{:S(2)}, u32[]{:S(2)}) %collective-permute-start.4) | collective-permute-done | bytes 262176 | tf_op jit(solution)/shard_map/ppermute | solution.py:63
  58.7 4.1 %collective-permute-done.5 = bf16[4,256,128]{2,1,0:T(8,128)(2,1)S(1)} collective-permute-done((bf16[4,256,128]{2,1,0:T(8,128)(2,1)S(1)}, bf16[4,256,128]{2,1,0:T(8,128)(2,1)S(1)}, u32[]{:S(2)}, u32[]{:S(2)}) %collective-permute-start.5) | collective-permute-done | bytes 262176 | tf_op jit(solution)/shard_map/ppermute | solution.py:60
  63.2 1.8 %broadcast_in_dim.19 = bf16[4,8,256,128]{3,2,1,0:T(8,128)(2,1)} broadcast(bf16[8,256,128]{2,1,0:T(8,128)(2,1)S(1)} %bitcast.67), dimensions={1,2,3} | broadcast | bytes 2621440 | tf_op jit(solution)/shard_map/broadcast_in_dim | solution.py:29
  65.0 4.5 %all-to-all-start.1 = ((bf16[4,8,256,128]{3,2,1,0:T(8,128)(2,1)}), bf16[4,8,256,128]{3,2,1,0:T(8,128)(2,1)}, u32[]{:S(2)}, u32[]{:S(2)}) async-start(bf16[4,8,256,128]{3,2,1,0:T(8,128)(2,1)} %broadcast_in_dim.19), calls=%async_computation.1 | async-start | bytes 4194304 | tf_op jit(solution)/shard_map/all_to_all | solution.py:72
  71.6 1.3 fusion.31
  72.9 2.3 %collective-permute-done.7 = bf16[2,2,128,1024]{3,2,1,0:T(8,128)(2,1)} collective-permute-done((bf16[2,2,128,1024]{3,2,1,0:T(8,128)(2,1)S(1)}, bf16[2,2,128,1024]{3,2,1,0:T(8,128)(2,1)}, u32[]{:S(2)}, u32[]{:S(2)}) %collective-permute-start.7) | collective-permute-done | bytes 1048608 | tf_op jit(solution)/shard_map/ppermute | solution.py:54
  78.1 1.4 %broadcast_select_fusion = (bf16[1024,128]{1,0:T(8,128)(2,1)}, bf16[1024,128]{1,0:T(8,128)(2,1)S(1)}) fusion(pred[]{:T(512)S(6)} %and.22, bf16[1024,128]{1,0:T(8,128)(2,1)S(1)} %dynamic-slice_negate_fusion, bf16[1024,1024]{1,0:T(8,128)(2,1)S(1)} %get-tuple-element.15, bf16[1024,128]{1,0:T(8,128)(2,1)S(1)} %convolution_convert_fusion.4, pred[]{:T(512)S(6)} %lt.46), kind=kOutput, calls=%fused_computation.39 | convolution fusion | flops 268828672 | bytes 3145730 | tf_op jit(solution)/shard_map/dot_general | solution.py:12
  79.6 6.0 %all-gather = bf16[2048,128]{1,0:T(8,128)(2,1)S(1)} all-gather(bf16[1024,128]{1,0:T(8,128)(2,1)S(1)} %get-tuple-element.41), channel_id=2, replica_groups=mesh['y'=4,'core'=2,'x'=4,'z'=16] {'core'}, dimensions={0}, use_global_device_ids=true | all-gather | bytes 786432 | tf_op jit(solution)/shard_map/all_gather | solution.py:33
  86.6 4.8 %collective-permute-start.13 = (bf16[256,1024]{0,1:T(8,128)(2,1)S(1)}, bf16[256,1024]{0,1:T(8,128)(2,1)S(1)}, u32[]{:S(2)}, u32[]{:S(2)}) collective-permute-start(bf16[256,1024]{0,1:T(8,128)(2,1)S(1)} %bitcast.62), channel_id=1, source_target_pairs={{144,128},{160,144},{176,160},{128,176},{272,256},{288,272},{304,2... | collective-permute-start | bytes 1572872 | tf_op jit(solution)/shard_map/ppermute | solution.py:105
  91.4 1.9 %collective-permute-start.15 = (bf16[256,1024]{0,1:T(8,128)(2,1)S(1)}, bf16[256,1024]{0,1:T(8,128)(2,1)}, u32[]{:S(2)}, u32[]{:S(2)}) collective-permute-start(bf16[256,1024]{0,1:T(8,128)(2,1)S(1)} %bitcast.63), channel_id=1, source_target_pairs={{176,128},{128,144},{144,160},{160,176},{304,256},{256,272},{272,2... | collective-permute-start | bytes 1572872 | tf_op jit(solution)/shard_map/ppermute | solution.py:105
  93.4 1.8 %copy.8 = bf16[4,256,128,8]{2,1,0,3:T(8,128)(2,1)S(1)} copy(bf16[4,256,128,8]{2,1,3,0:T(8,128)(2,1)} %bitcast.3) | data formatting | bytes 4194304 | tf_op jit(solution)/shard_map/xzrk,zkn->xrn/dot_general | solution.py:91
  98.4 5.7 %all-gather.1 = bf16[2048,128]{1,0:T(8,128)(2,1)S(1)} all-gather(bf16[1024,128]{1,0:T(8,128)(2,1)S(1)} %fusion.17), channel_id=3, replica_groups=mesh['y'=4,'core'=2,'x'=4,'z'=16] {'core'}, dimensions={0}, use_global_device_ids=true | all-gather | bytes 786432 | tf_op jit(solution)/shard_map/all_gather | solution.py:33
  107.0 1.3 collective-permute-start.11
  110.2 5.6 %collective-permute-start.14 = (bf16[128,1024]{0,1:T(8,128)(2,1)S(1)}, bf16[128,1024]{0,1:T(8,128)(2,1)S(1)}, u32[]{:S(2)}, u32[]{:S(2)}) collective-permute-start(bf16[128,1024]{0,1:T(8,128)(2,1)S(1)} %slice.78), channel_id=1, source_target_pairs={{144,128},{160,144},{176,160},{128,176},{272,256},{288,272},{304,2... | collective-permute-start | bytes 786440 | tf_op jit(solution)/shard_map/ppermute | solution.py:105
  115.8 1.9 %collective-permute-start.16 = (bf16[128,1024]{0,1:T(8,128)(2,1)S(1)}, bf16[128,1024]{0,1:T(8,128)(2,1)S(1)}, u32[]{:S(2)}, u32[]{:S(2)}) collective-permute-start(bf16[128,1024]{0,1:T(8,128)(2,1)S(1)} %slice.79), channel_id=1, source_target_pairs={{176,128},{128,144},{144,160},{160,176},{304,256},{256,272},{272,2... | collective-permute-start | bytes 786440 | tf_op jit(solution)/shard_map/ppermute | solution.py:105
  117.7 7.9 %collective-permute-done.11 = bf16[1024,128]{1,0:T(8,128)(2,1)S(1)} collective-permute-done((bf16[1024,128]{1,0:T(8,128)(2,1)S(1)}, bf16[1024,128]{1,0:T(8,128)(2,1)S(1)}, u32[]{:S(2)}, u32[]{:S(2)}) %collective-permute-start.11) | collective-permute-done | bytes 262176 | tf_op jit(solution)/shard_map/ppermute | solution.py:22
  125.7 3.0 %all-gather.2 = bf16[2048,128]{1,0:T(8,128)(2,1)S(1)} all-gather(bf16[1024,128]{1,0:T(8,128)(2,1)S(1)} %select_select_fusion), channel_id=4, replica_groups=mesh['y'=4,'core'=2,'x'=4,'z'=16] {'core'}, dimensions={0}, use_global_device_ids=true | all-gather | bytes 786432 | tf_op jit(solution)/shard_map/all_gather | solution.py:33
  131.1 1.5 %fusion.19 = bf16[1024,128]{1,0:T(8,128)(2,1)} fusion(f32[1024,128]{1,0:T(8,128)S(1)} %convolution_bitcast_fusion, bf16[1792,1024]{0,1:T(8,128)(2,1)S(1)} %constant_dynamic-update-slice_fusion.7, s32[]{:T(128)S(6)} %select_n.185, bf16[1024,128]{1,0:T(8,128)(2,1)S(1)} %copy-done.10, bf16[1024,128]{1,0:T(8,128)(2,1)S(1)} %copy-done.12, ...), kind=kOutput, calls=%fused_computation.28 | convolution fusion | flops 269746176 | bytes 4456458 | tf_op jit(solution)/shard_map/dot_general | solution.py:12
  (93 shorter events, 20.6 us)
Async XLA Ops:
  0.9 7.3 %collective-permute-start = (bf16[256,128]{1,0:T(8,128)(2,1)S(1)}, bf16[256,128]{1,0:T(8,128)(2,1)S(1)}, u32[]{:S(2)}, u32[]{:S(2)}) collective-permute-start(bf16[256,128]{1,0:T(8,128)(2,1)S(1)} %get-tuple-element.39), channel_id=1, source_target_pairs={{0,32},{1,33},{2,34},{3,35},{4,36},{5,37},{6,38},{7,39},{8,40},{9,... | collective-permute-start | bytes 196616 | tf_op jit(solution)/shard_map/ppermute | solution.py:22
  5.6 3.0 %collective-permute-start.1 = (bf16[256,128]{1,0:T(8,128)(2,1)S(1)}, bf16[256,128]{1,0:T(8,128)(2,1)S(1)}, u32[]{:S(2)}, u32[]{:S(2)}) collective-permute-start(bf16[256,128]{1,0:T(8,128)(2,1)S(1)} %get-tuple-element.38), channel_id=1, source_target_pairs={{0,16},{1,17},{2,18},{3,19},{4,20},{5,21},{6,22},{7,23},{8,24},{9,... | collective-permute-start | bytes 196616 | tf_op jit(solution)/shard_map/ppermute | solution.py:22
  6.9 2.6 %collective-permute-start.2 = (bf16[256,128]{1,0:T(8,128)(2,1)S(1)}, bf16[256,128]{1,0:T(8,128)(2,1)S(1)}, u32[]{:S(2)}, u32[]{:S(2)}) collective-permute-start(bf16[256,128]{1,0:T(8,128)(2,1)S(1)} %get-tuple-element.37), channel_id=1, source_target_pairs={{0,48},{1,49},{2,50},{3,51},{4,52},{5,53},{6,54},{7,55},{8,56},{9,... | collective-permute-start | bytes 196616 | tf_op jit(solution)/shard_map/ppermute | solution.py:22
  11.1 28.0 %all-to-all-start = ((bf16[4,256,128]{2,1,0:T(8,128)(2,1)}), bf16[4,256,128]{2,1,0:T(8,128)(2,1)S(1)}, u32[]{:S(2)}, u32[]{:S(2)}) async-start(bf16[4,256,128]{2,1,0:T(8,128)(2,1)} %broadcast_in_dim.17), calls=%async_computation | async-start | bytes 524288 | tf_op jit(solution)/shard_map/all_to_all | solution.py:57
  27.2 5.2 %collective-permute-start.6 = (bf16[2,128,1024]{2,1,0:T(8,128)(2,1)S(1)}, bf16[2,128,1024]{2,1,0:T(8,128)(2,1)S(1)}, u32[]{:S(2)}, u32[]{:S(2)}) collective-permute-start(bf16[2,128,1024]{2,1,0:T(8,128)(2,1)S(1)} %get-tuple-element.34), channel_id=1, source_target_pairs={{0,64},{64,0},{1,65},{65,1},{2,66},{66,2},{3,67},{67,3},{4,68},{68... | collective-permute-start | bytes 1572872 | tf_op jit(solution)/shard_map/ppermute | solution.py:51
  32.6 37.8 %collective-permute-start.9 = (bf16[2,2,128,1024]{3,2,1,0:T(8,128)(2,1)S(1)}, bf16[2,2,128,1024]{3,2,1,0:T(8,128)(2,1)}, u32[]{:S(2)}, u32[]{:S(2)}) collective-permute-start(bf16[2,2,128,1024]{3,2,1,0:T(8,128)(2,1)S(1)} %maximum_select_fusion), channel_id=1, source_target_pairs={{384,0},{385,1},{386,2},{387,3},{388,4},{389,5},{390,6},{391,7},{3... | collective-permute-start | bytes 3145736 | tf_op jit(solution)/shard_map/ppermute | solution.py:54
  34.2 37.4 %collective-permute-start.8 = (bf16[2,2,128,1024]{3,2,1,0:T(8,128)(2,1)S(1)}, bf16[2,2,128,1024]{3,2,1,0:T(8,128)(2,1)}, u32[]{:S(2)}, u32[]{:S(2)}) collective-permute-start(bf16[2,2,128,1024]{3,2,1,0:T(8,128)(2,1)S(1)} %maximum_select_fusion), channel_id=1, source_target_pairs={{256,0},{257,1},{258,2},{259,3},{260,4},{261,5},{262,6},{263,7},{2... | collective-permute-start | bytes 3145736 | tf_op jit(solution)/shard_map/ppermute | solution.py:54
  39.1 14.9 %collective-permute-start.3 = (bf16[4,256,128]{2,1,0:T(8,128)(2,1)S(1)}, bf16[4,256,128]{2,1,0:T(8,128)(2,1)S(1)}, u32[]{:S(2)}, u32[]{:S(2)}) collective-permute-start(bf16[4,256,128]{2,1,0:T(8,128)(2,1)S(1)} %all-to-all-done), channel_id=1, source_target_pairs={{1,0},{2,1},{3,2},{4,3},{5,4},{6,5},{7,6},{8,7},{9,8},{10,9},{11,1... | collective-permute-start | bytes 786440 | tf_op jit(solution)/shard_map/ppermute | solution.py:60
  43.9 14.8 %collective-permute-start.4 = (bf16[4,256,128]{2,1,0:T(8,128)(2,1)S(1)}, bf16[4,256,128]{2,1,0:T(8,128)(2,1)S(1)}, u32[]{:S(2)}, u32[]{:S(2)}) collective-permute-start(bf16[4,256,128]{2,1,0:T(8,128)(2,1)S(1)} %all-to-all-done), channel_id=1, source_target_pairs={{2,0},{15,1},{4,2},{1,3},{6,4},{3,5},{8,6},{5,7},{10,8},{7,9},{12,... | collective-permute-start | bytes 786440 | tf_op jit(solution)/shard_map/ppermute | solution.py:63
  51.0 11.8 %collective-permute-start.5 = (bf16[4,256,128]{2,1,0:T(8,128)(2,1)S(1)}, bf16[4,256,128]{2,1,0:T(8,128)(2,1)S(1)}, u32[]{:S(2)}, u32[]{:S(2)}) collective-permute-start(bf16[4,256,128]{2,1,0:T(8,128)(2,1)S(1)} %all-to-all-done), channel_id=1, source_target_pairs={{15,0},{0,1},{1,2},{2,3},{3,4},{4,5},{5,6},{6,7},{7,8},{8,9},{9,10... | collective-permute-start | bytes 786440 | tf_op jit(solution)/shard_map/ppermute | solution.py:60
  53.9 21.2 %collective-permute-start.7 = (bf16[2,2,128,1024]{3,2,1,0:T(8,128)(2,1)S(1)}, bf16[2,2,128,1024]{3,2,1,0:T(8,128)(2,1)}, u32[]{:S(2)}, u32[]{:S(2)}) collective-permute-start(bf16[2,2,128,1024]{3,2,1,0:T(8,128)(2,1)S(1)} %maximum_select_fusion), channel_id=1, source_target_pairs={{128,0},{129,1},{130,2},{131,3},{132,4},{133,5},{134,6},{135,7},{1... | collective-permute-start | bytes 3145736 | tf_op jit(solution)/shard_map/ppermute | solution.py:54
  65.0 28.4 %all-to-all-start.1 = ((bf16[4,8,256,128]{3,2,1,0:T(8,128)(2,1)}), bf16[4,8,256,128]{3,2,1,0:T(8,128)(2,1)}, u32[]{:S(2)}, u32[]{:S(2)}) async-start(bf16[4,8,256,128]{3,2,1,0:T(8,128)(2,1)} %broadcast_in_dim.19), calls=%async_computation.1 | async-start | bytes 4194304 | tf_op jit(solution)/shard_map/all_to_all | solution.py:72
  77.1 2.5 %copy-start.2 = (bf16[1024,1024]{1,0:T(8,128)(2,1)}, bf16[1024,1024]{1,0:T(8,128)(2,1)S(1)}, u32[]{:S(2)}) copy-start(bf16[1024,1024]{1,0:T(8,128)(2,1)S(1)} %get-tuple-element.15) | copy-start | bytes 6291460
  77.3 2.3 %copy-start.13 = (bf16[1024,128]{1,0:T(8,128)(2,1)}, bf16[1024,128]{1,0:T(8,128)(2,1)S(1)}, u32[]{:S(2)}) copy-start(bf16[1024,128]{1,0:T(8,128)(2,1)S(1)} %dynamic-slice_negate_fusion) | copy-start | bytes 786436
  78.1 1.5 %copy-start.7 = (bf16[1024,128]{1,0:T(8,128)(2,1)}, bf16[1024,128]{1,0:T(8,128)(2,1)S(1)}, u32[]{:S(2)}) copy-start(bf16[1024,128]{1,0:T(8,128)(2,1)S(1)} %convolution_convert_fusion.4) | copy-start | bytes 786436
  78.1 8.3 %copy-start.4 = (bf16[2,4,256,128]{3,2,1,0:T(8,128)(2,1)S(1)}, bf16[2,4,256,128]{3,2,1,0:T(8,128)(2,1)}, u32[]{:S(2)}) copy-start(bf16[2,4,256,128]{3,2,1,0:T(8,128)(2,1)} %copy.9) | copy-start | bytes 1572868
  86.6 22.5 %collective-permute-start.13 = (bf16[256,1024]{0,1:T(8,128)(2,1)S(1)}, bf16[256,1024]{0,1:T(8,128)(2,1)S(1)}, u32[]{:S(2)}, u32[]{:S(2)}) collective-permute-start(bf16[256,1024]{0,1:T(8,128)(2,1)S(1)} %bitcast.62), channel_id=1, source_target_pairs={{144,128},{160,144},{176,160},{128,176},{272,256},{288,272},{304,2... | collective-permute-start | bytes 1572872 | tf_op jit(solution)/shard_map/ppermute | solution.py:105
  91.4 17.7 %collective-permute-start.15 = (bf16[256,1024]{0,1:T(8,128)(2,1)S(1)}, bf16[256,1024]{0,1:T(8,128)(2,1)}, u32[]{:S(2)}, u32[]{:S(2)}) collective-permute-start(bf16[256,1024]{0,1:T(8,128)(2,1)S(1)} %bitcast.63), channel_id=1, source_target_pairs={{176,128},{128,144},{144,160},{160,176},{304,256},{256,272},{272,2... | collective-permute-start | bytes 1572872 | tf_op jit(solution)/shard_map/ppermute | solution.py:105
  93.4 1.8 %slice-start = ((bf16[2048,128]{1,0:T(8,128)(2,1)}), bf16[1024,128]{1,0:T(8,128)(2,1)S(1)}, s32[]{:S(2)}) async-start(bf16[2048,128]{1,0:T(8,128)(2,1)} %copy-done.5), calls=%async_computation.2 | async-start | bytes 524288 | tf_op jit(solution)/shard_map/slice | solution.py:86
  95.2 9.0 %copy-start = (bf16[4,256,128,8]{2,1,0,3:T(8,128)(2,1)}, bf16[4,256,128,8]{2,1,0,3:T(8,128)(2,1)S(1)}, u32[]{:S(2)}) copy-start(bf16[4,256,128,8]{2,1,0,3:T(8,128)(2,1)S(1)} %copy.8) | copy-start | bytes 6291460
  95.2 2.4 %copy-start.3 = (bf16[1024,1024]{1,0:T(8,128)(2,1)S(1)}, bf16[1024,1024]{1,0:T(8,128)(2,1)}, u32[]{:S(2)}) copy-start(bf16[1024,1024]{1,0:T(8,128)(2,1)} %copy-done.2) | copy-start | bytes 6291460
  95.2 2.5 %copy-start.14 = (bf16[1024,128]{1,0:T(8,128)(2,1)S(1)}, bf16[1024,128]{1,0:T(8,128)(2,1)}, u32[]{:S(2)}) copy-start(bf16[1024,128]{1,0:T(8,128)(2,1)} %copy-done.13) | copy-start | bytes 786436
  104.2 1.4 %copy-start.15 = (bf16[1024,128]{1,0:T(8,128)(2,1)S(1)}, bf16[1024,128]{1,0:T(8,128)(2,1)}, u32[]{:S(2)}) copy-start(bf16[1024,128]{1,0:T(8,128)(2,1)} %get-tuple-element.40) | copy-start | bytes 786436
  106.3 11.4 %collective-permute-start.10 = (bf16[1024,128]{1,0:T(8,128)(2,1)S(1)}, bf16[1024,128]{1,0:T(8,128)(2,1)S(1)}, u32[]{:S(2)}, u32[]{:S(2)}) collective-permute-start(bf16[1024,128]{1,0:T(8,128)(2,1)S(1)} %fusion.18), channel_id=1, source_target_pairs={{0,256},{1,257},{2,258},{3,259},{4,260},{5,261},{6,262},{7,263},{8... | collective-permute-start | bytes 786440 | tf_op jit(solution)/shard_map/ppermute | solution.py:22
  107.0 18.6 %collective-permute-start.11 = (bf16[1024,128]{1,0:T(8,128)(2,1)S(1)}, bf16[1024,128]{1,0:T(8,128)(2,1)S(1)}, u32[]{:S(2)}, u32[]{:S(2)}) collective-permute-start(bf16[1024,128]{1,0:T(8,128)(2,1)S(1)} %fusion.18), channel_id=1, source_target_pairs={{0,128},{1,129},{2,130},{3,131},{4,132},{5,133},{6,134},{7,135},{8... | collective-permute-start | bytes 786440 | tf_op jit(solution)/shard_map/ppermute | solution.py:22
  108.3 17.3 %collective-permute-start.12 = (bf16[1024,128]{1,0:T(8,128)(2,1)S(1)}, bf16[1024,128]{1,0:T(8,128)(2,1)S(1)}, u32[]{:S(2)}, u32[]{:S(2)}) collective-permute-start(bf16[1024,128]{1,0:T(8,128)(2,1)S(1)} %fusion.18), channel_id=1, source_target_pairs={{0,384},{1,385},{2,386},{3,387},{4,388},{5,389},{6,390},{7,391},{8... | collective-permute-start | bytes 786440 | tf_op jit(solution)/shard_map/ppermute | solution.py:22
  110.1 18.7 %copy-start.1 = (bf16[4,256,128,8]{2,1,0,3:T(8,128)(2,1)S(1)}, bf16[4,256,128,8]{2,1,0,3:T(8,128)(2,1)}, u32[]{:S(2)}) copy-start(bf16[4,256,128,8]{2,1,0,3:T(8,128)(2,1)} %copy-done) | copy-start | bytes 6291460
  110.2 18.6 %collective-permute-start.14 = (bf16[128,1024]{0,1:T(8,128)(2,1)S(1)}, bf16[128,1024]{0,1:T(8,128)(2,1)S(1)}, u32[]{:S(2)}, u32[]{:S(2)}) collective-permute-start(bf16[128,1024]{0,1:T(8,128)(2,1)S(1)} %slice.78), channel_id=1, source_target_pairs={{144,128},{160,144},{176,160},{128,176},{272,256},{288,272},{304,2... | collective-permute-start | bytes 786440 | tf_op jit(solution)/shard_map/ppermute | solution.py:105
  115.8 13.8 %collective-permute-start.16 = (bf16[128,1024]{0,1:T(8,128)(2,1)S(1)}, bf16[128,1024]{0,1:T(8,128)(2,1)S(1)}, u32[]{:S(2)}, u32[]{:S(2)}) collective-permute-start(bf16[128,1024]{0,1:T(8,128)(2,1)S(1)} %slice.79), channel_id=1, source_target_pairs={{176,128},{128,144},{144,160},{160,176},{304,256},{256,272},{272,2... | collective-permute-start | bytes 786440 | tf_op jit(solution)/shard_map/ppermute | solution.py:105
  129.7 1.4 %copy-start.8 = (bf16[1024,128]{1,0:T(8,128)(2,1)S(1)}, bf16[1024,128]{1,0:T(8,128)(2,1)}, u32[]{:S(2)}) copy-start(bf16[1024,128]{1,0:T(8,128)(2,1)} %copy-done.7) | copy-start | bytes 786436
  129.7 1.4 %copy-start.10 = (bf16[1024,128]{1,0:T(8,128)(2,1)S(1)}, bf16[1024,128]{1,0:T(8,128)(2,1)}, u32[]{:S(2)}) copy-start(bf16[1024,128]{1,0:T(8,128)(2,1)} %copy-done.9) | copy-start | bytes 786436
  129.7 1.4 %copy-start.12 = (bf16[1024,128]{1,0:T(8,128)(2,1)S(1)}, bf16[1024,128]{1,0:T(8,128)(2,1)}, u32[]{:S(2)}) copy-start(bf16[1024,128]{1,0:T(8,128)(2,1)} %copy-done.11) | copy-start | bytes 786436
  (4 other events, 3.2 us)

commit v8 on v7

--- a/solution.py
+++ b/solution.py
@@ -61,8 +61,8 @@
 
     plus, minus = from_z(own, 1), from_z(own, -1)
     two = lax.ppermute(own, "z", [((k + 2 - 4 * (k % 2)) % 16, k) for k in range(16)])
-    along = jnp.concatenate([own, plus, two, minus, own, plus, two])
-    along = lax.dynamic_slice_in_dim(along, (4 - z % 4) % 4 * 4, 16, 0).reshape(4, 4, 256, 128)
+    along = jnp.concatenate([two, minus, own, plus, two, minus, own])
+    along = lax.dynamic_slice_in_dim(along, (6 - z % 4) % 4 * 4, 16, 0).reshape(4, 4, 256, 128)
 
     def half(which):
         blocks = lax.dynamic_slice_in_dim(along, 2 * which, 2, 1)
@@ -109,9 +109,7 @@
     two = jnp.concatenate([late, ahead, across, behind, late, ahead, across])
     two = lax.dynamic_slice_in_dim(two, (4 - x) % 4 * 256, NB, 0)
     right = from_first([right] * 4, "y")
-    d, c1 = lax.optimization_barrier(tuple(cores(right)))
-    changed = product(one, jnp.where(core == 1, d, c1))
-    changed += dot(two, jnp.where(core == 1, c1, d))
+    changed = dot(two, right) + product(one, lax.ppermute(right, "core", [(0, 1), (1, 0)]))
     trail = (jnp.where(j >= 16, a, zeros).astype(F32) - changed).astype(BF)
     row0 = jnp.where(in0, a, r)
     row1 = jnp.where(j < 16, w, r1)

time: 134 us -> 134 us (level)
  the two profiles are of different devices: /device:TPU:9 before, /device:TPU:43 now
where the time goes in v8:
time: 134 us; the launch traced here: 133 us
  starting transfers between devices  52.7 us (39%)
  waiting for transfers between devices  34.1 us (25%)
  blocking collectives  17.9 us (13%)
  local copies, waits for them, and re-layouts  15.6 us (12%)
  matrix products  8.59 us (6%)
  other arithmetic  3.13 us (2%)
    all_gather x2, blocking collectives, cores(): return lax.all_gather(value, 'core', axis=0)  17.9 us
    all_to_all x1, starting transfers between devices, shards(): own = lax.all_to_all(copies(share, 4), 'z', 0, 0, axis_index_groups=fours)  13.9 us
    ppermute x6, waiting for transfers between devices, from_first(): got = {k: lax.ppermute(values[k], axis, [(0, k)]) for k in (3, 1, 2)}  13.6 us
    ppermute x4, starting transfers between devices, from_x(): return lax.ppermute(value, ('y', 'x'), planes)  10.6 us
    all_to_all x1, waiting for transfers between devices, shards(): own = lax.all_to_all(copies(share, 4), 'z', 0, 0, axis_index_groups=fours)  7.75 us
    dot_general x7, matrix products, dot(): return jnp.dot(a, b, preferred_element_type=F32)  6.45 us
    ppermute x2, waiting for transfers between devices, from_z(): lax.ppermute(value, 'z', [((k + distance) % 16, k) for k in range(16)])  6.38 us
    ppermute x3, starting transfers between devices, shards(): parts = [pair] + [lax.ppermute(pair, 'y', [(k, 0)]) for k in range(1, 4)]  5.66 us
  transfers between devices with their start and end apart: 20, of which 6 were waited for; matrix products, arithmetic and copies ran while one was open for 15% of the time, Pallas kernels for 0%

profile of v8, /device:TPU:43, one launch (start us, length us, event | category | flops | bytes accessed | tf_op | source)
XLA Modules:
  0.0 132.8 jit_solution(12753681401312804896)
XLA Ops:
  1.6 1.3 collective-permute-start.1
  3.6 6.1 %collective-permute-done.1 = bf16[256,128]{1,0:T(8,128)(2,1)S(1)} collective-permute-done((bf16[256,128]{1,0:T(8,128)(2,1)S(1)}, bf16[256,128]{1,0:T(8,128)(2,1)S(1)}, u32[]{:S(2)}, u32[]{:S(2)}) %collective-permute-start.1) | collective-permute-done | bytes 65568 | tf_op jit(solution)/shard_map/ppermute | solution.py:22
  11.3 13.9 %all-to-all-start = ((bf16[4,256,128]{2,1,0:T(8,128)(2,1)}), bf16[4,256,128]{2,1,0:T(8,128)(2,1)S(1)}, u32[]{:S(2)}, u32[]{:S(2)}) async-start(bf16[4,256,128]{2,1,0:T(8,128)(2,1)} %broadcast_in_dim.17), calls=%async_computation | async-start | bytes 524288 | tf_op jit(solution)/shard_map/all_to_all | solution.py:57
  25.2 1.3 fusion.25
  26.5 3.2 %collective-permute-start.6 = (bf16[2,128,1024]{2,1,0:T(8,128)(2,1)S(1)}, bf16[2,128,1024]{2,1,0:T(8,128)(2,1)S(1)}, u32[]{:S(2)}, u32[]{:S(2)}) collective-permute-start(bf16[2,128,1024]{2,1,0:T(8,128)(2,1)S(1)} %get-tuple-element.30), channel_id=1, source_target_pairs={{0,64},{64,0},{1,65},{65,1},{2,66},{66,2},{3,67},{67,3},{4,68},{68... | collective-permute-start | bytes 1572872 | tf_op jit(solution)/shard_map/ppermute | solution.py:51
  29.7 1.5 %collective-permute-done.6 = bf16[2,128,1024]{2,1,0:T(8,128)(2,1)S(1)} collective-permute-done((bf16[2,128,1024]{2,1,0:T(8,128)(2,1)S(1)}, bf16[2,128,1024]{2,1,0:T(8,128)(2,1)S(1)}, u32[]{:S(2)}, u32[]{:S(2)}) %collective-permute-start.6) | collective-permute-done | bytes 524320 | tf_op jit(solution)/shard_map/ppermute | solution.py:51
  31.3 1.7 %collective-permute-start.9 = (bf16[2,2,128,1024]{3,2,1,0:T(8,128)(2,1)S(1)}, bf16[2,2,128,1024]{3,2,1,0:T(8,128)(2,1)}, u32[]{:S(2)}, u32[]{:S(2)}) collective-permute-start(bf16[2,2,128,1024]{3,2,1,0:T(8,128)(2,1)S(1)} %maximum_select_fusion), channel_id=1, source_target_pairs={{384,0},{385,1},{386,2},{387,3},{388,4},{389,5},{390,6},{391,7},{3... | collective-permute-start | bytes 3145736 | tf_op jit(solution)/shard_map/ppermute | solution.py:54
  33.0 1.6 %collective-permute-start.8 = (bf16[2,2,128,1024]{3,2,1,0:T(8,128)(2,1)S(1)}, bf16[2,2,128,1024]{3,2,1,0:T(8,128)(2,1)}, u32[]{:S(2)}, u32[]{:S(2)}) collective-permute-start(bf16[2,2,128,1024]{3,2,1,0:T(8,128)(2,1)S(1)} %maximum_select_fusion), channel_id=1, source_target_pairs={{256,0},{257,1},{258,2},{259,3},{260,4},{261,5},{262,6},{263,7},{2... | collective-permute-start | bytes 3145736 | tf_op jit(solution)/shard_map/ppermute | solution.py:54
  34.6 2.4 %collective-permute-start.7 = (bf16[2,2,128,1024]{3,2,1,0:T(8,128)(2,1)S(1)}, bf16[2,2,128,1024]{3,2,1,0:T(8,128)(2,1)}, u32[]{:S(2)}, u32[]{:S(2)}) collective-permute-start(bf16[2,2,128,1024]{3,2,1,0:T(8,128)(2,1)S(1)} %maximum_select_fusion), channel_id=1, source_target_pairs={{128,0},{129,1},{130,2},{131,3},{132,4},{133,5},{134,6},{135,7},{1... | collective-permute-start | bytes 3145736 | tf_op jit(solution)/shard_map/ppermute | solution.py:54
  37.0 7.7 %all-to-all-done = bf16[4,256,128]{2,1,0:T(8,128)(2,1)S(1)} async-done(((bf16[4,256,128]{2,1,0:T(8,128)(2,1)}), bf16[4,256,128]{2,1,0:T(8,128)(2,1)S(1)}, u32[]{:S(2)}, u32[]{:S(2)}) %all-to-all-start) | async-done | bytes 262176 | tf_op jit(solution)/shard_map/all_to_all | solution.py:57
  44.7 1.9 %collective-permute-start.3 = (bf16[4,256,128]{2,1,0:T(8,128)(2,1)S(1)}, bf16[4,256,128]{2,1,0:T(8,128)(2,1)S(1)}, u32[]{:S(2)}, u32[]{:S(2)}) collective-permute-start(bf16[4,256,128]{2,1,0:T(8,128)(2,1)S(1)} %all-to-all-done), channel_id=1, source_target_pairs={{2,0},{15,1},{4,2},{1,3},{6,4},{3,5},{8,6},{5,7},{10,8},{7,9},{12,... | collective-permute-start | bytes 786440 | tf_op jit(solution)/shard_map/ppermute | solution.py:63
  46.7 2.6 %collective-permute-start.4 = (bf16[4,256,128]{2,1,0:T(8,128)(2,1)S(1)}, bf16[4,256,128]{2,1,0:T(8,128)(2,1)S(1)}, u32[]{:S(2)}, u32[]{:S(2)}) collective-permute-start(bf16[4,256,128]{2,1,0:T(8,128)(2,1)S(1)} %all-to-all-done), channel_id=1, source_target_pairs={{15,0},{0,1},{1,2},{2,3},{3,4},{4,5},{5,6},{6,7},{7,8},{8,9},{9,10... | collective-permute-start | bytes 786440 | tf_op jit(solution)/shard_map/ppermute | solution.py:60
  49.4 4.9 %collective-permute-done.3 = bf16[4,256,128]{2,1,0:T(8,128)(2,1)S(1)} collective-permute-done((bf16[4,256,128]{2,1,0:T(8,128)(2,1)S(1)}, bf16[4,256,128]{2,1,0:T(8,128)(2,1)S(1)}, u32[]{:S(2)}, u32[]{:S(2)}) %collective-permute-start.3) | collective-permute-done | bytes 262176 | tf_op jit(solution)/shard_map/ppermute | solution.py:63
  54.3 1.9 %collective-permute-start.5 = (bf16[4,256,128]{2,1,0:T(8,128)(2,1)S(1)}, bf16[4,256,128]{2,1,0:T(8,128)(2,1)S(1)}, u32[]{:S(2)}, u32[]{:S(2)}) collective-permute-start(bf16[4,256,128]{2,1,0:T(8,128)(2,1)S(1)} %all-to-all-done), channel_id=1, source_target_pairs={{1,0},{2,1},{3,2},{4,3},{5,4},{6,5},{7,6},{8,7},{9,8},{10,9},{11,1... | collective-permute-start | bytes 786440 | tf_op jit(solution)/shard_map/ppermute | solution.py:60
  56.2 6.4 %collective-permute-done.4 = bf16[4,256,128]{2,1,0:T(8,128)(2,1)S(1)} collective-permute-done((bf16[4,256,128]{2,1,0:T(8,128)(2,1)S(1)}, bf16[4,256,128]{2,1,0:T(8,128)(2,1)S(1)}, u32[]{:S(2)}, u32[]{:S(2)}) %collective-permute-start.4) | collective-permute-done | bytes 262176 | tf_op jit(solution)/shard_map/ppermute | solution.py:60
  63.1 1.8 %broadcast_in_dim.19 = bf16[4,8,256,128]{3,2,1,0:T(8,128)(2,1)} broadcast(bf16[8,256,128]{2,1,0:T(8,128)(2,1)S(1)} %bitcast.68), dimensions={1,2,3} | broadcast | bytes 2621440 | tf_op jit(solution)/shard_map/broadcast_in_dim | solution.py:29
  64.9 4.5 %all-to-all-start.1 = ((bf16[4,8,256,128]{3,2,1,0:T(8,128)(2,1)}), bf16[4,8,256,128]{3,2,1,0:T(8,128)(2,1)}, u32[]{:S(2)}, u32[]{:S(2)}) async-start(bf16[4,8,256,128]{3,2,1,0:T(8,128)(2,1)} %broadcast_in_dim.19), calls=%async_computation.1 | async-start | bytes 4194304 | tf_op jit(solution)/shard_map/all_to_all | solution.py:72
  70.3 1.3 fusion.30
  71.6 1.3 fusion.29
  72.9 1.3 fusion.28
  75.8 1.4 %broadcast_select_fusion = (bf16[1024,128]{1,0:T(8,128)(2,1)}, bf16[1024,128]{1,0:T(8,128)(2,1)S(1)}) fusion(pred[]{:T(512)S(6)} %and.22, bf16[1024,128]{1,0:T(8,128)(2,1)S(1)} %dynamic-slice_negate_fusion, bf16[1024,1024]{1,0:T(8,128)(2,1)S(1)} %get-tuple-element.13, bf16[1024,128]{1,0:T(8,128)(2,1)S(1)} %convolution_convert_fusion.4, pred[]{:T(512)S(6)} %lt.45), kind=kOutput, calls=%fused_computation.38 | convolution fusion | flops 268828672 | bytes 3145730 | tf_op jit(solution)/shard_map/dot_general | solution.py:12
  77.3 7.7 %all-gather = bf16[2048,128]{1,0:T(8,128)(2,1)S(1)} all-gather(bf16[1024,128]{1,0:T(8,128)(2,1)S(1)} %get-tuple-element.35), channel_id=2, replica_groups=mesh['y'=4,'core'=2,'x'=4,'z'=16] {'core'}, dimensions={0}, use_global_device_ids=true | all-gather | bytes 786432 | tf_op jit(solution)/shard_map/all_gather | solution.py:33
  86.0 1.9 %collective-permute-start.10 = (bf16[256,1024]{0,1:T(8,128)(2,1)S(1)}, bf16[256,1024]{0,1:T(8,128)(2,1)S(1)}, u32[]{:S(2)}, u32[]{:S(2)}) collective-permute-start(bf16[256,1024]{0,1:T(8,128)(2,1)S(1)} %bitcast.63), channel_id=1, source_target_pairs={{144,128},{160,144},{176,160},{128,176},{272,256},{288,272},{304,2... | collective-permute-start | bytes 1572872 | tf_op jit(solution)/shard_map/ppermute | solution.py:105
  88.0 3.4 %collective-permute-start.12 = (bf16[256,1024]{0,1:T(8,128)(2,1)S(1)}, bf16[256,1024]{0,1:T(8,128)(2,1)}, u32[]{:S(2)}, u32[]{:S(2)}) collective-permute-start(bf16[256,1024]{0,1:T(8,128)(2,1)S(1)} %bitcast.64), channel_id=1, source_target_pairs={{176,128},{128,144},{144,160},{160,176},{304,256},{256,272},{272,2... | collective-permute-start | bytes 1572872 | tf_op jit(solution)/shard_map/ppermute | solution.py:105
  91.4 1.8 %copy.10 = bf16[4,256,128,8]{2,1,0,3:T(8,128)(2,1)S(1)} copy(bf16[4,256,128,8]{2,1,3,0:T(8,128)(2,1)} %bitcast.20) | data formatting | bytes 4194304 | tf_op jit(solution)/shard_map/xzrk,zkn->xrn/dot_general | solution.py:91
  96.4 10.2 %all-gather.1 = bf16[2048,128]{1,0:T(8,128)(2,1)S(1)} all-gather(bf16[1024,128]{1,0:T(8,128)(2,1)S(1)} %fusion.17), channel_id=3, replica_groups=mesh['y'=4,'core'=2,'x'=4,'z'=16] {'core'}, dimensions={0}, use_global_device_ids=true | all-gather | bytes 786432 | tf_op jit(solution)/shard_map/all_gather | solution.py:33
  109.4 1.3 collective-permute-start.15
  111.5 1.9 %collective-permute-start.11 = (bf16[128,1024]{0,1:T(8,128)(2,1)S(1)}, bf16[128,1024]{0,1:T(8,128)(2,1)S(1)}, u32[]{:S(2)}, u32[]{:S(2)}) collective-permute-start(bf16[128,1024]{0,1:T(8,128)(2,1)S(1)} %slice.73), channel_id=1, source_target_pairs={{144,128},{160,144},{176,160},{128,176},{272,256},{288,272},{304,2... | collective-permute-start | bytes 786440 | tf_op jit(solution)/shard_map/ppermute | solution.py:105
  114.5 3.4 %collective-permute-start.13 = (bf16[128,1024]{0,1:T(8,128)(2,1)S(1)}, bf16[128,1024]{0,1:T(8,128)(2,1)S(1)}, u32[]{:S(2)}, u32[]{:S(2)}) collective-permute-start(bf16[128,1024]{0,1:T(8,128)(2,1)S(1)} %slice.75), channel_id=1, source_target_pairs={{176,128},{128,144},{144,160},{160,176},{304,256},{256,272},{272,2... | collective-permute-start | bytes 786440 | tf_op jit(solution)/shard_map/ppermute | solution.py:105
  117.9 7.5 %collective-permute-done.15 = bf16[1024,128]{1,0:T(8,128)(2,1)S(1)} collective-permute-done((bf16[1024,128]{1,0:T(8,128)(2,1)S(1)}, bf16[1024,128]{1,0:T(8,128)(2,1)S(1)}, u32[]{:S(2)}, u32[]{:S(2)}) %collective-permute-start.15) | collective-permute-done | bytes 262176 | tf_op jit(solution)/shard_map/ppermute | solution.py:22
  125.5 3.1 %collective-permute-start.17 = (bf16[1024,128]{1,0:T(8,128)(2,1)S(1)}, bf16[1024,128]{1,0:T(8,128)(2,1)S(1)}, u32[]{:S(2)}, u32[]{:S(2)}) collective-permute-start(bf16[1024,128]{1,0:T(8,128)(2,1)S(1)} %select_select_fusion), channel_id=1, source_target_pairs={{0,64},{64,0},{1,65},{65,1},{2,66},{66,2},{3,67},{67,3},{4,68},{68... | collective-permute-start | bytes 786440 | tf_op jit(solution)/shard_map/ppermute | solution.py:112
  131.3 1.5 %fusion.19 = bf16[1024,128]{1,0:T(8,128)(2,1)} fusion(f32[1024,128]{1,0:T(8,128)S(1)} %convolution_bitcast_fusion, bf16[1024,128]{1,0:T(8,128)(2,1)S(1)} %select_select_fusion, bf16[1792,1024]{0,1:T(8,128)(2,1)S(1)} %constant_dynamic-update-slice_fusion.7, s32[]{:T(128)S(6)} %select_n.167, bf16[1024,128]{1,0:T(8,128)(2,1)S(1)} %copy-done.10, ...), kind=kOutput, calls=%fused_computation.28 | convolution fusion | flops 269615104 | bytes 4194313 | tf_op jit(solution)/shard_map/dot_general | solution.py:12
  (92 shorter events, 18.5 us)
Async XLA Ops:
  0.9 2.7 %collective-permute-start = (bf16[256,128]{1,0:T(8,128)(2,1)S(1)}, bf16[256,128]{1,0:T(8,128)(2,1)S(1)}, u32[]{:S(2)}, u32[]{:S(2)}) collective-permute-start(bf16[256,128]{1,0:T(8,128)(2,1)S(1)} %get-tuple-element.33), channel_id=1, source_target_pairs={{0,32},{1,33},{2,34},{3,35},{4,36},{5,37},{6,38},{7,39},{8,40},{9,... | collective-permute-start | bytes 196616 | tf_op jit(solution)/shard_map/ppermute | solution.py:22
  1.6 8.1 %collective-permute-start.1 = (bf16[256,128]{1,0:T(8,128)(2,1)S(1)}, bf16[256,128]{1,0:T(8,128)(2,1)S(1)}, u32[]{:S(2)}, u32[]{:S(2)}) collective-permute-start(bf16[256,128]{1,0:T(8,128)(2,1)S(1)} %get-tuple-element.32), channel_id=1, source_target_pairs={{0,16},{1,17},{2,18},{3,19},{4,20},{5,21},{6,22},{7,23},{8,24},{9,... | collective-permute-start | bytes 196616 | tf_op jit(solution)/shard_map/ppermute | solution.py:22
  2.9 6.8 %collective-permute-start.2 = (bf16[256,128]{1,0:T(8,128)(2,1)S(1)}, bf16[256,128]{1,0:T(8,128)(2,1)S(1)}, u32[]{:S(2)}, u32[]{:S(2)}) collective-permute-start(bf16[256,128]{1,0:T(8,128)(2,1)S(1)} %get-tuple-element.31), channel_id=1, source_target_pairs={{0,48},{1,49},{2,50},{3,51},{4,52},{5,53},{6,54},{7,55},{8,56},{9,... | collective-permute-start | bytes 196616 | tf_op jit(solution)/shard_map/ppermute | solution.py:22
  11.3 33.5 %all-to-all-start = ((bf16[4,256,128]{2,1,0:T(8,128)(2,1)}), bf16[4,256,128]{2,1,0:T(8,128)(2,1)S(1)}, u32[]{:S(2)}, u32[]{:S(2)}) async-start(bf16[4,256,128]{2,1,0:T(8,128)(2,1)} %broadcast_in_dim.17), calls=%async_computation | async-start | bytes 524288 | tf_op jit(solution)/shard_map/all_to_all | solution.py:57
  26.5 4.7 %collective-permute-start.6 = (bf16[2,128,1024]{2,1,0:T(8,128)(2,1)S(1)}, bf16[2,128,1024]{2,1,0:T(8,128)(2,1)S(1)}, u32[]{:S(2)}, u32[]{:S(2)}) collective-permute-start(bf16[2,128,1024]{2,1,0:T(8,128)(2,1)S(1)} %get-tuple-element.30), channel_id=1, source_target_pairs={{0,64},{64,0},{1,65},{65,1},{2,66},{66,2},{3,67},{67,3},{4,68},{68... | collective-permute-start | bytes 1572872 | tf_op jit(solution)/shard_map/ppermute | solution.py:51
  31.3 39.0 %collective-permute-start.9 = (bf16[2,2,128,1024]{3,2,1,0:T(8,128)(2,1)S(1)}, bf16[2,2,128,1024]{3,2,1,0:T(8,128)(2,1)}, u32[]{:S(2)}, u32[]{:S(2)}) collective-permute-start(bf16[2,2,128,1024]{3,2,1,0:T(8,128)(2,1)S(1)} %maximum_select_fusion), channel_id=1, source_target_pairs={{384,0},{385,1},{386,2},{387,3},{388,4},{389,5},{390,6},{391,7},{3... | collective-permute-start | bytes 3145736 | tf_op jit(solution)/shard_map/ppermute | solution.py:54
  33.0 38.6 %collective-permute-start.8 = (bf16[2,2,128,1024]{3,2,1,0:T(8,128)(2,1)S(1)}, bf16[2,2,128,1024]{3,2,1,0:T(8,128)(2,1)}, u32[]{:S(2)}, u32[]{:S(2)}) collective-permute-start(bf16[2,2,128,1024]{3,2,1,0:T(8,128)(2,1)S(1)} %maximum_select_fusion), channel_id=1, source_target_pairs={{256,0},{257,1},{258,2},{259,3},{260,4},{261,5},{262,6},{263,7},{2... | collective-permute-start | bytes 3145736 | tf_op jit(solution)/shard_map/ppermute | solution.py:54
  34.6 38.2 %collective-permute-start.7 = (bf16[2,2,128,1024]{3,2,1,0:T(8,128)(2,1)S(1)}, bf16[2,2,128,1024]{3,2,1,0:T(8,128)(2,1)}, u32[]{:S(2)}, u32[]{:S(2)}) collective-permute-start(bf16[2,2,128,1024]{3,2,1,0:T(8,128)(2,1)S(1)} %maximum_select_fusion), channel_id=1, source_target_pairs={{128,0},{129,1},{130,2},{131,3},{132,4},{133,5},{134,6},{135,7},{1... | collective-permute-start | bytes 3145736 | tf_op jit(solution)/shard_map/ppermute | solution.py:54
  44.7 9.5 %collective-permute-start.3 = (bf16[4,256,128]{2,1,0:T(8,128)(2,1)S(1)}, bf16[4,256,128]{2,1,0:T(8,128)(2,1)S(1)}, u32[]{:S(2)}, u32[]{:S(2)}) collective-permute-start(bf16[4,256,128]{2,1,0:T(8,128)(2,1)S(1)} %all-to-all-done), channel_id=1, source_target_pairs={{2,0},{15,1},{4,2},{1,3},{6,4},{3,5},{8,6},{5,7},{10,8},{7,9},{12,... | collective-permute-start | bytes 786440 | tf_op jit(solution)/shard_map/ppermute | solution.py:63
  46.7 15.9 %collective-permute-start.4 = (bf16[4,256,128]{2,1,0:T(8,128)(2,1)S(1)}, bf16[4,256,128]{2,1,0:T(8,128)(2,1)S(1)}, u32[]{:S(2)}, u32[]{:S(2)}) collective-permute-start(bf16[4,256,128]{2,1,0:T(8,128)(2,1)S(1)} %all-to-all-done), channel_id=1, source_target_pairs={{15,0},{0,1},{1,2},{2,3},{3,4},{4,5},{5,6},{6,7},{7,8},{8,9},{9,10... | collective-permute-start | bytes 786440 | tf_op jit(solution)/shard_map/ppermute | solution.py:60
  54.3 8.4 %collective-permute-start.5 = (bf16[4,256,128]{2,1,0:T(8,128)(2,1)S(1)}, bf16[4,256,128]{2,1,0:T(8,128)(2,1)S(1)}, u32[]{:S(2)}, u32[]{:S(2)}) collective-permute-start(bf16[4,256,128]{2,1,0:T(8,128)(2,1)S(1)} %all-to-all-done), channel_id=1, source_target_pairs={{1,0},{2,1},{3,2},{4,3},{5,4},{6,5},{7,6},{8,7},{9,8},{10,9},{11,1... | collective-permute-start | bytes 786440 | tf_op jit(solution)/shard_map/ppermute | solution.py:60
  64.9 26.4 %all-to-all-start.1 = ((bf16[4,8,256,128]{3,2,1,0:T(8,128)(2,1)}), bf16[4,8,256,128]{3,2,1,0:T(8,128)(2,1)}, u32[]{:S(2)}, u32[]{:S(2)}) async-start(bf16[4,8,256,128]{3,2,1,0:T(8,128)(2,1)} %broadcast_in_dim.19), calls=%async_computation.1 | async-start | bytes 4194304 | tf_op jit(solution)/shard_map/all_to_all | solution.py:72
  74.8 2.5 %copy-start.2 = (bf16[1024,1024]{1,0:T(8,128)(2,1)}, bf16[1024,1024]{1,0:T(8,128)(2,1)S(1)}, u32[]{:S(2)}) copy-start(bf16[1024,1024]{1,0:T(8,128)(2,1)S(1)} %get-tuple-element.13) | copy-start | bytes 6291460
  75.0 2.3 %copy-start.13 = (bf16[1024,128]{1,0:T(8,128)(2,1)}, bf16[1024,128]{1,0:T(8,128)(2,1)S(1)}, u32[]{:S(2)}) copy-start(bf16[1024,128]{1,0:T(8,128)(2,1)S(1)} %dynamic-slice_negate_fusion) | copy-start | bytes 786436
  75.8 1.5 %copy-start.7 = (bf16[1024,128]{1,0:T(8,128)(2,1)}, bf16[1024,128]{1,0:T(8,128)(2,1)S(1)}, u32[]{:S(2)}) copy-start(bf16[1024,128]{1,0:T(8,128)(2,1)S(1)} %convolution_convert_fusion.4) | copy-start | bytes 786436
  75.8 10.0 %copy-start.4 = (bf16[2,4,256,128]{3,2,1,0:T(8,128)(2,1)S(1)}, bf16[2,4,256,128]{3,2,1,0:T(8,128)(2,1)}, u32[]{:S(2)}) copy-start(bf16[2,4,256,128]{3,2,1,0:T(8,128)(2,1)} %copy.7) | copy-start | bytes 1572868
  86.0 25.5 %collective-permute-start.10 = (bf16[256,1024]{0,1:T(8,128)(2,1)S(1)}, bf16[256,1024]{0,1:T(8,128)(2,1)S(1)}, u32[]{:S(2)}, u32[]{:S(2)}) collective-permute-start(bf16[256,1024]{0,1:T(8,128)(2,1)S(1)} %bitcast.63), channel_id=1, source_target_pairs={{144,128},{160,144},{176,160},{128,176},{272,256},{288,272},{304,2... | collective-permute-start | bytes 1572872 | tf_op jit(solution)/shard_map/ppermute | solution.py:105
  88.0 25.5 %collective-permute-start.12 = (bf16[256,1024]{0,1:T(8,128)(2,1)S(1)}, bf16[256,1024]{0,1:T(8,128)(2,1)}, u32[]{:S(2)}, u32[]{:S(2)}) collective-permute-start(bf16[256,1024]{0,1:T(8,128)(2,1)S(1)} %bitcast.64), channel_id=1, source_target_pairs={{176,128},{128,144},{144,160},{160,176},{304,256},{256,272},{272,2... | collective-permute-start | bytes 1572872 | tf_op jit(solution)/shard_map/ppermute | solution.py:105
  91.4 1.8 %slice-start = ((bf16[2048,128]{1,0:T(8,128)(2,1)}), bf16[1024,128]{1,0:T(8,128)(2,1)S(1)}, s32[]{:S(2)}) async-start(bf16[2048,128]{1,0:T(8,128)(2,1)} %copy-done.5), calls=%async_computation.2 | async-start | bytes 524288 | tf_op jit(solution)/shard_map/slice | solution.py:86
  93.1 13.4 %copy-start = (bf16[4,256,128,8]{2,1,0,3:T(8,128)(2,1)}, bf16[4,256,128,8]{2,1,0,3:T(8,128)(2,1)S(1)}, u32[]{:S(2)}) copy-start(bf16[4,256,128,8]{2,1,0,3:T(8,128)(2,1)S(1)} %copy.10) | copy-start | bytes 6291460
  93.2 2.4 %copy-start.3 = (bf16[1024,1024]{1,0:T(8,128)(2,1)S(1)}, bf16[1024,1024]{1,0:T(8,128)(2,1)}, u32[]{:S(2)}) copy-start(bf16[1024,1024]{1,0:T(8,128)(2,1)} %copy-done.2) | copy-start | bytes 6291460
  93.2 2.5 %copy-start.14 = (bf16[1024,128]{1,0:T(8,128)(2,1)S(1)}, bf16[1024,128]{1,0:T(8,128)(2,1)}, u32[]{:S(2)}) copy-start(bf16[1024,128]{1,0:T(8,128)(2,1)} %copy-done.13) | copy-start | bytes 786436
  106.6 1.4 %copy-start.15 = (bf16[1024,128]{1,0:T(8,128)(2,1)S(1)}, bf16[1024,128]{1,0:T(8,128)(2,1)}, u32[]{:S(2)}) copy-start(bf16[1024,128]{1,0:T(8,128)(2,1)} %get-tuple-element.34) | copy-start | bytes 786436
  108.8 9.1 %collective-permute-start.14 = (bf16[1024,128]{1,0:T(8,128)(2,1)S(1)}, bf16[1024,128]{1,0:T(8,128)(2,1)S(1)}, u32[]{:S(2)}, u32[]{:S(2)}) collective-permute-start(bf16[1024,128]{1,0:T(8,128)(2,1)S(1)} %fusion.18), channel_id=1, source_target_pairs={{0,256},{1,257},{2,258},{3,259},{4,260},{5,261},{6,262},{7,263},{8... | collective-permute-start | bytes 786440 | tf_op jit(solution)/shard_map/ppermute | solution.py:22
  109.4 16.0 %collective-permute-start.15 = (bf16[1024,128]{1,0:T(8,128)(2,1)S(1)}, bf16[1024,128]{1,0:T(8,128)(2,1)S(1)}, u32[]{:S(2)}, u32[]{:S(2)}) collective-permute-start(bf16[1024,128]{1,0:T(8,128)(2,1)S(1)} %fusion.18), channel_id=1, source_target_pairs={{0,128},{1,129},{2,130},{3,131},{4,132},{5,133},{6,134},{7,135},{8... | collective-permute-start | bytes 786440 | tf_op jit(solution)/shard_map/ppermute | solution.py:22
  110.7 14.7 %collective-permute-start.16 = (bf16[1024,128]{1,0:T(8,128)(2,1)S(1)}, bf16[1024,128]{1,0:T(8,128)(2,1)S(1)}, u32[]{:S(2)}, u32[]{:S(2)}) collective-permute-start(bf16[1024,128]{1,0:T(8,128)(2,1)S(1)} %fusion.18), channel_id=1, source_target_pairs={{0,384},{1,385},{2,386},{3,387},{4,388},{5,389},{6,390},{7,391},{8... | collective-permute-start | bytes 786440 | tf_op jit(solution)/shard_map/ppermute | solution.py:22
  111.5 17.0 %collective-permute-start.11 = (bf16[128,1024]{0,1:T(8,128)(2,1)S(1)}, bf16[128,1024]{0,1:T(8,128)(2,1)S(1)}, u32[]{:S(2)}, u32[]{:S(2)}) collective-permute-start(bf16[128,1024]{0,1:T(8,128)(2,1)S(1)} %slice.73), channel_id=1, source_target_pairs={{144,128},{160,144},{176,160},{128,176},{272,256},{288,272},{304,2... | collective-permute-start | bytes 786440 | tf_op jit(solution)/shard_map/ppermute | solution.py:105
  114.5 14.2 %collective-permute-start.13 = (bf16[128,1024]{0,1:T(8,128)(2,1)S(1)}, bf16[128,1024]{0,1:T(8,128)(2,1)S(1)}, u32[]{:S(2)}, u32[]{:S(2)}) collective-permute-start(bf16[128,1024]{0,1:T(8,128)(2,1)S(1)} %slice.75), channel_id=1, source_target_pairs={{176,128},{128,144},{144,160},{160,176},{304,256},{256,272},{272,2... | collective-permute-start | bytes 786440 | tf_op jit(solution)/shard_map/ppermute | solution.py:105
  125.5 4.8 %collective-permute-start.17 = (bf16[1024,128]{1,0:T(8,128)(2,1)S(1)}, bf16[1024,128]{1,0:T(8,128)(2,1)S(1)}, u32[]{:S(2)}, u32[]{:S(2)}) collective-permute-start(bf16[1024,128]{1,0:T(8,128)(2,1)S(1)} %select_select_fusion), channel_id=1, source_target_pairs={{0,64},{64,0},{1,65},{65,1},{2,66},{66,2},{3,67},{67,3},{4,68},{68... | collective-permute-start | bytes 786440 | tf_op jit(solution)/shard_map/ppermute | solution.py:112
  128.7 1.7 %copy-start.1 = (bf16[4,256,128,8]{2,1,0,3:T(8,128)(2,1)S(1)}, bf16[4,256,128,8]{2,1,0,3:T(8,128)(2,1)}, u32[]{:S(2)}) copy-start(bf16[4,256,128,8]{2,1,0,3:T(8,128)(2,1)} %copy-done) | copy-start | bytes 6291460
  130.1 1.1 copy-start.8
  130.1 1.2 copy-start.12
  (5 other events, 4.3 us)

commit v9 on v8

--- a/solution.py
+++ b/solution.py
@@ -93,8 +93,8 @@
     w = (jnp.where(in0, zeros, a).astype(F32) - product(one, c0x)).astype(BF)
     r1 = times(inv_l, w)
     c1 = jnp.where(in0, zeros, jnp.where(in1, minus_u, times(inv_u, r1)))
-    c1 = cores(c1)[1]
-    t = lax.optimization_barrier(product(one, c1).astype(BF))
+    c1x = lax.ppermute(c1, ("y", "core"), [(1, 0)])
+    t = lax.optimization_barrier(product(one, c1x).astype(BF))
     s = lax.optimization_barrier(times(inv_l, t))
     d = (base.astype(F32) - dot(inv_u, s)).astype(BF)
     right = jnp.where(core == 0, d, c1)

time: 134 us -> 136 us (1.015)
  the two profiles are of different devices: /device:TPU:43 before, /device:TPU:40 now
where the time goes in v9:
time: 136 us; the launch traced here: 135 us
  starting transfers between devices  58.8 us (43%)
  waiting for transfers between devices  44 us (32%)
  local copies, waits for them, and re-layouts  14.7 us (11%)
  matrix products  11 us (8%)
  other arithmetic  3.13 us (2%)
  blocking collectives  2.17 us (2%)
    all_to_all x1, starting transfers between devices, shards(): own = lax.all_to_all(copies(share, 4), 'z', 0, 0, axis_index_groups=fours)  14.2 us
    ppermute x4, starting transfers between devices, from_x(): return lax.ppermute(value, ('y', 'x'), planes)  12.1 us
    all_to_all x1, waiting for transfers between devices, shards(): one = lax.all_to_all(sent, 'x', 0, 0)  11.7 us
    ppermute x6, starting transfers between devices, from_first(): got = {k: lax.ppermute(values[k], axis, [(0, k)]) for k in (3, 1, 2)}  10.2 us
    all_to_all x1, waiting for transfers between devices, shards(): own = lax.all_to_all(copies(share, 4), 'z', 0, 0, axis_index_groups=fours)  8.91 us
    ppermute x1, waiting for transfers between devices, shards(): lax.ppermute(own, 'z', [((k + 2 - 4 * (k % 2)) % 16, k) for k in range(16)])  7.99 us
    dot_general x7, matrix products, dot(): return jnp.dot(a, b, preferred_element_type=F32)  7.14 us
    ppermute x2, waiting for transfers between devices, from_z(): lax.ppermute(value, 'z', [((k + distance) % 16, k) for k in range(16)])  6.23 us
  transfers between devices with their start and end apart: 21, of which 10 were waited for; matrix products, arithmetic and copies ran while one was open for 14% of the time, Pallas kernels for 0%

profile of v9, /device:TPU:40, one launch (start us, length us, event | category | flops | bytes accessed | tf_op | source)
XLA Modules:
  0.0 134.6 jit_solution(13725933043377604543)
XLA Ops:
  0.9 4.9 %collective-permute-start = (bf16[256,128]{1,0:T(8,128)(2,1)S(1)}, bf16[256,128]{1,0:T(8,128)(2,1)S(1)}, u32[]{:S(2)}, u32[]{:S(2)}) collective-permute-start(bf16[256,128]{1,0:T(8,128)(2,1)S(1)} %get-tuple-element.33), channel_id=1, source_target_pairs={{0,32},{1,33},{2,34},{3,35},{4,36},{5,37},{6,38},{7,39},{8,40},{9,... | collective-permute-start | bytes 196616 | tf_op jit(solution)/shard_map/ppermute | solution.py:22
  5.9 1.3 collective-permute-start.1
  9.0 1.3 collective-permute-done.2
  11.9 14.2 %all-to-all-start = ((bf16[4,256,128]{2,1,0:T(8,128)(2,1)}), bf16[4,256,128]{2,1,0:T(8,128)(2,1)S(1)}, u32[]{:S(2)}, u32[]{:S(2)}) async-start(bf16[4,256,128]{2,1,0:T(8,128)(2,1)} %broadcast_in_dim.17), calls=%async_computation | async-start | bytes 524288 | tf_op jit(solution)/shard_map/all_to_all | solution.py:57
  27.4 1.9 %collective-permute-start.6 = (bf16[2,128,1024]{2,1,0:T(8,128)(2,1)S(1)}, bf16[2,128,1024]{2,1,0:T(8,128)(2,1)S(1)}, u32[]{:S(2)}, u32[]{:S(2)}) collective-permute-start(bf16[2,128,1024]{2,1,0:T(8,128)(2,1)S(1)} %get-tuple-element.30), channel_id=1, source_target_pairs={{0,64},{64,0},{1,65},{65,1},{2,66},{66,2},{3,67},{67,3},{4,68},{68... | collective-permute-start | bytes 1572872 | tf_op jit(solution)/shard_map/ppermute | solution.py:51
  29.4 1.8 %collective-permute-done.6 = bf16[2,128,1024]{2,1,0:T(8,128)(2,1)S(1)} collective-permute-done((bf16[2,128,1024]{2,1,0:T(8,128)(2,1)S(1)}, bf16[2,128,1024]{2,1,0:T(8,128)(2,1)S(1)}, u32[]{:S(2)}, u32[]{:S(2)}) %collective-permute-start.6) | collective-permute-done | bytes 524320 | tf_op jit(solution)/shard_map/ppermute | solution.py:51
  31.4 1.7 %collective-permute-start.9 = (bf16[2,2,128,1024]{3,2,1,0:T(8,128)(2,1)S(1)}, bf16[2,2,128,1024]{3,2,1,0:T(8,128)(2,1)}, u32[]{:S(2)}, u32[]{:S(2)}) collective-permute-start(bf16[2,2,128,1024]{3,2,1,0:T(8,128)(2,1)S(1)} %maximum_select_fusion), channel_id=1, source_target_pairs={{384,0},{385,1},{386,2},{387,3},{388,4},{389,5},{390,6},{391,7},{3... | collective-permute-start | bytes 3145736 | tf_op jit(solution)/shard_map/ppermute | solution.py:54
  33.0 1.6 %collective-permute-start.8 = (bf16[2,2,128,1024]{3,2,1,0:T(8,128)(2,1)S(1)}, bf16[2,2,128,1024]{3,2,1,0:T(8,128)(2,1)}, u32[]{:S(2)}, u32[]{:S(2)}) collective-permute-start(bf16[2,2,128,1024]{3,2,1,0:T(8,128)(2,1)S(1)} %maximum_select_fusion), channel_id=1, source_target_pairs={{256,0},{257,1},{258,2},{259,3},{260,4},{261,5},{262,6},{263,7},{2... | collective-permute-start | bytes 3145736 | tf_op jit(solution)/shard_map/ppermute | solution.py:54
  34.7 2.6 %collective-permute-start.7 = (bf16[2,2,128,1024]{3,2,1,0:T(8,128)(2,1)S(1)}, bf16[2,2,128,1024]{3,2,1,0:T(8,128)(2,1)}, u32[]{:S(2)}, u32[]{:S(2)}) collective-permute-start(bf16[2,2,128,1024]{3,2,1,0:T(8,128)(2,1)S(1)} %maximum_select_fusion), channel_id=1, source_target_pairs={{128,0},{129,1},{130,2},{131,3},{132,4},{133,5},{134,6},{135,7},{1... | collective-permute-start | bytes 3145736 | tf_op jit(solution)/shard_map/ppermute | solution.py:54
  37.3 8.9 %all-to-all-done = bf16[4,256,128]{2,1,0:T(8,128)(2,1)S(1)} async-done(((bf16[4,256,128]{2,1,0:T(8,128)(2,1)}), bf16[4,256,128]{2,1,0:T(8,128)(2,1)S(1)}, u32[]{:S(2)}, u32[]{:S(2)}) %all-to-all-start) | async-done | bytes 262176 | tf_op jit(solution)/shard_map/all_to_all | solution.py:57
  46.2 1.9 %collective-permute-start.3 = (bf16[4,256,128]{2,1,0:T(8,128)(2,1)S(1)}, bf16[4,256,128]{2,1,0:T(8,128)(2,1)S(1)}, u32[]{:S(2)}, u32[]{:S(2)}) collective-permute-start(bf16[4,256,128]{2,1,0:T(8,128)(2,1)S(1)} %all-to-all-done), channel_id=1, source_target_pairs={{2,0},{15,1},{4,2},{1,3},{6,4},{3,5},{8,6},{5,7},{10,8},{7,9},{12,... | collective-permute-start | bytes 786440 | tf_op jit(solution)/shard_map/ppermute | solution.py:63
  48.1 3.0 %collective-permute-start.4 = (bf16[4,256,128]{2,1,0:T(8,128)(2,1)S(1)}, bf16[4,256,128]{2,1,0:T(8,128)(2,1)S(1)}, u32[]{:S(2)}, u32[]{:S(2)}) collective-permute-start(bf16[4,256,128]{2,1,0:T(8,128)(2,1)S(1)} %all-to-all-done), channel_id=1, source_target_pairs={{15,0},{0,1},{1,2},{2,3},{3,4},{4,5},{5,6},{6,7},{7,8},{8,9},{9,10... | collective-permute-start | bytes 786440 | tf_op jit(solution)/shard_map/ppermute | solution.py:60
  51.2 8.0 %collective-permute-done.3 = bf16[4,256,128]{2,1,0:T(8,128)(2,1)S(1)} collective-permute-done((bf16[4,256,128]{2,1,0:T(8,128)(2,1)S(1)}, bf16[4,256,128]{2,1,0:T(8,128)(2,1)S(1)}, u32[]{:S(2)}, u32[]{:S(2)}) %collective-permute-start.3) | collective-permute-done | bytes 262176 | tf_op jit(solution)/shard_map/ppermute | solution.py:63
  59.2 1.9 %collective-permute-start.5 = (bf16[4,256,128]{2,1,0:T(8,128)(2,1)S(1)}, bf16[4,256,128]{2,1,0:T(8,128)(2,1)S(1)}, u32[]{:S(2)}, u32[]{:S(2)}) collective-permute-start(bf16[4,256,128]{2,1,0:T(8,128)(2,1)S(1)} %all-to-all-done), channel_id=1, source_target_pairs={{1,0},{2,1},{3,2},{4,3},{5,4},{6,5},{7,6},{8,7},{9,8},{10,9},{11,1... | collective-permute-start | bytes 786440 | tf_op jit(solution)/shard_map/ppermute | solution.py:60
  62.3 5.1 %collective-permute-done.5 = bf16[4,256,128]{2,1,0:T(8,128)(2,1)S(1)} collective-permute-done((bf16[4,256,128]{2,1,0:T(8,128)(2,1)S(1)}, bf16[4,256,128]{2,1,0:T(8,128)(2,1)S(1)}, u32[]{:S(2)}, u32[]{:S(2)}) %collective-permute-start.5) | collective-permute-done | bytes 262176 | tf_op jit(solution)/shard_map/ppermute | solution.py:60
  67.9 1.8 %broadcast_in_dim.19 = bf16[4,8,256,128]{3,2,1,0:T(8,128)(2,1)} broadcast(bf16[8,256,128]{2,1,0:T(8,128)(2,1)S(1)} %bitcast.68), dimensions={1,2,3} | broadcast | bytes 2621440 | tf_op jit(solution)/shard_map/broadcast_in_dim | solution.py:29
  69.7 4.5 %all-to-all-start.1 = ((bf16[4,8,256,128]{3,2,1,0:T(8,128)(2,1)}), bf16[4,8,256,128]{3,2,1,0:T(8,128)(2,1)}, u32[]{:S(2)}, u32[]{:S(2)}) async-start(bf16[4,8,256,128]{3,2,1,0:T(8,128)(2,1)} %broadcast_in_dim.19), calls=%async_computation.1 | async-start | bytes 4194304 | tf_op jit(solution)/shard_map/all_to_all | solution.py:72
  80.6 1.4 %broadcast_select_fusion = (bf16[1024,128]{1,0:T(8,128)(2,1)}, bf16[1024,128]{1,0:T(8,128)(2,1)S(1)}) fusion(pred[]{:T(512)S(6)} %and.22, bf16[1024,128]{1,0:T(8,128)(2,1)S(1)} %dynamic-slice_negate_fusion, bf16[1024,1024]{1,0:T(8,128)(2,1)S(1)} %get-tuple-element.13, bf16[1024,128]{1,0:T(8,128)(2,1)S(1)} %convolution_convert_fusion.4, pred[]{:T(512)S(6)} %lt.45), kind=kOutput, calls=%fused_computation.38 | convolution fusion | flops 268828672 | bytes 3145730 | tf_op jit(solution)/shard_map/dot_general | solution.py:12
  82.0 2.2 %all-gather = bf16[2048,128]{1,0:T(8,128)(2,1)S(1)} all-gather(bf16[1024,128]{1,0:T(8,128)(2,1)S(1)} %get-tuple-element.35), channel_id=2, replica_groups=mesh['y'=4,'core'=2,'x'=4,'z'=16] {'core'}, dimensions={0}, use_global_device_ids=true | all-gather | bytes 786432 | tf_op jit(solution)/shard_map/all_gather | solution.py:33
  84.2 11.7 %all-to-all-done.1 = bf16[4,8,256,128]{3,2,1,0:T(8,128)(2,1)} async-done(((bf16[4,8,256,128]{3,2,1,0:T(8,128)(2,1)}), bf16[4,8,256,128]{3,2,1,0:T(8,128)(2,1)}, u32[]{:S(2)}, u32[]{:S(2)}) %all-to-all-start.1) | async-done | bytes 2097184 | tf_op jit(solution)/shard_map/all_to_all | solution.py:72
  95.9 1.7 %copy.10 = bf16[4,256,128,8]{2,1,0,3:T(8,128)(2,1)S(1)} copy(bf16[4,256,128,8]{2,1,3,0:T(8,128)(2,1)} %bitcast.20) | data formatting | bytes 4194304 | tf_op jit(solution)/shard_map/xzrk,zkn->xrn/dot_general | solution.py:91
  100.1 1.4 %fusion.17 = bf16[1024,128]{1,0:T(8,128)(2,1)} fusion(bf16[1024,128]{1,0:T(8,128)(2,1)S(1)} %copy-done.14, bf16[1024,1024]{1,0:T(8,128)(2,1)S(1)} %copy-done.3, bf16[1024,128]{1,0:T(8,128)(2,1)S(1)} %convolution_convert_fusion.2, pred[]{:T(512)S(6)} %and.22, pred[]{:T(512)S(6)} %lt.45), kind=kOutput, calls=%fused_computation.26 | convolution fusion | flops 268828672 | bytes 2883586 | tf_op jit(solution)/shard_map/dot_general | solution.py:12
  101.5 1.4 %collective-permute-start.11 = (bf16[1024,128]{1,0:T(8,128)(2,1)}, bf16[1024,128]{1,0:T(8,128)(2,1)}, u32[]{:S(2)}, u32[]{:S(2)}) collective-permute-start(bf16[1024,128]{1,0:T(8,128)(2,1)} %fusion.17), channel_id=1, source_target_pairs={{64,0},{65,1},{66,2},{67,3},{68,4},{69,5},{70,6},{71,7},{72,8},{73... | collective-permute-start | bytes 786440 | tf_op jit(solution)/shard_map/ppermute | solution.py:96
  103.1 3.1 %collective-permute-start.10 = (bf16[256,1024]{0,1:T(8,128)(2,1)S(1)}, bf16[256,1024]{0,1:T(8,128)(2,1)S(1)}, u32[]{:S(2)}, u32[]{:S(2)}) collective-permute-start(bf16[256,1024]{0,1:T(8,128)(2,1)S(1)} %bitcast.63), channel_id=1, source_target_pairs={{144,128},{160,144},{176,160},{128,176},{272,256},{288,272},{304,2... | collective-permute-start | bytes 1572872 | tf_op jit(solution)/shard_map/ppermute | solution.py:105
  106.2 2.8 %collective-permute-start.13 = (bf16[256,1024]{0,1:T(8,128)(2,1)S(1)}, bf16[256,1024]{0,1:T(8,128)(2,1)}, u32[]{:S(2)}, u32[]{:S(2)}) collective-permute-start(bf16[256,1024]{0,1:T(8,128)(2,1)S(1)} %bitcast.64), channel_id=1, source_target_pairs={{176,128},{128,144},{144,160},{160,176},{304,256},{256,272},{272,2... | collective-permute-start | bytes 1572872 | tf_op jit(solution)/shard_map/ppermute | solution.py:105
  109.0 2.4 %fusion.9 = bf16[1024,128]{1,0:T(8,128)(2,1)S(1)} fusion(bf16[1024,128,8]{1,0,2:T(8,128)(2,1)} %bitcast.61, bf16[8,128,128]{2,1,0:T(8,128)(2,1)} %bitcast.24), kind=kOutput, calls=%fused_computation.11 | convolution fusion | flops 268566528 | bytes 2621440 | tf_op jit(solution)/shard_map/xzrk,zkn->xrn/dot_general | solution.py:91
  115.7 4.3 %collective-permute-start.12 = (bf16[128,1024]{0,1:T(8,128)(2,1)S(1)}, bf16[128,1024]{0,1:T(8,128)(2,1)S(1)}, u32[]{:S(2)}, u32[]{:S(2)}) collective-permute-start(bf16[128,1024]{0,1:T(8,128)(2,1)S(1)} %slice.68), channel_id=1, source_target_pairs={{144,128},{160,144},{176,160},{128,176},{272,256},{288,272},{304,2... | collective-permute-start | bytes 786440 | tf_op jit(solution)/shard_map/ppermute | solution.py:105
  121.1 1.9 %collective-permute-start.14 = (bf16[128,1024]{0,1:T(8,128)(2,1)S(1)}, bf16[128,1024]{0,1:T(8,128)(2,1)S(1)}, u32[]{:S(2)}, u32[]{:S(2)}) collective-permute-start(bf16[128,1024]{0,1:T(8,128)(2,1)S(1)} %slice.69), channel_id=1, source_target_pairs={{176,128},{128,144},{144,160},{160,176},{304,256},{256,272},{272,2... | collective-permute-start | bytes 786440 | tf_op jit(solution)/shard_map/ppermute | solution.py:105
  123.0 2.9 %collective-permute-done.16 = bf16[1024,128]{1,0:T(8,128)(2,1)S(1)} collective-permute-done((bf16[1024,128]{1,0:T(8,128)(2,1)S(1)}, bf16[1024,128]{1,0:T(8,128)(2,1)S(1)}, u32[]{:S(2)}, u32[]{:S(2)}) %collective-permute-start.16) | collective-permute-done | bytes 262176 | tf_op jit(solution)/shard_map/ppermute | solution.py:22
  125.9 1.9 %collective-permute-start.18 = (bf16[1024,128]{1,0:T(8,128)(2,1)S(1)}, bf16[1024,128]{1,0:T(8,128)(2,1)S(1)}, u32[]{:S(2)}, u32[]{:S(2)}) collective-permute-start(bf16[1024,128]{1,0:T(8,128)(2,1)S(1)} %select_select_fusion), channel_id=1, source_target_pairs={{0,64},{64,0},{1,65},{65,1},{2,66},{66,2},{3,67},{67,3},{4,68},{68... | collective-permute-start | bytes 786440 | tf_op jit(solution)/shard_map/ppermute | solution.py:112
  127.9 2.6 %collective-permute-done.14 = bf16[128,1024]{0,1:T(8,128)(2,1)S(1)} collective-permute-done((bf16[128,1024]{0,1:T(8,128)(2,1)S(1)}, bf16[128,1024]{0,1:T(8,128)(2,1)S(1)}, u32[]{:S(2)}, u32[]{:S(2)}) %collective-permute-start.14) | collective-permute-done | bytes 262176 | tf_op jit(solution)/shard_map/ppermute | solution.py:105
  133.1 1.5 %fusion.19 = bf16[1024,128]{1,0:T(8,128)(2,1)} fusion(f32[1024,128]{1,0:T(8,128)S(1)} %convolution_bitcast_fusion, bf16[1024,128]{1,0:T(8,128)(2,1)S(1)} %select_select_fusion, bf16[1792,1024]{0,1:T(8,128)(2,1)S(1)} %constant_dynamic-update-slice_fusion.7, s32[]{:T(128)S(6)} %select_n.167, bf16[1024,128]{1,0:T(8,128)(2,1)S(1)} %copy-done.10, ...), kind=kOutput, calls=%fused_computation.28 | convolution fusion | flops 269615104 | bytes 4194313 | tf_op jit(solution)/shard_map/dot_general | solution.py:12
  (91 shorter events, 24.2 us)
Async XLA Ops:
  0.9 7.6 %collective-permute-start = (bf16[256,128]{1,0:T(8,128)(2,1)S(1)}, bf16[256,128]{1,0:T(8,128)(2,1)S(1)}, u32[]{:S(2)}, u32[]{:S(2)}) collective-permute-start(bf16[256,128]{1,0:T(8,128)(2,1)S(1)} %get-tuple-element.33), channel_id=1, source_target_pairs={{0,32},{1,33},{2,34},{3,35},{4,36},{5,37},{6,38},{7,39},{8,40},{9,... | collective-permute-start | bytes 196616 | tf_op jit(solution)/shard_map/ppermute | solution.py:22
  5.9 3.2 %collective-permute-start.1 = (bf16[256,128]{1,0:T(8,128)(2,1)S(1)}, bf16[256,128]{1,0:T(8,128)(2,1)S(1)}, u32[]{:S(2)}, u32[]{:S(2)}) collective-permute-start(bf16[256,128]{1,0:T(8,128)(2,1)S(1)} %get-tuple-element.32), channel_id=1, source_target_pairs={{0,16},{1,17},{2,18},{3,19},{4,20},{5,21},{6,22},{7,23},{8,24},{9,... | collective-permute-start | bytes 196616 | tf_op jit(solution)/shard_map/ppermute | solution.py:22
  7.2 3.2 %collective-permute-start.2 = (bf16[256,128]{1,0:T(8,128)(2,1)S(1)}, bf16[256,128]{1,0:T(8,128)(2,1)S(1)}, u32[]{:S(2)}, u32[]{:S(2)}) collective-permute-start(bf16[256,128]{1,0:T(8,128)(2,1)S(1)} %get-tuple-element.31), channel_id=1, source_target_pairs={{0,48},{1,49},{2,50},{3,51},{4,52},{5,53},{6,54},{7,55},{8,56},{9,... | collective-permute-start | bytes 196616 | tf_op jit(solution)/shard_map/ppermute | solution.py:22
  11.9 34.3 %all-to-all-start = ((bf16[4,256,128]{2,1,0:T(8,128)(2,1)}), bf16[4,256,128]{2,1,0:T(8,128)(2,1)S(1)}, u32[]{:S(2)}, u32[]{:S(2)}) async-start(bf16[4,256,128]{2,1,0:T(8,128)(2,1)} %broadcast_in_dim.17), calls=%async_computation | async-start | bytes 524288 | tf_op jit(solution)/shard_map/all_to_all | solution.py:57
  27.4 3.8 %collective-permute-start.6 = (bf16[2,128,1024]{2,1,0:T(8,128)(2,1)S(1)}, bf16[2,128,1024]{2,1,0:T(8,128)(2,1)S(1)}, u32[]{:S(2)}, u32[]{:S(2)}) collective-permute-start(bf16[2,128,1024]{2,1,0:T(8,128)(2,1)S(1)} %get-tuple-element.30), channel_id=1, source_target_pairs={{0,64},{64,0},{1,65},{65,1},{2,66},{66,2},{3,67},{67,3},{4,68},{68... | collective-permute-start | bytes 1572872 | tf_op jit(solution)/shard_map/ppermute | solution.py:51
  31.4 43.7 %collective-permute-start.9 = (bf16[2,2,128,1024]{3,2,1,0:T(8,128)(2,1)S(1)}, bf16[2,2,128,1024]{3,2,1,0:T(8,128)(2,1)}, u32[]{:S(2)}, u32[]{:S(2)}) collective-permute-start(bf16[2,2,128,1024]{3,2,1,0:T(8,128)(2,1)S(1)} %maximum_select_fusion), channel_id=1, source_target_pairs={{384,0},{385,1},{386,2},{387,3},{388,4},{389,5},{390,6},{391,7},{3... | collective-permute-start | bytes 3145736 | tf_op jit(solution)/shard_map/ppermute | solution.py:54
  33.0 43.3 %collective-permute-start.8 = (bf16[2,2,128,1024]{3,2,1,0:T(8,128)(2,1)S(1)}, bf16[2,2,128,1024]{3,2,1,0:T(8,128)(2,1)}, u32[]{:S(2)}, u32[]{:S(2)}) collective-permute-start(bf16[2,2,128,1024]{3,2,1,0:T(8,128)(2,1)S(1)} %maximum_select_fusion), channel_id=1, source_target_pairs={{256,0},{257,1},{258,2},{259,3},{260,4},{261,5},{262,6},{263,7},{2... | collective-permute-start | bytes 3145736 | tf_op jit(solution)/shard_map/ppermute | solution.py:54
  34.7 42.9 %collective-permute-start.7 = (bf16[2,2,128,1024]{3,2,1,0:T(8,128)(2,1)S(1)}, bf16[2,2,128,1024]{3,2,1,0:T(8,128)(2,1)}, u32[]{:S(2)}, u32[]{:S(2)}) collective-permute-start(bf16[2,2,128,1024]{3,2,1,0:T(8,128)(2,1)S(1)} %maximum_select_fusion), channel_id=1, source_target_pairs={{128,0},{129,1},{130,2},{131,3},{132,4},{133,5},{134,6},{135,7},{1... | collective-permute-start | bytes 3145736 | tf_op jit(solution)/shard_map/ppermute | solution.py:54
  46.2 13.0 %collective-permute-start.3 = (bf16[4,256,128]{2,1,0:T(8,128)(2,1)S(1)}, bf16[4,256,128]{2,1,0:T(8,128)(2,1)S(1)}, u32[]{:S(2)}, u32[]{:S(2)}) collective-permute-start(bf16[4,256,128]{2,1,0:T(8,128)(2,1)S(1)} %all-to-all-done), channel_id=1, source_target_pairs={{2,0},{15,1},{4,2},{1,3},{6,4},{3,5},{8,6},{5,7},{10,8},{7,9},{12,... | collective-permute-start | bytes 786440 | tf_op jit(solution)/shard_map/ppermute | solution.py:63
  48.1 14.1 %collective-permute-start.4 = (bf16[4,256,128]{2,1,0:T(8,128)(2,1)S(1)}, bf16[4,256,128]{2,1,0:T(8,128)(2,1)S(1)}, u32[]{:S(2)}, u32[]{:S(2)}) collective-permute-start(bf16[4,256,128]{2,1,0:T(8,128)(2,1)S(1)} %all-to-all-done), channel_id=1, source_target_pairs={{15,0},{0,1},{1,2},{2,3},{3,4},{4,5},{5,6},{6,7},{7,8},{8,9},{9,10... | collective-permute-start | bytes 786440 | tf_op jit(solution)/shard_map/ppermute | solution.py:60
  59.2 8.3 %collective-permute-start.5 = (bf16[4,256,128]{2,1,0:T(8,128)(2,1)S(1)}, bf16[4,256,128]{2,1,0:T(8,128)(2,1)S(1)}, u32[]{:S(2)}, u32[]{:S(2)}) collective-permute-start(bf16[4,256,128]{2,1,0:T(8,128)(2,1)S(1)} %all-to-all-done), channel_id=1, source_target_pairs={{1,0},{2,1},{3,2},{4,3},{5,4},{6,5},{7,6},{8,7},{9,8},{10,9},{11,1... | collective-permute-start | bytes 786440 | tf_op jit(solution)/shard_map/ppermute | solution.py:60
  69.7 26.2 %all-to-all-start.1 = ((bf16[4,8,256,128]{3,2,1,0:T(8,128)(2,1)}), bf16[4,8,256,128]{3,2,1,0:T(8,128)(2,1)}, u32[]{:S(2)}, u32[]{:S(2)}) async-start(bf16[4,8,256,128]{3,2,1,0:T(8,128)(2,1)} %broadcast_in_dim.19), calls=%async_computation.1 | async-start | bytes 4194304 | tf_op jit(solution)/shard_map/all_to_all | solution.py:72
  79.6 2.4 %copy-start.2 = (bf16[1024,1024]{1,0:T(8,128)(2,1)}, bf16[1024,1024]{1,0:T(8,128)(2,1)S(1)}, u32[]{:S(2)}) copy-start(bf16[1024,1024]{1,0:T(8,128)(2,1)S(1)} %get-tuple-element.13) | copy-start | bytes 6291460
  79.8 2.3 %copy-start.13 = (bf16[1024,128]{1,0:T(8,128)(2,1)}, bf16[1024,128]{1,0:T(8,128)(2,1)S(1)}, u32[]{:S(2)}) copy-start(bf16[1024,128]{1,0:T(8,128)(2,1)S(1)} %dynamic-slice_negate_fusion) | copy-start | bytes 786436
  80.6 3.6 %copy-start.7 = (bf16[1024,128]{1,0:T(8,128)(2,1)}, bf16[1024,128]{1,0:T(8,128)(2,1)S(1)}, u32[]{:S(2)}) copy-start(bf16[1024,128]{1,0:T(8,128)(2,1)S(1)} %convolution_convert_fusion.4) | copy-start | bytes 786436
  97.7 2.4 %copy-start.3 = (bf16[1024,1024]{1,0:T(8,128)(2,1)S(1)}, bf16[1024,1024]{1,0:T(8,128)(2,1)}, u32[]{:S(2)}) copy-start(bf16[1024,1024]{1,0:T(8,128)(2,1)} %copy-done.2) | copy-start | bytes 6291460
  97.7 2.4 %copy-start.14 = (bf16[1024,128]{1,0:T(8,128)(2,1)S(1)}, bf16[1024,128]{1,0:T(8,128)(2,1)}, u32[]{:S(2)}) copy-start(bf16[1024,128]{1,0:T(8,128)(2,1)} %copy-done.13) | copy-start | bytes 786436
  98.4 3.1 %copy-start.9 = (bf16[1024,128]{1,0:T(8,128)(2,1)}, bf16[1024,128]{1,0:T(8,128)(2,1)S(1)}, u32[]{:S(2)}) copy-start(bf16[1024,128]{1,0:T(8,128)(2,1)S(1)} %fusion.13) | copy-start | bytes 786436
  100.1 2.8 %copy-start.11 = (bf16[1024,128]{1,0:T(8,128)(2,1)}, bf16[1024,128]{1,0:T(8,128)(2,1)S(1)}, u32[]{:S(2)}) copy-start(bf16[1024,128]{1,0:T(8,128)(2,1)S(1)} %convolution_convert_fusion.2) | copy-start | bytes 786436
  100.1 2.8 %copy-start.5 = (bf16[2,4,256,128]{3,2,1,0:T(8,128)(2,1)S(1)}, bf16[2,4,256,128]{3,2,1,0:T(8,128)(2,1)}, u32[]{:S(2)}) copy-start(bf16[2,4,256,128]{3,2,1,0:T(8,128)(2,1)} %copy.7) | copy-start | bytes 1572868
  101.5 7.5 %collective-permute-start.11 = (bf16[1024,128]{1,0:T(8,128)(2,1)}, bf16[1024,128]{1,0:T(8,128)(2,1)}, u32[]{:S(2)}, u32[]{:S(2)}) collective-permute-start(bf16[1024,128]{1,0:T(8,128)(2,1)} %fusion.17), channel_id=1, source_target_pairs={{64,0},{65,1},{66,2},{67,3},{68,4},{69,5},{70,6},{71,7},{72,8},{73... | collective-permute-start | bytes 786440 | tf_op jit(solution)/shard_map/ppermute | solution.py:96
  103.1 12.6 %collective-permute-start.10 = (bf16[256,1024]{0,1:T(8,128)(2,1)S(1)}, bf16[256,1024]{0,1:T(8,128)(2,1)S(1)}, u32[]{:S(2)}, u32[]{:S(2)}) collective-permute-start(bf16[256,1024]{0,1:T(8,128)(2,1)S(1)} %bitcast.63), channel_id=1, source_target_pairs={{144,128},{160,144},{176,160},{128,176},{272,256},{288,272},{304,2... | collective-permute-start | bytes 1572872 | tf_op jit(solution)/shard_map/ppermute | solution.py:105
  106.2 13.8 %collective-permute-start.13 = (bf16[256,1024]{0,1:T(8,128)(2,1)S(1)}, bf16[256,1024]{0,1:T(8,128)(2,1)}, u32[]{:S(2)}, u32[]{:S(2)}) collective-permute-start(bf16[256,1024]{0,1:T(8,128)(2,1)S(1)} %bitcast.64), channel_id=1, source_target_pairs={{176,128},{128,144},{144,160},{160,176},{304,256},{256,272},{272,2... | collective-permute-start | bytes 1572872 | tf_op jit(solution)/shard_map/ppermute | solution.py:105
  109.0 3.2 %copy-start.4 = (bf16[1024,1024]{1,0:T(8,128)(2,1)S(1)}, bf16[1024,1024]{1,0:T(8,128)(2,1)}, u32[]{:S(2)}) copy-start(bf16[1024,1024]{1,0:T(8,128)(2,1)} %copy-done.2) | copy-start | bytes 6291460
  109.0 3.2 %copy-start.15 = (bf16[1024,128]{1,0:T(8,128)(2,1)S(1)}, bf16[1024,128]{1,0:T(8,128)(2,1)}, u32[]{:S(2)}) copy-start(bf16[1024,128]{1,0:T(8,128)(2,1)} %get-tuple-element.34) | copy-start | bytes 786436
  112.9 10.0 %collective-permute-start.15 = (bf16[1024,128]{1,0:T(8,128)(2,1)S(1)}, bf16[1024,128]{1,0:T(8,128)(2,1)S(1)}, u32[]{:S(2)}, u32[]{:S(2)}) collective-permute-start(bf16[1024,128]{1,0:T(8,128)(2,1)S(1)} %fusion.18), channel_id=1, source_target_pairs={{0,256},{1,257},{2,258},{3,259},{4,260},{5,261},{6,262},{7,263},{8... | collective-permute-start | bytes 786440 | tf_op jit(solution)/shard_map/ppermute | solution.py:22
  113.6 12.2 %collective-permute-start.16 = (bf16[1024,128]{1,0:T(8,128)(2,1)S(1)}, bf16[1024,128]{1,0:T(8,128)(2,1)S(1)}, u32[]{:S(2)}, u32[]{:S(2)}) collective-permute-start(bf16[1024,128]{1,0:T(8,128)(2,1)S(1)} %fusion.18), channel_id=1, source_target_pairs={{0,128},{1,129},{2,130},{3,131},{4,132},{5,133},{6,134},{7,135},{8... | collective-permute-start | bytes 786440 | tf_op jit(solution)/shard_map/ppermute | solution.py:22
  114.9 10.9 %collective-permute-start.17 = (bf16[1024,128]{1,0:T(8,128)(2,1)S(1)}, bf16[1024,128]{1,0:T(8,128)(2,1)S(1)}, u32[]{:S(2)}, u32[]{:S(2)}) collective-permute-start(bf16[1024,128]{1,0:T(8,128)(2,1)S(1)} %fusion.18), channel_id=1, source_target_pairs={{0,384},{1,385},{2,386},{3,387},{4,388},{5,389},{6,390},{7,391},{8... | collective-permute-start | bytes 786440 | tf_op jit(solution)/shard_map/ppermute | solution.py:22
  115.7 12.1 %collective-permute-start.12 = (bf16[128,1024]{0,1:T(8,128)(2,1)S(1)}, bf16[128,1024]{0,1:T(8,128)(2,1)S(1)}, u32[]{:S(2)}, u32[]{:S(2)}) collective-permute-start(bf16[128,1024]{0,1:T(8,128)(2,1)S(1)} %slice.68), channel_id=1, source_target_pairs={{144,128},{160,144},{176,160},{128,176},{272,256},{288,272},{304,2... | collective-permute-start | bytes 786440 | tf_op jit(solution)/shard_map/ppermute | solution.py:105
  121.1 9.5 %collective-permute-start.14 = (bf16[128,1024]{0,1:T(8,128)(2,1)S(1)}, bf16[128,1024]{0,1:T(8,128)(2,1)S(1)}, u32[]{:S(2)}, u32[]{:S(2)}) collective-permute-start(bf16[128,1024]{0,1:T(8,128)(2,1)S(1)} %slice.69), channel_id=1, source_target_pairs={{176,128},{128,144},{144,160},{160,176},{304,256},{256,272},{272,2... | collective-permute-start | bytes 786440 | tf_op jit(solution)/shard_map/ppermute | solution.py:105
  125.9 6.2 %collective-permute-start.18 = (bf16[1024,128]{1,0:T(8,128)(2,1)S(1)}, bf16[1024,128]{1,0:T(8,128)(2,1)S(1)}, u32[]{:S(2)}, u32[]{:S(2)}) collective-permute-start(bf16[1024,128]{1,0:T(8,128)(2,1)S(1)} %select_select_fusion), channel_id=1, source_target_pairs={{0,64},{64,0},{1,65},{65,1},{2,66},{66,2},{3,67},{67,3},{4,68},{68... | collective-permute-start | bytes 786440 | tf_op jit(solution)/shard_map/ppermute | solution.py:112
  130.6 1.7 %copy-start.1 = (bf16[4,256,128,8]{2,1,0,3:T(8,128)(2,1)S(1)}, bf16[4,256,128,8]{2,1,0,3:T(8,128)(2,1)}, u32[]{:S(2)}) copy-start(bf16[4,256,128,8]{2,1,0,3:T(8,128)(2,1)} %copy-done) | copy-start | bytes 6291460
  (5 other events, 5.9 us)

commit v10 on v8

--- a/solution.py
+++ b/solution.py
@@ -16,11 +16,11 @@
     return lax.optimization_barrier((value,) + others)[0]
 
 
-def from_first(values, axis):
+def from_first(values, axis, order=(3, 1, 2)):
     at = lax.axis_index(axis)
     out = values[0]
     got = {k: lax.ppermute(values[k], axis, [(0, k)]) for k in (3, 1, 2)}
-    for k in (3, 1, 2):
+    for k in order:
         out = jnp.where(at == k, got[k], out)
     return out
 
@@ -108,7 +108,7 @@
     across = jnp.concatenate([from_x(after(ahead[:128], right), 1), from_x(after(behind[128:], right), -1)])
     two = jnp.concatenate([late, ahead, across, behind, late, ahead, across])
     two = lax.dynamic_slice_in_dim(two, (4 - x) % 4 * 256, NB, 0)
-    right = from_first([right] * 4, "y")
+    right = from_first([right] * 4, "y", (2, 3, 1))
     changed = dot(two, right) + product(one, lax.ppermute(right, "core", [(0, 1), (1, 0)]))
     trail = (jnp.where(j >= 16, a, zeros).astype(F32) - changed).astype(BF)
     row0 = jnp.where(in0, a, r)

time: 134 us -> 133 us (level)
  the two profiles are of different devices: /device:TPU:43 before, /device:TPU:48 now
where the time goes in v10:
time: 133 us; the launch traced here: 132 us
  starting transfers between devices  61 us (46%)
  waiting for transfers between devices  38.1 us (29%)
  local copies, waits for them, and re-layouts  15.6 us (12%)
  matrix products  8.58 us (6%)
  blocking collectives  4.36 us (3%)
  other arithmetic  3.13 us (2%)
    ppermute x4, starting transfers between devices, from_x(): return lax.ppermute(value, ('y', 'x'), planes)  15.4 us
    all_to_all x1, starting transfers between devices, shards(): own = lax.all_to_all(copies(share, 4), 'z', 0, 0, axis_index_groups=fours)  14.2 us
    ppermute x6, starting transfers between devices, from_first(): got = {k: lax.ppermute(values[k], axis, [(0, k)]) for k in (3, 1, 2)}  10.2 us
    all_to_all x1, waiting for transfers between devices, shards(): own = lax.all_to_all(copies(share, 4), 'z', 0, 0, axis_index_groups=fours)  8.69 us
    ppermute x1, waiting for transfers between devices, shards(): lax.ppermute(own, 'z', [((k + 2 - 4 * (k % 2)) % 16, k) for k in range(16)])  7.99 us
    dot_general x7, matrix products, dot(): return jnp.dot(a, b, preferred_element_type=F32)  6.43 us
    ppermute x2, waiting for transfers between devices, from_z(): lax.ppermute(value, 'z', [((k + distance) % 16, k) for k in range(16)])  6.23 us
    ppermute x3, starting transfers between devices, shards(): parts = [pair] + [lax.ppermute(pair, 'y', [(k, 0)]) for k in range(1, 4)]  6.15 us
  transfers between devices with their start and end apart: 20, of which 10 were waited for; matrix products, arithmetic and copies ran while one was open for 15% of the time, Pallas kernels for 0%

profile of v10, /device:TPU:48, one launch (start us, length us, event | category | flops | bytes accessed | tf_op | source)
XLA Modules:
  0.0 131.5 jit_solution(2458711810557309687)
XLA Ops:
  0.9 4.9 %collective-permute-start = (bf16[256,128]{1,0:T(8,128)(2,1)S(1)}, bf16[256,128]{1,0:T(8,128)(2,1)S(1)}, u32[]{:S(2)}, u32[]{:S(2)}) collective-permute-start(bf16[256,128]{1,0:T(8,128)(2,1)S(1)} %get-tuple-element.33), channel_id=1, source_target_pairs={{0,32},{1,33},{2,34},{3,35},{4,36},{5,37},{6,38},{7,39},{8,40},{9,... | collective-permute-start | bytes 196616 | tf_op jit(solution)/shard_map/ppermute | solution.py:22
  5.9 1.3 collective-permute-start.1
  7.2 1.3 collective-permute-start.2
  9.0 1.3 collective-permute-done.2
  11.9 14.2 %all-to-all-start = ((bf16[4,256,128]{2,1,0:T(8,128)(2,1)}), bf16[4,256,128]{2,1,0:T(8,128)(2,1)S(1)}, u32[]{:S(2)}, u32[]{:S(2)}) async-start(bf16[4,256,128]{2,1,0:T(8,128)(2,1)} %broadcast_in_dim.17), calls=%async_computation | async-start | bytes 524288 | tf_op jit(solution)/shard_map/all_to_all | solution.py:57
  27.4 1.9 %collective-permute-start.6 = (bf16[2,128,1024]{2,1,0:T(8,128)(2,1)S(1)}, bf16[2,128,1024]{2,1,0:T(8,128)(2,1)S(1)}, u32[]{:S(2)}, u32[]{:S(2)}) collective-permute-start(bf16[2,128,1024]{2,1,0:T(8,128)(2,1)S(1)} %get-tuple-element.30), channel_id=1, source_target_pairs={{0,64},{64,0},{1,65},{65,1},{2,66},{66,2},{3,67},{67,3},{4,68},{68... | collective-permute-start | bytes 1572872 | tf_op jit(solution)/shard_map/ppermute | solution.py:51
  29.4 1.8 %collective-permute-done.6 = bf16[2,128,1024]{2,1,0:T(8,128)(2,1)S(1)} collective-permute-done((bf16[2,128,1024]{2,1,0:T(8,128)(2,1)S(1)}, bf16[2,128,1024]{2,1,0:T(8,128)(2,1)S(1)}, u32[]{:S(2)}, u32[]{:S(2)}) %collective-permute-start.6) | collective-permute-done | bytes 524320 | tf_op jit(solution)/shard_map/ppermute | solution.py:51
  31.4 1.7 %collective-permute-start.9 = (bf16[2,2,128,1024]{3,2,1,0:T(8,128)(2,1)S(1)}, bf16[2,2,128,1024]{3,2,1,0:T(8,128)(2,1)}, u32[]{:S(2)}, u32[]{:S(2)}) collective-permute-start(bf16[2,2,128,1024]{3,2,1,0:T(8,128)(2,1)S(1)} %maximum_select_fusion), channel_id=1, source_target_pairs={{384,0},{385,1},{386,2},{387,3},{388,4},{389,5},{390,6},{391,7},{3... | collective-permute-start | bytes 3145736 | tf_op jit(solution)/shard_map/ppermute | solution.py:54
  33.0 2.9 %collective-permute-start.8 = (bf16[2,2,128,1024]{3,2,1,0:T(8,128)(2,1)S(1)}, bf16[2,2,128,1024]{3,2,1,0:T(8,128)(2,1)}, u32[]{:S(2)}, u32[]{:S(2)}) collective-permute-start(bf16[2,2,128,1024]{3,2,1,0:T(8,128)(2,1)S(1)} %maximum_select_fusion), channel_id=1, source_target_pairs={{256,0},{257,1},{258,2},{259,3},{260,4},{261,5},{262,6},{263,7},{2... | collective-permute-start | bytes 3145736 | tf_op jit(solution)/shard_map/ppermute | solution.py:54
  35.9 1.6 %collective-permute-start.7 = (bf16[2,2,128,1024]{3,2,1,0:T(8,128)(2,1)S(1)}, bf16[2,2,128,1024]{3,2,1,0:T(8,128)(2,1)}, u32[]{:S(2)}, u32[]{:S(2)}) collective-permute-start(bf16[2,2,128,1024]{3,2,1,0:T(8,128)(2,1)S(1)} %maximum_select_fusion), channel_id=1, source_target_pairs={{128,0},{129,1},{130,2},{131,3},{132,4},{133,5},{134,6},{135,7},{1... | collective-permute-start | bytes 3145736 | tf_op jit(solution)/shard_map/ppermute | solution.py:54
  37.5 8.7 %all-to-all-done = bf16[4,256,128]{2,1,0:T(8,128)(2,1)S(1)} async-done(((bf16[4,256,128]{2,1,0:T(8,128)(2,1)}), bf16[4,256,128]{2,1,0:T(8,128)(2,1)S(1)}, u32[]{:S(2)}, u32[]{:S(2)}) %all-to-all-start) | async-done | bytes 262176 | tf_op jit(solution)/shard_map/all_to_all | solution.py:57
  46.2 1.9 %collective-permute-start.3 = (bf16[4,256,128]{2,1,0:T(8,128)(2,1)S(1)}, bf16[4,256,128]{2,1,0:T(8,128)(2,1)S(1)}, u32[]{:S(2)}, u32[]{:S(2)}) collective-permute-start(bf16[4,256,128]{2,1,0:T(8,128)(2,1)S(1)} %all-to-all-done), channel_id=1, source_target_pairs={{2,0},{15,1},{4,2},{1,3},{6,4},{3,5},{8,6},{5,7},{10,8},{7,9},{12,... | collective-permute-start | bytes 786440 | tf_op jit(solution)/shard_map/ppermute | solution.py:63
  48.1 3.0 %collective-permute-start.4 = (bf16[4,256,128]{2,1,0:T(8,128)(2,1)S(1)}, bf16[4,256,128]{2,1,0:T(8,128)(2,1)S(1)}, u32[]{:S(2)}, u32[]{:S(2)}) collective-permute-start(bf16[4,256,128]{2,1,0:T(8,128)(2,1)S(1)} %all-to-all-done), channel_id=1, source_target_pairs={{15,0},{0,1},{1,2},{2,3},{3,4},{4,5},{5,6},{6,7},{7,8},{8,9},{9,10... | collective-permute-start | bytes 786440 | tf_op jit(solution)/shard_map/ppermute | solution.py:60
  51.2 8.0 %collective-permute-done.3 = bf16[4,256,128]{2,1,0:T(8,128)(2,1)S(1)} collective-permute-done((bf16[4,256,128]{2,1,0:T(8,128)(2,1)S(1)}, bf16[4,256,128]{2,1,0:T(8,128)(2,1)S(1)}, u32[]{:S(2)}, u32[]{:S(2)}) %collective-permute-start.3) | collective-permute-done | bytes 262176 | tf_op jit(solution)/shard_map/ppermute | solution.py:63
  59.2 1.9 %collective-permute-start.5 = (bf16[4,256,128]{2,1,0:T(8,128)(2,1)S(1)}, bf16[4,256,128]{2,1,0:T(8,128)(2,1)S(1)}, u32[]{:S(2)}, u32[]{:S(2)}) collective-permute-start(bf16[4,256,128]{2,1,0:T(8,128)(2,1)S(1)} %all-to-all-done), channel_id=1, source_target_pairs={{1,0},{2,1},{3,2},{4,3},{5,4},{6,5},{7,6},{8,7},{9,8},{10,9},{11,1... | collective-permute-start | bytes 786440 | tf_op jit(solution)/shard_map/ppermute | solution.py:60
  62.3 5.1 %collective-permute-done.5 = bf16[4,256,128]{2,1,0:T(8,128)(2,1)S(1)} collective-permute-done((bf16[4,256,128]{2,1,0:T(8,128)(2,1)S(1)}, bf16[4,256,128]{2,1,0:T(8,128)(2,1)S(1)}, u32[]{:S(2)}, u32[]{:S(2)}) %collective-permute-start.5) | collective-permute-done | bytes 262176 | tf_op jit(solution)/shard_map/ppermute | solution.py:60
  67.9 1.8 %broadcast_in_dim.19 = bf16[4,8,256,128]{3,2,1,0:T(8,128)(2,1)} broadcast(bf16[8,256,128]{2,1,0:T(8,128)(2,1)S(1)} %bitcast.68), dimensions={1,2,3} | broadcast | bytes 2621440 | tf_op jit(solution)/shard_map/broadcast_in_dim | solution.py:29
  69.7 4.5 %all-to-all-start.1 = ((bf16[4,8,256,128]{3,2,1,0:T(8,128)(2,1)}), bf16[4,8,256,128]{3,2,1,0:T(8,128)(2,1)}, u32[]{:S(2)}, u32[]{:S(2)}) async-start(bf16[4,8,256,128]{3,2,1,0:T(8,128)(2,1)} %broadcast_in_dim.19), calls=%async_computation.1 | async-start | bytes 4194304 | tf_op jit(solution)/shard_map/all_to_all | solution.py:72
  80.6 1.4 %broadcast_select_fusion = (bf16[1024,128]{1,0:T(8,128)(2,1)}, bf16[1024,128]{1,0:T(8,128)(2,1)S(1)}) fusion(pred[]{:T(512)S(6)} %and.22, bf16[1024,128]{1,0:T(8,128)(2,1)S(1)} %dynamic-slice_negate_fusion, bf16[1024,1024]{1,0:T(8,128)(2,1)S(1)} %get-tuple-element.13, bf16[1024,128]{1,0:T(8,128)(2,1)S(1)} %convolution_convert_fusion.4, pred[]{:T(512)S(6)} %lt.45), kind=kOutput, calls=%fused_computation.38 | convolution fusion | flops 268828672 | bytes 3145730 | tf_op jit(solution)/shard_map/dot_general | solution.py:12
  82.0 2.2 %all-gather = bf16[2048,128]{1,0:T(8,128)(2,1)S(1)} all-gather(bf16[1024,128]{1,0:T(8,128)(2,1)S(1)} %get-tuple-element.35), channel_id=2, replica_groups=mesh['y'=4,'core'=2,'x'=4,'z'=16] {'core'}, dimensions={0}, use_global_device_ids=true | all-gather | bytes 786432 | tf_op jit(solution)/shard_map/all_gather | solution.py:33
  85.2 5.1 %collective-permute-start.10 = (bf16[256,1024]{0,1:T(8,128)(2,1)S(1)}, bf16[256,1024]{0,1:T(8,128)(2,1)S(1)}, u32[]{:S(2)}, u32[]{:S(2)}) collective-permute-start(bf16[256,1024]{0,1:T(8,128)(2,1)S(1)} %bitcast.63), channel_id=1, source_target_pairs={{144,128},{160,144},{176,160},{128,176},{272,256},{288,272},{304,2... | collective-permute-start | bytes 1572872 | tf_op jit(solution)/shard_map/ppermute | solution.py:105
  90.4 1.9 %collective-permute-start.12 = (bf16[256,1024]{0,1:T(8,128)(2,1)S(1)}, bf16[256,1024]{0,1:T(8,128)(2,1)}, u32[]{:S(2)}, u32[]{:S(2)}) collective-permute-start(bf16[256,1024]{0,1:T(8,128)(2,1)S(1)} %bitcast.64), channel_id=1, source_target_pairs={{176,128},{128,144},{144,160},{160,176},{304,256},{256,272},{272,2... | collective-permute-start | bytes 1572872 | tf_op jit(solution)/shard_map/ppermute | solution.py:105
  92.3 4.3 %all-to-all-done.1 = bf16[4,8,256,128]{3,2,1,0:T(8,128)(2,1)} async-done(((bf16[4,8,256,128]{3,2,1,0:T(8,128)(2,1)}), bf16[4,8,256,128]{3,2,1,0:T(8,128)(2,1)}, u32[]{:S(2)}, u32[]{:S(2)}) %all-to-all-start.1) | async-done | bytes 2097184 | tf_op jit(solution)/shard_map/all_to_all | solution.py:72
  96.6 1.8 %copy.10 = bf16[4,256,128,8]{2,1,0,3:T(8,128)(2,1)S(1)} copy(bf16[4,256,128,8]{2,1,3,0:T(8,128)(2,1)} %bitcast.20) | data formatting | bytes 4194304 | tf_op jit(solution)/shard_map/xzrk,zkn->xrn/dot_general | solution.py:91
  101.6 2.2 %all-gather.1 = bf16[2048,128]{1,0:T(8,128)(2,1)S(1)} all-gather(bf16[1024,128]{1,0:T(8,128)(2,1)S(1)} %fusion.17), channel_id=3, replica_groups=mesh['y'=4,'core'=2,'x'=4,'z'=16] {'core'}, dimensions={0}, use_global_device_ids=true | all-gather | bytes 786432 | tf_op jit(solution)/shard_map/all_gather | solution.py:33
  107.4 1.3 collective-permute-start.16
  108.8 6.4 %collective-permute-start.11 = (bf16[128,1024]{0,1:T(8,128)(2,1)S(1)}, bf16[128,1024]{0,1:T(8,128)(2,1)S(1)}, u32[]{:S(2)}, u32[]{:S(2)}) collective-permute-start(bf16[128,1024]{0,1:T(8,128)(2,1)S(1)} %slice.73), channel_id=1, source_target_pairs={{144,128},{160,144},{176,160},{128,176},{272,256},{288,272},{304,2... | collective-permute-start | bytes 786440 | tf_op jit(solution)/shard_map/ppermute | solution.py:105
  116.3 1.9 %collective-permute-start.13 = (bf16[128,1024]{0,1:T(8,128)(2,1)S(1)}, bf16[128,1024]{0,1:T(8,128)(2,1)S(1)}, u32[]{:S(2)}, u32[]{:S(2)}) collective-permute-start(bf16[128,1024]{0,1:T(8,128)(2,1)S(1)} %slice.75), channel_id=1, source_target_pairs={{176,128},{128,144},{144,160},{160,176},{304,256},{256,272},{272,2... | collective-permute-start | bytes 786440 | tf_op jit(solution)/shard_map/ppermute | solution.py:105
  118.2 3.5 %collective-permute-done.16 = bf16[1024,128]{1,0:T(8,128)(2,1)S(1)} collective-permute-done((bf16[1024,128]{1,0:T(8,128)(2,1)S(1)}, bf16[1024,128]{1,0:T(8,128)(2,1)S(1)}, u32[]{:S(2)}, u32[]{:S(2)}) %collective-permute-start.16) | collective-permute-done | bytes 262176 | tf_op jit(solution)/shard_map/ppermute | solution.py:22
  121.8 1.9 %collective-permute-start.17 = (bf16[1024,128]{1,0:T(8,128)(2,1)S(1)}, bf16[1024,128]{1,0:T(8,128)(2,1)S(1)}, u32[]{:S(2)}, u32[]{:S(2)}) collective-permute-start(bf16[1024,128]{1,0:T(8,128)(2,1)S(1)} %select_select_fusion), channel_id=1, source_target_pairs={{0,64},{64,0},{1,65},{65,1},{2,66},{66,2},{3,67},{67,3},{4,68},{68... | collective-permute-start | bytes 786440 | tf_op jit(solution)/shard_map/ppermute | solution.py:112
  123.8 3.6 %collective-permute-done.13 = bf16[128,1024]{0,1:T(8,128)(2,1)S(1)} collective-permute-done((bf16[128,1024]{0,1:T(8,128)(2,1)S(1)}, bf16[128,1024]{0,1:T(8,128)(2,1)S(1)}, u32[]{:S(2)}, u32[]{:S(2)}) %collective-permute-start.13) | collective-permute-done | bytes 262176 | tf_op jit(solution)/shard_map/ppermute | solution.py:105
  130.1 1.5 %fusion.19 = bf16[1024,128]{1,0:T(8,128)(2,1)} fusion(f32[1024,128]{1,0:T(8,128)S(1)} %convolution_bitcast_fusion, bf16[1024,128]{1,0:T(8,128)(2,1)S(1)} %select_select_fusion, bf16[1792,1024]{0,1:T(8,128)(2,1)S(1)} %constant_dynamic-update-slice_fusion.7, s32[]{:T(128)S(6)} %select_n.167, bf16[1024,128]{1,0:T(8,128)(2,1)S(1)} %copy-done.10, ...), kind=kOutput, calls=%fused_computation.28 | convolution fusion | flops 269615104 | bytes 4194313 | tf_op jit(solution)/shard_map/dot_general | solution.py:12
  (92 shorter events, 23.9 us)
Async XLA Ops:
  0.9 7.6 %collective-permute-start = (bf16[256,128]{1,0:T(8,128)(2,1)S(1)}, bf16[256,128]{1,0:T(8,128)(2,1)S(1)}, u32[]{:S(2)}, u32[]{:S(2)}) collective-permute-start(bf16[256,128]{1,0:T(8,128)(2,1)S(1)} %get-tuple-element.33), channel_id=1, source_target_pairs={{0,32},{1,33},{2,34},{3,35},{4,36},{5,37},{6,38},{7,39},{8,40},{9,... | collective-permute-start | bytes 196616 | tf_op jit(solution)/shard_map/ppermute | solution.py:22
  5.9 3.2 %collective-permute-start.1 = (bf16[256,128]{1,0:T(8,128)(2,1)S(1)}, bf16[256,128]{1,0:T(8,128)(2,1)S(1)}, u32[]{:S(2)}, u32[]{:S(2)}) collective-permute-start(bf16[256,128]{1,0:T(8,128)(2,1)S(1)} %get-tuple-element.32), channel_id=1, source_target_pairs={{0,16},{1,17},{2,18},{3,19},{4,20},{5,21},{6,22},{7,23},{8,24},{9,... | collective-permute-start | bytes 196616 | tf_op jit(solution)/shard_map/ppermute | solution.py:22
  7.2 3.2 %collective-permute-start.2 = (bf16[256,128]{1,0:T(8,128)(2,1)S(1)}, bf16[256,128]{1,0:T(8,128)(2,1)S(1)}, u32[]{:S(2)}, u32[]{:S(2)}) collective-permute-start(bf16[256,128]{1,0:T(8,128)(2,1)S(1)} %get-tuple-element.31), channel_id=1, source_target_pairs={{0,48},{1,49},{2,50},{3,51},{4,52},{5,53},{6,54},{7,55},{8,56},{9,... | collective-permute-start | bytes 196616 | tf_op jit(solution)/shard_map/ppermute | solution.py:22
  11.9 34.3 %all-to-all-start = ((bf16[4,256,128]{2,1,0:T(8,128)(2,1)}), bf16[4,256,128]{2,1,0:T(8,128)(2,1)S(1)}, u32[]{:S(2)}, u32[]{:S(2)}) async-start(bf16[4,256,128]{2,1,0:T(8,128)(2,1)} %broadcast_in_dim.17), calls=%async_computation | async-start | bytes 524288 | tf_op jit(solution)/shard_map/all_to_all | solution.py:57
  27.4 3.8 %collective-permute-start.6 = (bf16[2,128,1024]{2,1,0:T(8,128)(2,1)S(1)}, bf16[2,128,1024]{2,1,0:T(8,128)(2,1)S(1)}, u32[]{:S(2)}, u32[]{:S(2)}) collective-permute-start(bf16[2,128,1024]{2,1,0:T(8,128)(2,1)S(1)} %get-tuple-element.30), channel_id=1, source_target_pairs={{0,64},{64,0},{1,65},{65,1},{2,66},{66,2},{3,67},{67,3},{4,68},{68... | collective-permute-start | bytes 1572872 | tf_op jit(solution)/shard_map/ppermute | solution.py:51
  31.4 43.7 %collective-permute-start.9 = (bf16[2,2,128,1024]{3,2,1,0:T(8,128)(2,1)S(1)}, bf16[2,2,128,1024]{3,2,1,0:T(8,128)(2,1)}, u32[]{:S(2)}, u32[]{:S(2)}) collective-permute-start(bf16[2,2,128,1024]{3,2,1,0:T(8,128)(2,1)S(1)} %maximum_select_fusion), channel_id=1, source_target_pairs={{384,0},{385,1},{386,2},{387,3},{388,4},{389,5},{390,6},{391,7},{3... | collective-permute-start | bytes 3145736 | tf_op jit(solution)/shard_map/ppermute | solution.py:54
  33.0 43.3 %collective-permute-start.8 = (bf16[2,2,128,1024]{3,2,1,0:T(8,128)(2,1)S(1)}, bf16[2,2,128,1024]{3,2,1,0:T(8,128)(2,1)}, u32[]{:S(2)}, u32[]{:S(2)}) collective-permute-start(bf16[2,2,128,1024]{3,2,1,0:T(8,128)(2,1)S(1)} %maximum_select_fusion), channel_id=1, source_target_pairs={{256,0},{257,1},{258,2},{259,3},{260,4},{261,5},{262,6},{263,7},{2... | collective-permute-start | bytes 3145736 | tf_op jit(solution)/shard_map/ppermute | solution.py:54
  35.9 41.7 %collective-permute-start.7 = (bf16[2,2,128,1024]{3,2,1,0:T(8,128)(2,1)S(1)}, bf16[2,2,128,1024]{3,2,1,0:T(8,128)(2,1)}, u32[]{:S(2)}, u32[]{:S(2)}) collective-permute-start(bf16[2,2,128,1024]{3,2,1,0:T(8,128)(2,1)S(1)} %maximum_select_fusion), channel_id=1, source_target_pairs={{128,0},{129,1},{130,2},{131,3},{132,4},{133,5},{134,6},{135,7},{1... | collective-permute-start | bytes 3145736 | tf_op jit(solution)/shard_map/ppermute | solution.py:54
  46.2 13.0 %collective-permute-start.3 = (bf16[4,256,128]{2,1,0:T(8,128)(2,1)S(1)}, bf16[4,256,128]{2,1,0:T(8,128)(2,1)S(1)}, u32[]{:S(2)}, u32[]{:S(2)}) collective-permute-start(bf16[4,256,128]{2,1,0:T(8,128)(2,1)S(1)} %all-to-all-done), channel_id=1, source_target_pairs={{2,0},{15,1},{4,2},{1,3},{6,4},{3,5},{8,6},{5,7},{10,8},{7,9},{12,... | collective-permute-start | bytes 786440 | tf_op jit(solution)/shard_map/ppermute | solution.py:63
  48.1 14.1 %collective-permute-start.4 = (bf16[4,256,128]{2,1,0:T(8,128)(2,1)S(1)}, bf16[4,256,128]{2,1,0:T(8,128)(2,1)S(1)}, u32[]{:S(2)}, u32[]{:S(2)}) collective-permute-start(bf16[4,256,128]{2,1,0:T(8,128)(2,1)S(1)} %all-to-all-done), channel_id=1, source_target_pairs={{15,0},{0,1},{1,2},{2,3},{3,4},{4,5},{5,6},{6,7},{7,8},{8,9},{9,10... | collective-permute-start | bytes 786440 | tf_op jit(solution)/shard_map/ppermute | solution.py:60
  59.2 8.3 %collective-permute-start.5 = (bf16[4,256,128]{2,1,0:T(8,128)(2,1)S(1)}, bf16[4,256,128]{2,1,0:T(8,128)(2,1)S(1)}, u32[]{:S(2)}, u32[]{:S(2)}) collective-permute-start(bf16[4,256,128]{2,1,0:T(8,128)(2,1)S(1)} %all-to-all-done), channel_id=1, source_target_pairs={{1,0},{2,1},{3,2},{4,3},{5,4},{6,5},{7,6},{8,7},{9,8},{10,9},{11,1... | collective-permute-start | bytes 786440 | tf_op jit(solution)/shard_map/ppermute | solution.py:60
  69.7 26.9 %all-to-all-start.1 = ((bf16[4,8,256,128]{3,2,1,0:T(8,128)(2,1)}), bf16[4,8,256,128]{3,2,1,0:T(8,128)(2,1)}, u32[]{:S(2)}, u32[]{:S(2)}) async-start(bf16[4,8,256,128]{3,2,1,0:T(8,128)(2,1)} %broadcast_in_dim.19), calls=%async_computation.1 | async-start | bytes 4194304 | tf_op jit(solution)/shard_map/all_to_all | solution.py:72
  79.6 2.5 %copy-start.2 = (bf16[1024,1024]{1,0:T(8,128)(2,1)}, bf16[1024,1024]{1,0:T(8,128)(2,1)S(1)}, u32[]{:S(2)}) copy-start(bf16[1024,1024]{1,0:T(8,128)(2,1)S(1)} %get-tuple-element.13) | copy-start | bytes 6291460
  79.7 2.3 %copy-start.13 = (bf16[1024,128]{1,0:T(8,128)(2,1)}, bf16[1024,128]{1,0:T(8,128)(2,1)S(1)}, u32[]{:S(2)}) copy-start(bf16[1024,128]{1,0:T(8,128)(2,1)S(1)} %dynamic-slice_negate_fusion) | copy-start | bytes 786436
  80.5 1.5 %copy-start.7 = (bf16[1024,128]{1,0:T(8,128)(2,1)}, bf16[1024,128]{1,0:T(8,128)(2,1)S(1)}, u32[]{:S(2)}) copy-start(bf16[1024,128]{1,0:T(8,128)(2,1)S(1)} %convolution_convert_fusion.4) | copy-start | bytes 786436
  80.6 4.4 %copy-start.4 = (bf16[2,4,256,128]{3,2,1,0:T(8,128)(2,1)S(1)}, bf16[2,4,256,128]{3,2,1,0:T(8,128)(2,1)}, u32[]{:S(2)}) copy-start(bf16[2,4,256,128]{3,2,1,0:T(8,128)(2,1)} %copy.7) | copy-start | bytes 1572868
  85.2 23.5 %collective-permute-start.10 = (bf16[256,1024]{0,1:T(8,128)(2,1)S(1)}, bf16[256,1024]{0,1:T(8,128)(2,1)S(1)}, u32[]{:S(2)}, u32[]{:S(2)}) collective-permute-start(bf16[256,1024]{0,1:T(8,128)(2,1)S(1)} %bitcast.63), channel_id=1, source_target_pairs={{144,128},{160,144},{176,160},{128,176},{272,256},{288,272},{304,2... | collective-permute-start | bytes 1572872 | tf_op jit(solution)/shard_map/ppermute | solution.py:105
  90.4 24.9 %collective-permute-start.12 = (bf16[256,1024]{0,1:T(8,128)(2,1)S(1)}, bf16[256,1024]{0,1:T(8,128)(2,1)}, u32[]{:S(2)}, u32[]{:S(2)}) collective-permute-start(bf16[256,1024]{0,1:T(8,128)(2,1)S(1)} %bitcast.64), channel_id=1, source_target_pairs={{176,128},{128,144},{144,160},{160,176},{304,256},{256,272},{272,2... | collective-permute-start | bytes 1572872 | tf_op jit(solution)/shard_map/ppermute | solution.py:105
  96.6 1.8 %slice-start = ((bf16[2048,128]{1,0:T(8,128)(2,1)}), bf16[1024,128]{1,0:T(8,128)(2,1)S(1)}, s32[]{:S(2)}) async-start(bf16[2048,128]{1,0:T(8,128)(2,1)} %copy-done.5), calls=%async_computation.2 | async-start | bytes 524288 | tf_op jit(solution)/shard_map/slice | solution.py:86
  98.4 5.5 %copy-start = (bf16[4,256,128,8]{2,1,0,3:T(8,128)(2,1)}, bf16[4,256,128,8]{2,1,0,3:T(8,128)(2,1)S(1)}, u32[]{:S(2)}) copy-start(bf16[4,256,128,8]{2,1,0,3:T(8,128)(2,1)S(1)} %copy.10) | copy-start | bytes 6291460
  98.4 2.4 %copy-start.3 = (bf16[1024,1024]{1,0:T(8,128)(2,1)S(1)}, bf16[1024,1024]{1,0:T(8,128)(2,1)}, u32[]{:S(2)}) copy-start(bf16[1024,1024]{1,0:T(8,128)(2,1)} %copy-done.2) | copy-start | bytes 6291460
  98.4 2.5 %copy-start.14 = (bf16[1024,128]{1,0:T(8,128)(2,1)S(1)}, bf16[1024,128]{1,0:T(8,128)(2,1)}, u32[]{:S(2)}) copy-start(bf16[1024,128]{1,0:T(8,128)(2,1)} %copy-done.13) | copy-start | bytes 786436
  103.8 1.4 %copy-start.15 = (bf16[1024,128]{1,0:T(8,128)(2,1)S(1)}, bf16[1024,128]{1,0:T(8,128)(2,1)}, u32[]{:S(2)}) copy-start(bf16[1024,128]{1,0:T(8,128)(2,1)} %get-tuple-element.34) | copy-start | bytes 786436
  106.0 12.2 %collective-permute-start.14 = (bf16[1024,128]{1,0:T(8,128)(2,1)S(1)}, bf16[1024,128]{1,0:T(8,128)(2,1)S(1)}, u32[]{:S(2)}, u32[]{:S(2)}) collective-permute-start(bf16[1024,128]{1,0:T(8,128)(2,1)S(1)} %fusion.18), channel_id=1, source_target_pairs={{0,128},{1,129},{2,130},{3,131},{4,132},{5,133},{6,134},{7,135},{8... | collective-permute-start | bytes 786440 | tf_op jit(solution)/shard_map/ppermute | solution.py:22
  106.7 11.5 %collective-permute-start.15 = (bf16[1024,128]{1,0:T(8,128)(2,1)S(1)}, bf16[1024,128]{1,0:T(8,128)(2,1)S(1)}, u32[]{:S(2)}, u32[]{:S(2)}) collective-permute-start(bf16[1024,128]{1,0:T(8,128)(2,1)S(1)} %fusion.18), channel_id=1, source_target_pairs={{0,384},{1,385},{2,386},{3,387},{4,388},{5,389},{6,390},{7,391},{8... | collective-permute-start | bytes 786440 | tf_op jit(solution)/shard_map/ppermute | solution.py:22
  107.4 14.4 %collective-permute-start.16 = (bf16[1024,128]{1,0:T(8,128)(2,1)S(1)}, bf16[1024,128]{1,0:T(8,128)(2,1)S(1)}, u32[]{:S(2)}, u32[]{:S(2)}) collective-permute-start(bf16[1024,128]{1,0:T(8,128)(2,1)S(1)} %fusion.18), channel_id=1, source_target_pairs={{0,256},{1,257},{2,258},{3,259},{4,260},{5,261},{6,262},{7,263},{8... | collective-permute-start | bytes 786440 | tf_op jit(solution)/shard_map/ppermute | solution.py:22
  108.8 14.9 %collective-permute-start.11 = (bf16[128,1024]{0,1:T(8,128)(2,1)S(1)}, bf16[128,1024]{0,1:T(8,128)(2,1)S(1)}, u32[]{:S(2)}, u32[]{:S(2)}) collective-permute-start(bf16[128,1024]{0,1:T(8,128)(2,1)S(1)} %slice.73), channel_id=1, source_target_pairs={{144,128},{160,144},{176,160},{128,176},{272,256},{288,272},{304,2... | collective-permute-start | bytes 786440 | tf_op jit(solution)/shard_map/ppermute | solution.py:105
  116.3 11.2 %collective-permute-start.13 = (bf16[128,1024]{0,1:T(8,128)(2,1)S(1)}, bf16[128,1024]{0,1:T(8,128)(2,1)S(1)}, u32[]{:S(2)}, u32[]{:S(2)}) collective-permute-start(bf16[128,1024]{0,1:T(8,128)(2,1)S(1)} %slice.75), channel_id=1, source_target_pairs={{176,128},{128,144},{144,160},{160,176},{304,256},{256,272},{272,2... | collective-permute-start | bytes 786440 | tf_op jit(solution)/shard_map/ppermute | solution.py:105
  121.8 7.2 %collective-permute-start.17 = (bf16[1024,128]{1,0:T(8,128)(2,1)S(1)}, bf16[1024,128]{1,0:T(8,128)(2,1)S(1)}, u32[]{:S(2)}, u32[]{:S(2)}) collective-permute-start(bf16[1024,128]{1,0:T(8,128)(2,1)S(1)} %select_select_fusion), channel_id=1, source_target_pairs={{0,64},{64,0},{1,65},{65,1},{2,66},{66,2},{3,67},{67,3},{4,68},{68... | collective-permute-start | bytes 786440 | tf_op jit(solution)/shard_map/ppermute | solution.py:112
  127.5 1.7 %copy-start.1 = (bf16[4,256,128,8]{2,1,0,3:T(8,128)(2,1)S(1)}, bf16[4,256,128,8]{2,1,0,3:T(8,128)(2,1)}, u32[]{:S(2)}) copy-start(bf16[4,256,128,8]{2,1,0,3:T(8,128)(2,1)} %copy-done) | copy-start | bytes 6291460
  128.8 1.1 copy-start.8
  128.9 1.2 copy-start.12
  (5 other events, 4.3 us)
